TPU v7x, 32 devices: a whole 2x2x4 slice. The times are simulated.
32 devices in a mesh: rep: 4 (over y, x), shard: 8 (over z, core).
Axes of the slice: x: 2, y: 2, z: 4, core: 2. Of those that a mesh axis runs over, the one named last changes fastest.
Arguments:
- tokens: bfloat16 [4096, 960], P(('rep', 'shard')), may hold values from -6 to 6
- lengths: int32 [4, 6], P('rep'), may hold values from 0 to 1024, as said below
- norm_one: bfloat16 [960], P('shard'), may hold values from 0.099609375 to 1.8984375
- w_query: bfloat16 [960, 960], P('shard'), may hold values from -0.1875 to 0.1875
- w_key: bfloat16 [960, 320], P('shard'), may hold values from -0.1875 to 0.1875
- w_value: bfloat16 [960, 320], P('shard'), may hold values from -0.1875 to 0.1875
- w_out: bfloat16 [960, 960], P('shard'), may hold values from -1 to 1
- norm_two: bfloat16 [960], P('shard'), may hold values from 0.099609375 to 1.8984375
- w_gate: bfloat16 [960, 2560], P('shard'), may hold values from -0.1875 to 0.1875
- w_up: bfloat16 [960, 2560], P('shard'), may hold values from -0.1875 to 0.1875
- w_down: bfloat16 [2560, 960], P('shard'), may hold values from -0.125 to 0.125
- cotangent: bfloat16 [4096, 960], P(('rep', 'shard')), may hold values from -6 to 6
Outputs:
- output: bfloat16 [4096, 960], P(('rep', 'shard'))
- input_grad: float32 [4096, 960], P(('rep', 'shard'))
- grad_norm_one: float32 [960], P('shard')
- grad_w_query: float32 [960, 960], P('shard')
- grad_w_key: float32 [960, 320], P('shard')
- grad_w_value: float32 [960, 320], P('shard')
- grad_w_out: float32 [960, 960], P('shard')
- grad_norm_two: float32 [960], P('shard')
- grad_w_gate: float32 [960, 2560], P('shard')
- grad_w_up: float32 [960, 2560], P('shard')
- grad_w_down: float32 [2560, 960], P('shard')
Inputs may be any that keep to these rules, and one draw needn't show every extreme that they name: `lengths`: each row packs documents in order, each of 200 to 2000 tokens, the last one cut at the sequence's end; the slots after it hold 0, and a row sums to 1024. In one sequence, drawn from the seed, the first document instead has the largest length allowed here, which reaches from the sequence's first device to its last.
All inputs are finite; a program needn't handle non-finite values.
Results may differ from a plain program's by a relative error of at most 0.02.
Values may be sent and summed in bfloat16 or wider, within the bound.
No kernel may reach another device: no remote copies, remote signals or barrier semaphores. Data moves between devices by JAX's collectives and lax.ppermute only.
A program may use at most 128 MiB of HBM per device.

v0:
```python
import jax
import jax.numpy as jnp
from jax import lax
from jax.experimental import pallas as pl
from jax.experimental.pallas import tpu as pltpu
from jax.sharding import PartitionSpec as P

D = 960
QH = 15
KVH = 5
HD = 64
FF = 2560
GROUP = QH // KVH

EPS = 1e-05
ROPE_BASE = 10000.0
MASKED = -1e30
SCALE = HD ** (-0.5)
BF16 = jnp.bfloat16
F32 = jnp.float32


def doc_layout(lengths_row, length):
    places = jnp.arange(length, dtype=jnp.int32)
    doc_ends = jnp.cumsum(lengths_row)
    passed = places[:, None] >= doc_ends[None, :]
    doc_start = jnp.sum(jnp.where(passed, lengths_row[None, :], 0), axis=1)
    return (doc_start, places - doc_start)


def rope_tables(position):
    half_dim = HD // 2
    fraction = jnp.arange(half_dim, dtype=F32) * (2.0 / HD)
    inverse = ROPE_BASE ** (-fraction)
    angles = position.astype(F32)[:, None] * inverse[None, :]
    return (jnp.cos(angles), jnp.sin(angles))


VMEM_LIMIT = 56 * 2**20


def dot(left, right):
    return jnp.dot(left, right, preferred_element_type=F32)


def contract_rows(left, right):
    return lax.dot_general(left, right, (((0,), (0,)), ((), ())), preferred_element_type=F32)


def contract_cols(left, right):
    return lax.dot_general(left, right, (((1,), (1,)), ((), ())), preferred_element_type=F32)


def inverse_rms(values):
    return lax.rsqrt(jnp.sum(values * values, axis=-1, keepdims=True) * (1.0 / D) + EPS)


def norm_backward(values, inverse, gain, grad_norm):
    scaled = grad_norm * gain
    mean = jnp.sum(scaled * values, axis=-1, keepdims=True) * (1.0 / D)
    return inverse * scaled - values * inverse**3 * mean


def round_up(value, step):
    return -(-value // step) * step


def rows_at(index, rows):
    return pl.ds(pl.multiple_of(index * rows, rows), rows)


def to_blocks(values, n, width):
    rows, own = values.shape[0], values.shape[1] // n
    gap = jnp.zeros((rows, width // n - own), values.dtype)
    parts = []
    for s in range(n):
        parts += [values[:, s * own : (s + 1) * own], gap]
    return jnp.concatenate(parts, axis=1)


def from_blocks(values, n, own):
    block = values.shape[1] // n
    return jnp.concatenate([values[:, s * block : s * block + own] for s in range(n)], axis=1)


def swap(block, axis, k):
    count = lax.axis_size(axis)
    return lax.ppermute(block, axis, [(i, i ^ k) for i in range(count)])


def exchange(block):
    return lax.all_to_all(block, "shard", split_axis=0, concat_axis=0, tiled=True)


def spread(block, axis, step):
    return [block] + [swap(block, axis, k) for k in range(step, lax.axis_size(axis), step)]


def with_cores(parts):
    return parts + [swap(part, "shard", 1) for part in parts]


def deliver(blocks, axis, step):
    return [blocks[0]] + [swap(block, axis, i * step) for i, block in enumerate(blocks) if i]


def call(kernel, name, outs, *operands, scalars=(), scratch=()):
    specs = [pl.BlockSpec(memory_space=pltpu.SMEM)] * len(scalars)
    specs += [pl.BlockSpec(memory_space=pltpu.VMEM)] * len(operands)
    return pl.pallas_call(
        kernel,
        out_shape=[jax.ShapeDtypeStruct(shape, dtype) for shape, dtype in outs],
        in_specs=specs,
        out_specs=[pl.BlockSpec(memory_space=pltpu.VMEM)] * len(outs),
        scratch_shapes=[pltpu.VMEM(shape, dtype) for shape, dtype in scratch],
        compiler_params=pltpu.CompilerParams(vmem_limit_bytes=VMEM_LIMIT),
        name=name,
    )(*scalars, *operands)


def turned(values):
    half = HD // 2
    parts = []
    for begin in range(0, values.shape[1], HD):
        parts.append(-values[:, begin + half : begin + HD])
        parts.append(values[:, begin : begin + half])
    return jnp.concatenate(parts, axis=1)


def head_of(values, h, heads):
    if heads == 1:
        return values
    lane = lax.broadcasted_iota(jnp.int32, values.shape, 1)
    return jnp.where(lane // HD == h, values, jnp.zeros_like(values))


def masked_probs(query, key, starts, row):
    rows, cols = query.shape[0], key.shape[0]
    logits = contract_cols(query, key) * SCALE
    place = lax.broadcasted_iota(jnp.int32, (rows, cols), 1)
    own = lax.broadcasted_iota(jnp.int32, (rows, cols), 0) + row
    logits = jnp.where((place <= own) & (place >= starts), logits, MASKED)
    raised = jnp.exp(logits - jnp.max(logits, axis=-1, keepdims=True))
    return raised * (1.0 / jnp.sum(raised, axis=-1, keepdims=True))


def blocks_kernel(n, in_ref, out_ref):
    values = in_ref[...].astype(F32)
    out_ref[...] = to_blocks(values, n, out_ref.shape[1]).astype(BF16)


def attention_message_kernel(n, rep_ref, q_ref, k_ref, v_ref, out_ref, gain_ref, qkv_msg_ref, out_msg_ref):
    own = q_ref.shape[0]
    piece, cols = qkv_msg_ref.shape[1:]
    head_cols = cols // 3
    heads = head_cols // HD
    row = lax.broadcasted_iota(jnp.int32, (piece, own), 0) + rep_ref[0] * piece
    pick = jnp.where(row == lax.broadcasted_iota(jnp.int32, (piece, own), 1), 1.0, 0.0).astype(BF16)
    query, key, value = (dot(pick, ref[...]) for ref in (q_ref, k_ref, v_ref))
    gap = jnp.zeros((piece, HD), F32)
    wide = lax.broadcasted_iota(jnp.int32, (piece, cols), 0) + rep_ref[0] * piece
    for s in range(n):
        slots = range(s * heads, (s + 1) * heads)
        parts = [query[:, h * HD : (h + 1) * HD] if h < QH else gap for h in slots]
        for array in (key, value):
            for h in slots:
                j = h // GROUP
                parts.append(array[:, j * HD : (j + 1) * HD] if h < QH else gap)
        block = jnp.concatenate(parts, axis=1)
        for i in range(2):
            block = jnp.where(wide == own + i, gain_ref[i : i + 1, :], block)
        qkv_msg_ref[s] = block.astype(BF16)
    rows = to_blocks(dot(pick, out_ref[...]), n, out_msg_ref.shape[2]).astype(BF16)
    for s in range(n):
        out_msg_ref[s] = rows


def join_kernel(reps, rep_ref, *refs):
    for i in range(reps):
        refs[reps][:, rep_ref[0] ^ i] = refs[i][...]


def hidden_message_kernel(n, reps, block, rep_ref, core_ref, gate_ref, up_ref, down_ref, *msg_refs):
    own, units = gate_ref.shape
    held = down_ref.shape[0]
    each = held // (2 * reps)
    cols = n * each
    padded = round_up(each, 16)
    place = lax.broadcasted_iota(jnp.int32, (1, cols), 1)
    for i, msg_ref in enumerate(msg_refs):
        begin = each * (2 * rep_ref[0] + (core_ref[0] ^ i))
        unit = place + begin
        for s in range(1, n):
            unit = unit + jnp.where(place >= each * s, held - each, 0)
        pick = jnp.where(lax.broadcasted_iota(jnp.int32, (units, cols), 0) == unit, 1.0, 0.0)
        pick = pick.astype(BF16)
        both = jnp.concatenate([dot(gate_ref[...], pick), dot(up_ref[...], pick)], axis=1)
        both = jnp.concatenate([both, jnp.zeros((block - own, 2 * cols), F32)], axis=0)
        msg_ref[pl.ds(0, block), :] = both.astype(BF16)
        row = lax.broadcasted_iota(jnp.int32, (padded, held), 0)
        take = (lax.broadcasted_iota(jnp.int32, (padded, held), 1) == row + begin) & (row < each)
        down = to_blocks(dot(jnp.where(take, 1.0, 0.0).astype(BF16), down_ref[...]), n, n * block)
        for j, part in enumerate(chunks(down, 2 * cols)):
            msg_ref[pl.ds(block + j * padded, padded), :] = part.astype(BF16)


def chunks(values, cols):
    rows, width = values.shape
    parts = []
    for begin in range(0, width, cols):
        part = values[:, begin : begin + cols]
        if part.shape[1] < cols:
            part = jnp.concatenate([part, jnp.zeros((rows, cols - part.shape[1]), F32)], axis=1)
        parts.append(part)
    return parts


def hidden_weights_in_kernel(n, each, me_ref, *refs):
    parts, (w_ref, down_ref, rows_ref) = refs[:n], refs[n:]
    block, cols = w_ref.shape[1:]
    width = down_ref.shape[1]
    padded = rows_ref.shape[1]
    for i, part in enumerate(parts):
        s = me_ref[0] ^ i
        w_ref[s] = part[pl.ds(0, block), :]
        for j, begin in enumerate(range(0, width, cols)):
            size = min(cols, width - begin)
            rows = part[pl.ds(block + j * padded, padded), :].astype(F32)
            rows_ref[s, :, begin : begin + size] = rows[:, :size]
    down_ref[...] = jnp.concatenate([rows_ref[s][:each] for s in range(n)], axis=0).astype(BF16)


def attend_kernel(rows, n, me_ref, *refs):
    tokens, refs = refs[:n], refs[n:]
    w_ref, cos_ref, sin_ref, start_ref, first_ref, q_ref, k_ref, v_ref, mixed_ref, gains_ref = refs
    length, head_cols = q_ref.shape
    heads = head_cols // HD
    width = first_ref.shape[1]
    block_rows = width // n
    own = D // n
    gap = jnp.zeros((1, block_rows - own), F32)
    gains = []
    for i in range(2):
        parts = []
        for s in range(n):
            group = w_ref[pl.ds(s * block_rows + own // 16 * 16, block_rows - own // 16 * 16), :]
            row = own % 16 + i
            spread_row = group.astype(F32)[row : row + 1, :own]
            parts += [spread_row, gap]
        gains.append(jnp.concatenate(parts, axis=1))
        gains_ref[i : i + 1, :] = gains[i]
    for i, ref in enumerate(tokens):
        inputs = ref[...].astype(F32)
        normed = inputs * inverse_rms(inputs) * gains[0]
        first_ref[rows_at(me_ref[0] ^ i, rows), :] = normed.astype(BF16)
    block = min(256, length)
    for i in range(length // block):
        span = pl.ds(i * block, block)
        raw = dot(first_ref[span, :], w_ref[...])
        cosines, sines = cos_ref[span, :], sin_ref[span, :]
        query, key = raw[:, :head_cols], raw[:, head_cols : 2 * head_cols]
        q_ref[span, :] = (query * cosines + turned(query) * sines).astype(BF16)
        k_ref[span, :] = (key * cosines + turned(key) * sines).astype(BF16)
        v_ref[span, :] = raw[:, 2 * head_cols :].astype(BF16)
    for i in range(length // block):
        span, past = pl.ds(i * block, block), pl.ds(0, (i + 1) * block)
        total = None
        for h in range(heads):
            probs = masked_probs(
                head_of(q_ref[span, :], h, heads), k_ref[past, :], start_ref[span, :], i * block
            )
            mixed = head_of(dot(probs.astype(BF16), v_ref[past, :]), h, heads)
            total = mixed if total is None else total + mixed
        mixed_ref[span, :] = total.astype(BF16)


def attend_back_kernel(
    first_ref, q_ref, k_ref, v_ref, g_ref, cos_ref, sin_ref, start_ref, dqkv_ref, piece_ref, dk_ref, dv_ref
):
    length, head_cols = q_ref.shape
    heads = head_cols // HD
    block = min(256, length)
    dk_ref[...] = jnp.zeros_like(dk_ref)
    dv_ref[...] = jnp.zeros_like(dv_ref)
    for i in range(length // block):
        span, past = pl.ds(i * block, block), pl.ds(0, (i + 1) * block)
        total = None
        for h in range(heads):
            query = head_of(q_ref[span, :], h, heads)
            grad = head_of(g_ref[span, :], h, heads)
            key = k_ref[past, :]
            probs = masked_probs(query, key, start_ref[span, :], i * block)
            grad_probs = contract_cols(grad, v_ref[past, :])
            delta = jnp.sum(probs * grad_probs, axis=-1, keepdims=True)
            grad_logits = (probs * (grad_probs - delta)).astype(BF16)
            grad_query = head_of(dot(grad_logits, key), h, heads)
            total = grad_query if total is None else total + grad_query
            dv_ref[past, :] += contract_rows(probs.astype(BF16), grad)
            dk_ref[past, :] += contract_rows(grad_logits, query)
        total = total * SCALE
        back = total * cos_ref[span, :] - turned(total) * sin_ref[span, :]
        dqkv_ref[span, :head_cols] = back.astype(BF16)
    for i in range(length // block):
        span = pl.ds(i * block, block)
        total = dk_ref[span, :] * SCALE
        back = total * cos_ref[span, :] - turned(total) * sin_ref[span, :]
        dqkv_ref[span, head_cols : 2 * head_cols] = back.astype(BF16)
        dqkv_ref[span, 2 * head_cols :] = dv_ref[span, :].astype(BF16)
    store_pieces(piece_ref, contract_rows(first_ref[...], dqkv_ref[...]))


def store_pieces(piece_ref, grad):
    reps, n, piece, cols = piece_ref.shape
    for s in range(n):
        for r in range(reps):
            begin = (s * reps + r) * piece
            piece_ref[r, s] = grad[begin : begin + piece].astype(BF16)


def first_grad_kernel(rows, side, me_ref, dqkv_ref, w_ref, out_ref):
    for z in range(out_ref.shape[0]):
        part = dqkv_ref[rows_at(me_ref[0] ^ (2 * z + side), rows), :]
        out_ref[z] = contract_cols(part, w_ref[...]).astype(BF16)


def pair_sum_kernel(mine_ref, other_ref, *out_refs):
    for i, ref in enumerate(out_refs):
        ref[...] = (mine_ref[i].astype(F32) + other_ref[i].astype(F32)).astype(BF16)


def middle_kernel(n, tokens_ref, mixed_ref, w_ref, gains_ref, middle_ref, second_ref, attended_ref):
    width = tokens_ref.shape[1]
    attended = jnp.concatenate([mixed_ref[s] for s in range(n)], axis=1)[:, :D]
    attended = to_blocks(attended.astype(F32), n, width).astype(BF16)
    attended_ref[...] = attended
    middle = tokens_ref[...].astype(F32) + dot(attended, w_ref[...])
    middle_ref[...] = middle
    second_ref[...] = (middle * inverse_rms(middle) * gains_ref[1:2, :]).astype(BF16)


def stacked(refs):
    return jnp.concatenate([ref[...] for ref in refs], axis=0)


def hidden_kernel(reps, *refs):
    seconds, cots = refs[:reps], refs[reps : 2 * reps]
    w_ref, down_ref, grad_ref, grads_ref, hidden_ref = refs[2 * reps :]
    rows = seconds[0].shape[0]
    units = down_ref.shape[0]
    for i in range(0, reps, 2):
        span = pl.ds(i * rows, 2 * rows)
        both = dot(stacked(seconds[i : i + 2]), w_ref[...])
        gate, up = both[:, :units], both[:, units:]
        grad_hidden = contract_cols(stacked(cots[i : i + 2]), down_ref[...])
        sigmoid = 1.0 / (1.0 + jnp.exp(-gate))
        silu = gate * sigmoid
        hidden_ref[span, :] = (silu * up).astype(BF16)
        grad_gate = grad_hidden * up * sigmoid * (1.0 + gate * (1.0 - sigmoid))
        grads = jnp.concatenate([grad_gate, grad_hidden * silu], axis=1).astype(BF16)
        grads_ref[span, :] = grads
        grad = contract_cols(grads, w_ref[...]).astype(BF16)
        for j in range(2):
            grad_ref[i + j] = grad[j * rows : (j + 1) * rows]


def hidden_weights_kernel(reps, n, each, me_ref, *refs):
    seconds, cots = refs[: 2 * reps], refs[2 * reps : 4 * reps]
    (grads_a, grads_b, hidden_a, hidden_b), refs = refs[4 * reps : 4 * reps + 4], refs[4 * reps + 4 :]
    msg_refs, (grad_ref, rows_ref) = refs[:n], refs[n:]
    block, cols = grad_ref.shape[1:]
    padded = rows_ref.shape[1]
    grad = contract_rows(stacked(seconds[:reps]), grads_a[...])
    grad = grad + contract_rows(stacked(seconds[reps:]), grads_b[...])
    down = contract_rows(hidden_a[...], stacked(cots[:reps]))
    down = down + contract_rows(hidden_b[...], stacked(cots[reps:]))
    gap = jnp.zeros((padded - each, down.shape[1]), F32)
    for s in range(n):
        grad_ref[s] = grad[s * block : (s + 1) * block].astype(BF16)
        rows_ref[s] = jnp.concatenate([down[s * each : (s + 1) * each], gap], axis=0)
    for i, msg_ref in enumerate(msg_refs):
        s = me_ref[0] ^ i
        msg_ref[pl.ds(0, block), :] = grad_ref[s]
        for j, part in enumerate(chunks(rows_ref[s], cols)):
            msg_ref[pl.ds(block + j * padded, padded), :] = part.astype(BF16)


def core_sums_kernel(n, *refs):
    for core in range(2):
        total = sum(refs[i][...].astype(F32) for i in range(core, n, 2))
        refs[n][core] = total.astype(BF16)


def hidden_out_kernel(n, reps, each, rep_ref, core_ref, *refs):
    parts, refs = refs[:reps], refs[reps:]
    gate_w_ref, up_w_ref, gain_ref, gate_ref, up_ref, down_ref, norm_ref, hold_ref = refs
    own = gate_ref.shape[0]
    for i, part in enumerate(parts):
        for core in range(2):
            hold_ref[2 * (rep_ref[0] ^ i) + (core_ref[0] ^ core)] = part[core]
    cols = hold_ref.shape[2]
    block = round_up(own + 2, 16)
    padded = round_up(each, 16)
    total = jnp.zeros((own, 1), F32)
    for begin, w_ref, out_ref in ((0, gate_w_ref, gate_ref), (cols // 2, up_w_ref, up_ref)):
        held = [hold_ref[f, pl.ds(0, block), :].astype(F32)[:own] for f in range(2 * reps)]
        for s in range(n):
            place = begin + s * each
            rows = jnp.concatenate([part[:, place : place + each] for part in held], axis=1)
            span = slice(s * 2 * reps * each, (s + 1) * 2 * reps * each)
            out_ref[:, span] = rows
            total = total + jnp.sum(rows * w_ref[:, span].astype(F32), axis=1, keepdims=True)
    norm_ref[...] = total / gain_ref[...]
    width = n * block
    for f in range(2 * reps):
        rows = []
        for j, start in enumerate(range(0, width, cols)):
            part = hold_ref[f, pl.ds(block + j * padded, padded), :].astype(F32)[:each]
            rows.append(part[:, : min(cols, width - start)])
        rows = from_blocks(jnp.concatenate(rows, axis=1), n, own)
        down_ref[f * each : (f + 1) * each, :] = rows


def down_kernel(hidden_ref, w_ref, out_ref):
    rows = out_ref.shape[1]
    for i in range(0, out_ref.shape[0], 2):
        both = dot(hidden_ref[pl.ds(i * rows, 2 * rows), :], w_ref[...]).astype(BF16)
        for j in range(2):
            out_ref[i + j] = both[j * rows : (j + 1) * rows]


def output_kernel(n, own, middle_ref, *refs):
    total = middle_ref[...]
    for ref in refs[:-1]:
        total = total + ref[...].astype(F32)
    refs[-1][...] = from_blocks(total, n, own).astype(BF16)


def middle_grad_kernel(n, own, reps, *refs):
    parts, refs = refs[:reps], refs[reps:]
    cot_ref, middle_ref, gains_ref, w_ref, grad_ref, branch_ref, heads_ref = refs
    rows = cot_ref.shape[0]
    middle = middle_ref[...]
    grad_second = sum(ref[...].astype(F32) for ref in parts)
    grad = cot_ref[...].astype(F32) + norm_backward(
        middle, inverse_rms(middle), gains_ref[1:2, :], grad_second
    )
    grad_ref[...] = grad
    branch = grad.astype(BF16)
    branch_ref[...] = branch
    attended = from_blocks(contract_cols(branch, w_ref[...]), n, own)
    head_cols = heads_ref.shape[2]
    if n * head_cols > D:
        attended = jnp.concatenate([attended, jnp.zeros((rows, n * head_cols - D), F32)], axis=1)
    for s in range(n):
        heads_ref[s] = attended[:, s * head_cols : (s + 1) * head_cols].astype(BF16)


def out_weights_kernel(attended_ref, branch_ref, piece_ref):
    store_pieces(piece_ref, contract_rows(attended_ref[...], branch_ref[...]))


def rep_sum_kernel(reps, *refs):
    total = sum(ref[...].astype(F32) for ref in refs[:reps])
    refs[reps][...] = total.astype(BF16)


def owner_sum_kernel(in_ref, out_ref):
    out_ref[...] = jnp.sum(in_ref[...].astype(F32), axis=0).astype(BF16)


def out_out_kernel(n, reps, rep_ref, *refs):
    out_ref, hold_ref = refs[reps:]
    for i in range(reps):
        hold_ref[rep_ref[0] ^ i] = refs[i][...].astype(F32)
    own = out_ref.shape[0]
    rows = jnp.concatenate([hold_ref[r] for r in range(reps)], axis=0)[:own]
    out_ref[...] = from_blocks(rows, n, own)


def attention_out_kernel(n, reps, rep_ref, *refs):
    parts, refs = refs[:reps], refs[reps:]
    q_w_ref, k_w_ref, v_w_ref, gain_ref, q_ref, k_ref, v_ref, norm_ref, hold_ref = refs
    own = q_ref.shape[0]
    cols = parts[0].shape[2]
    head_cols = cols // 3
    heads = head_cols // HD
    for i, part in enumerate(parts):
        for s in range(n):
            hold_ref[rep_ref[0] ^ i, s] = part[s].astype(F32)
    sides = [
        jnp.concatenate([hold_ref[r, s] for r in range(reps)], axis=0)[:own] for s in range(n)
    ]

    def slot(h, kind):
        begin = kind * head_cols + h % heads * HD
        return sides[h // heads][:, begin : begin + HD]

    query = jnp.concatenate([slot(h, 0) for h in range(QH)], axis=1)
    q_ref[...] = query
    total = jnp.sum(query * q_w_ref[...].astype(F32), axis=1, keepdims=True)
    for kind, w_ref, out_ref in ((1, k_w_ref, k_ref), (2, v_w_ref, v_ref)):
        wide = jnp.concatenate(
            [sum(slot(j * GROUP + g, kind) for g in range(GROUP)) for j in range(KVH)], axis=1
        )
        out_ref[...] = wide
        total = total + jnp.sum(wide * w_ref[...].astype(F32), axis=1, keepdims=True)
    norm_ref[...] = total / gain_ref[...]


def input_grad_kernel(n, own, nz, *refs):
    parts, (tokens_ref, gains_ref, grad_ref, out_ref) = refs[:nz], refs[nz:]
    inputs = tokens_ref[...].astype(F32)
    grad_first = sum(ref[...].astype(F32) for ref in parts)
    total = grad_ref[...] + norm_backward(inputs, inverse_rms(inputs), gains_ref[0:1, :], grad_first)
    out_ref[...] = from_blocks(total, n, own)


def shards(
    tokens,
    lengths,
    norm_one,
    w_query,
    w_key,
    w_value,
    w_out,
    norm_two,
    w_gate,
    w_up,
    w_down,
    cotangent,
):
    n = lax.axis_size("shard")
    reps = lax.axis_size("rep")
    nz = n // 2
    rows = tokens.shape[0]
    length = rows * n
    own = w_query.shape[0]
    held = w_down.shape[0]
    block = round_up(own + 2, 16)
    width = n * block
    piece = block // reps
    heads = -(-QH // n)
    head_cols = heads * HD
    qkv_cols = 3 * head_cols
    each = held // (2 * reps)
    units = n * each
    padded = round_up(each, 16)
    msg_rows = block + -(-width // (2 * units)) * padded
    shard_index = lax.axis_index("shard").astype(jnp.int32)
    me = shard_index.reshape(1)
    core = (shard_index % 2).reshape(1)
    rep = lax.axis_index("rep").astype(jnp.int32).reshape(1)
    own_block = (rows, width)

    (tokens_in,) = call(lambda *r: blocks_kernel(n, *r), "tokens_blocks", [(own_block, BF16)], tokens)
    tokens_all = spread(tokens_in, "shard", 2)
    tokens_all = [part for pair in zip(tokens_all, [swap(p, "shard", 1) for p in tokens_all]) for part in pair]
    gains_own = jnp.pad(jnp.stack([norm_one, norm_two]), ((0, 0), (0, qkv_cols - own))).astype(F32)
    qkv_message, out_message = call(
        lambda *r: attention_message_kernel(n, *r),
        "attention_message",
        [((n, piece, qkv_cols), BF16), ((n, piece, width), BF16)],
        w_query,
        w_key,
        w_value,
        w_out,
        gains_own,
        scalars=(rep,),
    )

    def joined(arrived, name):
        cols = arrived.shape[2]
        parts = spread(arrived, "rep", 1)
        (whole,) = call(
            lambda *r: join_kernel(reps, *r), name, [((n, reps, piece, cols), BF16)], *parts, scalars=(rep,)
        )
        return whole.reshape(width, cols)

    w_qkv = joined(exchange(qkv_message), "join_qkv")

    (cot_in,) = call(lambda *r: blocks_kernel(n, *r), "cot_blocks", [(own_block, BF16)], cotangent)
    cots = with_cores(spread(cot_in, "rep", 1))
    messages = call(
        lambda *r: hidden_message_kernel(n, reps, block, *r),
        "hidden_message",
        [((msg_rows, 2 * units), BF16)] * 2,
        w_gate,
        w_up,
        w_down,
        scalars=(rep, core),
    )
    out_message, messages, tokens_all = lax.optimization_barrier((out_message, messages, tokens_all))
    out_full = joined(exchange(out_message), "join_out")
    arrived = [messages[0]] + [swap(messages[k % 2], "shard", k) for k in range(1, n)]
    w_hidden, w_down_in = call(
        lambda *r: hidden_weights_in_kernel(n, each, *r),
        "hidden_weights_in",
        [((n, block, 2 * units), BF16), ((units, width), BF16)],
        *arrived,
        scalars=(me,),
        scratch=[((n, padded, width), F32)],
    )
    w_hidden = w_hidden.reshape(width, 2 * units)

    doc_start, position = doc_layout(lengths[0], length)
    cosines, sines = rope_tables(position)
    cosines = jnp.tile(cosines, (1, 2 * heads))
    sines = jnp.tile(sines, (1, 2 * heads))
    start = doc_start[:, None]
    head_shape = (length, head_cols)
    first_all, query, key, value, mixed, gains = call(
        lambda *r: attend_kernel(rows, n, *r),
        "attend",
        [((length, width), BF16)] + [(head_shape, BF16)] * 4 + [((2, width), F32)],
        *tokens_all,
        w_qkv,
        cosines,
        sines,
        start,
        scalars=(me,),
    )
    mixed = exchange(mixed.reshape(n, rows, head_cols))

    middle, second, attended = call(
        lambda *r: middle_kernel(n, *r),
        "middle",
        [(own_block, F32), (own_block, BF16), (own_block, BF16)],
        tokens_in,
        mixed,
        out_full,
        gains,
    )

    seconds = with_cores(spread(second, "rep", 1))
    side_outs = [
        ((reps, rows, width), BF16),
        ((reps * rows, 2 * units), BF16),
        ((reps * rows, units), BF16),
    ]

    def hidden_side(side, name):
        span = slice(side * reps, (side + 1) * reps)
        return call(
            lambda *r: hidden_kernel(reps, *r),
            name,
            side_outs,
            *seconds[span],
            *cots[span],
            w_hidden,
            w_down_in,
        )

    def plane_sums(mine, other):
        sums = call(pair_sum_kernel, "pair_sum", [(own_block, BF16)] * reps, mine, swap(other, "shard", 1))
        return deliver(sums, "rep", 1)

    grad_other, grads_other, hidden_other = hidden_side(1, "hidden_other")
    grad_mine, grads_mine, hidden_mine = hidden_side(0, "hidden_mine")
    grad_second = plane_sums(grad_mine, grad_other)
    hidden_messages = call(
        lambda *r: hidden_weights_kernel(reps, n, each, *r),
        "hidden_weights",
        [((msg_rows, 2 * units), BF16)] * n,
        *seconds,
        *cots,
        grads_mine,
        grads_other,
        hidden_mine,
        hidden_other,
        scalars=(me,),
        scratch=[((n, block, 2 * units), BF16), ((n, padded, width), F32)],
    )
    hidden_messages = deliver(hidden_messages, "shard", 1)

    grad_middle, grad_branch, grad_heads = call(
        lambda *r: middle_grad_kernel(n, own, reps, *r),
        "middle_grad",
        [(own_block, F32), (own_block, BF16), ((n, rows, head_cols), BF16)],
        *grad_second,
        cot_in,
        middle,
        gains,
        out_full,
    )
    grad_heads = exchange(grad_heads).reshape(head_shape)
    (out_pieces,) = call(
        out_weights_kernel, "out_weights", [((reps, n, piece, width), BF16)], attended, grad_branch
    )

    grad_qkv, attention_pieces = call(
        attend_back_kernel,
        "attend_back",
        [((length, qkv_cols), BF16), ((reps, n, piece, qkv_cols), BF16)],
        first_all,
        query,
        key,
        value,
        grad_heads,
        cosines,
        sines,
        start,
        scratch=[(head_shape, F32)] * 2,
    )
    first_sides = [
        call(
            lambda *r, side=side: first_grad_kernel(rows, side, *r),
            "first_grad",
            [((nz, rows, width), BF16)],
            grad_qkv,
            w_qkv,
            scalars=(me,),
        )[0]
        for side in (1, 0)
    ]
    first_sums = call(
        pair_sum_kernel, "pair_sum", [(own_block, BF16)] * nz, first_sides[1], swap(first_sides[0], "shard", 1)
    )
    (input_grad,) = call(
        lambda *r: input_grad_kernel(n, own, nz, *r),
        "input_grad",
        [((rows, D), F32)],
        *deliver(first_sums, "shard", 2),
        tokens_in,
        gains,
        grad_middle,
    )

    def owner_pieces(pieces):
        blocks = [lax.dynamic_index_in_dim(pieces, rep[0] ^ k, 0, keepdims=False) for k in range(reps)]
        parts = deliver(blocks, "rep", 1)
        (summed,) = call(
            lambda *r: rep_sum_kernel(reps, *r), "rep_sum", [(pieces.shape[1:], BF16)], *parts
        )
        return exchange(summed)

    gain_cols = [gain.astype(F32)[:, None] for gain in (norm_one, norm_two)]
    attention_parts = spread(owner_pieces(attention_pieces), "rep", 1)
    grad_w_query, grad_w_key, grad_w_value, grad_norm_one = call(
        lambda *r: attention_out_kernel(n, reps, *r),
        "attention_out",
        [(w_query.shape, F32), (w_key.shape, F32), (w_value.shape, F32), ((own, 1), F32)],
        *attention_parts,
        w_query,
        w_key,
        w_value,
        gain_cols[0],
        scalars=(rep,),
        scratch=[((reps, n, piece, qkv_cols), F32)],
    )

    (out_piece,) = call(owner_sum_kernel, "owner_sum", [((piece, width), BF16)], owner_pieces(out_pieces))
    (grad_w_out,) = call(
        lambda *r: out_out_kernel(n, reps, *r),
        "out_out",
        [(w_out.shape, F32)],
        *spread(out_piece, "rep", 1),
        scalars=(rep,),
        scratch=[((reps, piece, width), F32)],
    )

    (core_sums,) = call(
        lambda *r: core_sums_kernel(n, *r), "core_sums", [((2, msg_rows, 2 * units), BF16)], *hidden_messages
    )
    grad_w_gate, grad_w_up, grad_w_down, grad_norm_two = call(
        lambda *r: hidden_out_kernel(n, reps, each, *r),
        "hidden_out",
        [(w_gate.shape, F32), (w_up.shape, F32), (w_down.shape, F32), ((own, 1), F32)],
        *spread(core_sums, "rep", 1),
        w_gate,
        w_up,
        gain_cols[1],
        scalars=(rep, core),
        scratch=[((2 * reps, msg_rows, 2 * units), BF16)],
    )

    down_parts = [
        call(down_kernel, "down", [((reps, rows, width), BF16)], hidden, w_down_in)[0]
        for hidden in (hidden_other, hidden_mine)
    ]
    (output,) = call(
        lambda *r: output_kernel(n, own, *r),
        "output",
        [((rows, D), BF16)],
        middle,
        *plane_sums(down_parts[1], down_parts[0]),
    )
    return (
        output,
        input_grad,
        grad_norm_one[:, 0],
        grad_w_query,
        grad_w_key,
        grad_w_value,
        grad_w_out,
        grad_norm_two[:, 0],
        grad_w_gate,
        grad_w_up,
        grad_w_down,
    )


def solution(mesh):
    rows = P("shard", None)
    own_tokens = P(("rep", "shard"), None)
    return jax.shard_map(
        shards,
        mesh=mesh,
        in_specs=(
            own_tokens,
            P("rep", None),
            P("shard"),
            rows,
            rows,
            rows,
            rows,
            P("shard"),
            rows,
            rows,
            rows,
            own_tokens,
        ),
        out_specs=(
            own_tokens,
            own_tokens,
            P("shard"),
            rows,
            rows,
            rows,
            rows,
            P("shard"),
            rows,
            rows,
            rows,
        ),
        check_vma=False,
    )
```

profile of v0, /device:TPU:10, one launch (start us, length us, event | category | flops | bytes accessed | tf_op | source)
XLA Modules:
  0.0 400.0 jit_solution(9879692027777857436)
XLA Ops:
  14.6 6.2 %all-to-all-start = ((bf16[8,32,384]{2,1,0:T(8,128)(2,1)}), bf16[8,32,384]{2,1,0:T(8,128)(2,1)S(1)}, u32[]{:S(2)}, u32[]{:S(2)}) async-start(bf16[8,32,384]{2,1,0:T(8,128)(2,1)} %get-tuple-element.87), calls=%async_computation | async-start | bytes 393216 | tf_op jit(solution)/shard_map/all_to_all | solution.py:92
  21.4 6.3 %collective-permute-done.3.r_5_ = bf16[128,1024]{1,0:T(8,128)(2,1)S(1)} collective-permute-done((bf16[128,1024]{1,0:T(8,128)(2,1)}, bf16[128,1024]{1,0:T(8,128)(2,1)S(1)}, u32[]{:S(2)}, u32[]{:S(2)}) %collective-permute-start.3) | collective-permute-done | bytes 262176 | tf_op jit(solution)/shard_map/ppermute | solution.py:88
  27.7 6.1 %collective-permute-done.5.r_7_ = bf16[128,1024]{1,0:T(8,128)(2,1)S(1)} collective-permute-done((bf16[128,1024]{1,0:T(8,128)(2,1)}, bf16[128,1024]{1,0:T(8,128)(2,1)S(1)}, u32[]{:S(2)}, u32[]{:S(2)}) %collective-permute-start.5) | collective-permute-done | bytes 262176 | tf_op jit(solution)/shard_map/ppermute | solution.py:88
  49.6 5.9 %collective-permute-done.16.r_5_.r_10_ = bf16[128,1024]{1,0:T(8,128)(2,1)S(1)} collective-permute-done((bf16[128,1024]{1,0:T(8,128)(2,1)}, bf16[128,1024]{1,0:T(8,128)(2,1)S(1)}, u32[]{:S(2)}, u32[]{:S(2)}) %collective-permute-start.16) | collective-permute-done | bytes 262176 | tf_op jit(solution)/shard_map/ppermute | solution.py:88
  68.2 5.1 %collective-permute-done.8.r_3_ = bf16[8,32,384]{2,1,0:T(8,128)(2,1)} collective-permute-done((bf16[8,32,384]{2,1,0:T(8,128)(2,1)S(1)}, bf16[8,32,384]{2,1,0:T(8,128)(2,1)}, u32[]{:S(2)}, u32[]{:S(2)}) %collective-permute-start.8) | collective-permute-done | bytes 196640 | tf_op jit(solution)/shard_map/ppermute | solution.py:88
  81.1 9.2 %attend.1 = (bf16[1024,1024]{1,0:T(8,128)(2,1)}, bf16[1024,128]{1,0:T(8,128)(2,1)}, bf16[1024,128]{1,0:T(8,128)(2,1)}, bf16[1024,128]{1,0:T(8,128)(2,1)}, bf16[1024,128]{1,0:T(8,128)(2,1)}, /*index=5*/f32[2,1024]{1,0:T(2,128)}) custom-call(s32[1]{0:T(128)} %bitcast.r_0_, bf16[128,1024]{1,0:T(8,128)(2,1)} %tokens_blocks.1.r_1_.r_0_.r_4_, ...), custom_call_target="tpu_custom_call" | custom-call | tf_op jit(solution)/shard_map/attend/pallas_call | solution.py:110
  90.2 5.3 %all-to-all-start.1 = ((bf16[8,128,128]{2,1,0:T(8,128)(2,1)}), bf16[8,128,128]{2,1,0:T(8,128)(2,1)S(1)}, u32[]{:S(2)}, u32[]{:S(2)}) async-start(bf16[8,128,128]{2,1,0:T(8,128)(2,1)} %bitcast.48), calls=%async_computation.1 | async-start | bytes 524288 | tf_op jit(solution)/shard_map/all_to_all | solution.py:92
  114.1 18.5 %collective-permute-done.22.r_5_ = bf16[224,640]{1,0:T(8,128)(2,1)S(1)} collective-permute-done((bf16[224,640]{1,0:T(8,128)(2,1)}, bf16[224,640]{1,0:T(8,128)(2,1)S(1)}, u32[]{:S(2)}, u32[]{:S(2)}) %collective-permute-start.22) | collective-permute-done | bytes 286752 | tf_op jit(solution)/shard_map/ppermute | solution.py:88
  141.5 5.8 %collective-permute-done.24.r_7_ = bf16[224,640]{1,0:T(8,128)(2,1)S(1)} collective-permute-done((bf16[224,640]{1,0:T(8,128)(2,1)}, bf16[224,640]{1,0:T(8,128)(2,1)S(1)}, u32[]{:S(2)}, u32[]{:S(2)}) %collective-permute-start.24) | collective-permute-done | bytes 286752 | tf_op jit(solution)/shard_map/ppermute | solution.py:88
  157.9 5.7 %hidden_other.1 = (bf16[4,128,1024]{2,1,0:T(8,128)(2,1)}, bf16[512,640]{1,0:T(8,128)(2,1)}, bf16[512,320]{1,0:T(8,128)(2,1)}) custom-call(bf16[128,1024]{1,0:T(8,128)(2,1)} %copy-done.13, bf16[128,1024]{1,0:T(8,128)(2,1)} %copy-done.14, bf16[128,1024]{1,0:T(8,128)(2,1)} %copy-done.15, bf16[128,1024]{1,0:T(8,128)(2,1)} %copy-done.16, ...), custom_call_target="tpu_custom_call" | custom-call | tf_op jit(solution)/shard_map/hidden_other/pallas_call | solution.py:110
  163.9 5.7 %hidden_mine.1 = (bf16[4,128,1024]{2,1,0:T(8,128)(2,1)}, bf16[512,640]{1,0:T(8,128)(2,1)}, bf16[512,320]{1,0:T(8,128)(2,1)}) custom-call(bf16[128,1024]{1,0:T(8,128)(2,1)} %get-tuple-element.92.r_0_.r_1_, bf16[128,1024]{1,0:T(8,128)(2,1)} %copy-done.9, bf16[128,1024]{1,0:T(8,128)(2,1)} %copy-done.10, bf16[128,1024]{1,0:T(8,128)(2,1)} %copy-done.11, ...), custom_call_target="tpu_custom_call" | custom-call | tf_op jit(solution)/shard_map/hidden_mine/pallas_call | solution.py:110
  176.6 5.9 %collective-permute-done.39.r_1_ = bf16[128,1024]{1,0:T(8,128)(2,1)S(1)} collective-permute-done((bf16[128,1024]{1,0:T(8,128)(2,1)}, bf16[128,1024]{1,0:T(8,128)(2,1)S(1)}, u32[]{:S(2)}, u32[]{:S(2)}) %collective-permute-start.39) | collective-permute-done | bytes 262176 | tf_op jit(solution)/shard_map/ppermute | solution.py:88
  182.5 5.6 %collective-permute-done.40.r_2_ = bf16[128,1024]{1,0:T(8,128)(2,1)S(1)} collective-permute-done((bf16[128,1024]{1,0:T(8,128)(2,1)}, bf16[128,1024]{1,0:T(8,128)(2,1)S(1)}, u32[]{:S(2)}, u32[]{:S(2)}) %collective-permute-start.40) | collective-permute-done | bytes 262176 | tf_op jit(solution)/shard_map/ppermute | solution.py:88
  197.2 6.7 %hidden_weights.1 = (bf16[224,640]{1,0:T(8,128)(2,1)}, bf16[224,640]{1,0:T(8,128)(2,1)}, bf16[224,640]{1,0:T(8,128)(2,1)}, bf16[224,640]{1,0:T(8,128)(2,1)}, bf1...) custom-call(s32[1]{0:T(128)} %bitcast.r_0_, ...), custom_call_target="tpu_custom_call" | custom-call | tf_op jit(solution)/shard_map/hidden_weights/pallas_call | solution.py:110
  209.6 11.4 %attend_back.1 = (bf16[1024,384]{1,0:T(8,128)(2,1)}, bf16[4,8,32,384]{3,2,1,0:T(8,128)(2,1)}) custom-call(bf16[1024,1024]{1,0:T(8,128)(2,1)} %get-tuple-element.103.first_ref, bf16[1024,128]{1,0:T(8,128)(2,1)} %get-tuple-element.104.q_ref, bf16[1024,128]{1,0:T(8,128)(2,1)} %get-tuple-element.105.k_ref, bf16[1024,128]{1,0:T(8,128)(2,1)} %get-tuple-element.106.v_ref, ...), custom_call_target="tpu_custom_call" | custom-call | tf_op jit(solution)/shard_map/attend_back/pallas_call | solution.py:110
  238.1 20.1 %collective-permute-done.48.r_3_ = bf16[8,32,384]{2,1,0:T(8,128)(2,1)S(1)} collective-permute-done((bf16[8,32,384]{2,1,0:T(8,128)(2,1)S(1)}, bf16[8,32,384]{2,1,0:T(8,128)(2,1)S(1)}, u32[]{:S(2)}, u32[]{:S(2)}) %collective-permute-start.48) | collective-permute-done | bytes 196640 | tf_op jit(solution)/shard_map/ppermute | solution.py:88
  260.8 5.1 %all-to-all-start.4 = ((bf16[8,32,384]{2,1,0:T(8,128)(2,1)}), bf16[8,32,384]{2,1,0:T(8,128)(2,1)S(1)}, u32[]{:S(2)}, u32[]{:S(2)}) async-start(bf16[8,32,384]{2,1,0:T(8,128)(2,1)} %rep_sum.2), calls=%async_computation.4 | async-start | bytes 393216 | tf_op jit(solution)/shard_map/all_to_all | solution.py:92
  276.0 5.8 %all-to-all-start.5 = ((bf16[8,32,1024]{2,1,0:T(8,128)(2,1)}), bf16[8,32,1024]{2,1,0:T(8,128)(2,1)S(1)}, u32[]{:S(2)}, u32[]{:S(2)}) async-start(bf16[8,32,1024]{2,1,0:T(8,128)(2,1)} %rep_sum.3), calls=%async_computation.5 | async-start | bytes 1048576 | tf_op jit(solution)/shard_map/all_to_all | solution.py:92
  281.7 21.3 %collective-permute-done.62.r_5_ = bf16[224,640]{1,0:T(8,128)(2,1)} collective-permute-done((bf16[224,640]{1,0:T(8,128)(2,1)}, bf16[224,640]{1,0:T(8,128)(2,1)}, u32[]{:S(2)}, u32[]{:S(2)}) %collective-permute-start.62) | collective-permute-done | bytes 286752 | tf_op jit(solution)/shard_map/ppermute | solution.py:88
  303.0 6.3 %collective-permute-done.63.r_6_ = bf16[224,640]{1,0:T(8,128)(2,1)} collective-permute-done((bf16[224,640]{1,0:T(8,128)(2,1)}, bf16[224,640]{1,0:T(8,128)(2,1)}, u32[]{:S(2)}, u32[]{:S(2)}) %collective-permute-start.63) | collective-permute-done | bytes 286752 | tf_op jit(solution)/shard_map/ppermute | solution.py:88
  309.3 6.0 %collective-permute-done.64.r_7_ = bf16[224,640]{1,0:T(8,128)(2,1)} collective-permute-done((bf16[224,640]{1,0:T(8,128)(2,1)}, bf16[224,640]{1,0:T(8,128)(2,1)}, u32[]{:S(2)}, u32[]{:S(2)}) %collective-permute-start.64) | collective-permute-done | bytes 286752 | tf_op jit(solution)/shard_map/ppermute | solution.py:88
  328.6 5.4 %collective-permute-done.65.r_3_ = bf16[2,224,640]{2,1,0:T(8,128)(2,1)S(1)} collective-permute-done((bf16[2,224,640]{2,1,0:T(8,128)(2,1)}, bf16[2,224,640]{2,1,0:T(8,128)(2,1)S(1)}, u32[]{:S(2)}, u32[]{:S(2)}) %collective-permute-start.65) | collective-permute-done | bytes 573472 | tf_op jit(solution)/shard_map/ppermute | solution.py:88
  334.5 11.7 %collective-permute-done.66.r_4_ = bf16[2,224,640]{2,1,0:T(8,128)(2,1)S(1)} collective-permute-done((bf16[2,224,640]{2,1,0:T(8,128)(2,1)}, bf16[2,224,640]{2,1,0:T(8,128)(2,1)S(1)}, u32[]{:S(2)}, u32[]{:S(2)}) %collective-permute-start.66) | collective-permute-done | bytes 573472 | tf_op jit(solution)/shard_map/ppermute | solution.py:88
  370.7 7.2 %hidden_out.1 = (f32[120,2560]{1,0:T(8,128)}, f32[120,2560]{1,0:T(8,128)}, f32[320,960]{1,0:T(8,128)}, f32[120,1]{1,0:T(8,128)}) custom-call(s32[1]{0:T(128)} %bitcast.1.r_0_, s32[1]{0:T(128)} %bitcast.4.r_1_, bf16[2,224,640]{2,1,0:T(8,128)(2,1)} %core_sums.1.r_2_, bf16[2,224,640]{2,1,0:T(8,128)(2,1)} %copy-done.24, bf16[2,224,640]{2,1,0:T(8,128)(2,1)} %copy-done.25, ...), custom_call_target="tpu_custom_call" | custom-call | tf_op jit(solution)/shard_map/hidden_out/pallas_call | solution.py:110
  (314 shorter events, 200.5 us)
Async XLA Ops:
  7.3 26.5 %collective-permute-start.5 = (bf16[128,1024]{1,0:T(8,128)(2,1)}, bf16[128,1024]{1,0:T(8,128)(2,1)S(1)}, u32[]{:S(2)}, u32[]{:S(2)}) collective-permute-start(bf16[128,1024]{1,0:T(8,128)(2,1)} %tokens_blocks.1.r_1_.r_0_.r_4_), channel_id=1, source_target_pairs={{0,6},{1,7},{2,4},{3,5},{4,2},{5,3},{6,0},{7,1},{8,14},{9,15},{10,... | collective-permute-start | bytes 786440 | tf_op jit(solution)/shard_map/ppermute | solution.py:88
  63.7 34.7 %collective-permute-start.10 = (bf16[8,32,1024]{2,1,0:T(8,128)(2,1)S(1)}, bf16[8,32,1024]{2,1,0:T(8,128)(2,1)S(1)}, u32[]{:S(2)}, u32[]{:S(2)}) collective-permute-start(bf16[8,32,1024]{2,1,0:T(8,128)(2,1)S(1)} %all-to-all-done.2.r_1_), channel_id=1, source_target_pairs={{0,8},{8,0},{16,24},{24,16},{1,9},{9,1},{17,25},{25,17},{2,10},{10... | collective-permute-start | bytes 1572872 | tf_op jit(solution)/shard_map/ppermute | solution.py:88
  65.7 29.9 %collective-permute-start.19 = (bf16[224,640]{1,0:T(8,128)(2,1)}, bf16[224,640]{1,0:T(8,128)(2,1)}, u32[]{:S(2)}, u32[]{:S(2)}) collective-permute-start(bf16[224,640]{1,0:T(8,128)(2,1)} %get-tuple-element.94), channel_id=1, source_target_pairs={{0,1},{1,0},{2,3},{3,2},{4,5},{5,4},{6,7},{7,6},{8,9},{9,8},{10,11... | collective-permute-start | bytes 860168 | tf_op jit(solution)/shard_map/ppermute | solution.py:88
  67.8 27.9 %collective-permute-start.20 = (bf16[224,640]{1,0:T(8,128)(2,1)}, bf16[224,640]{1,0:T(8,128)(2,1)}, u32[]{:S(2)}, u32[]{:S(2)}) collective-permute-start(bf16[224,640]{1,0:T(8,128)(2,1)} %get-tuple-element.93.r_1_), channel_id=1, source_target_pairs={{0,2},{1,3},{2,0},{3,1},{4,6},{5,7},{6,4},{7,5},{8,10},{9,11},{10,... | collective-permute-start | bytes 860168 | tf_op jit(solution)/shard_map/ppermute | solution.py:88
  95.7 36.8 %collective-permute-start.22 = (bf16[224,640]{1,0:T(8,128)(2,1)}, bf16[224,640]{1,0:T(8,128)(2,1)S(1)}, u32[]{:S(2)}, u32[]{:S(2)}) collective-permute-start(bf16[224,640]{1,0:T(8,128)(2,1)} %get-tuple-element.93.r_1_), channel_id=1, source_target_pairs={{0,4},{1,5},{2,6},{3,7},{4,0},{5,1},{6,2},{7,3},{8,12},{9,13},{10,... | collective-permute-start | bytes 860168 | tf_op jit(solution)/shard_map/ppermute | solution.py:88
  98.3 40.4 %collective-permute-start.23 = (bf16[224,640]{1,0:T(8,128)(2,1)}, bf16[224,640]{1,0:T(8,128)(2,1)S(1)}, u32[]{:S(2)}, u32[]{:S(2)}) collective-permute-start(bf16[224,640]{1,0:T(8,128)(2,1)} %get-tuple-element.94), channel_id=1, source_target_pairs={{0,5},{1,4},{2,7},{3,6},{4,1},{5,0},{6,3},{7,2},{8,13},{9,12},{10,... | collective-permute-start | bytes 860168 | tf_op jit(solution)/shard_map/ppermute | solution.py:88
  98.4 48.9 %collective-permute-start.24 = (bf16[224,640]{1,0:T(8,128)(2,1)}, bf16[224,640]{1,0:T(8,128)(2,1)S(1)}, u32[]{:S(2)}, u32[]{:S(2)}) collective-permute-start(bf16[224,640]{1,0:T(8,128)(2,1)} %get-tuple-element.93.r_1_), channel_id=1, source_target_pairs={{0,6},{1,7},{2,4},{3,5},{4,2},{5,3},{6,0},{7,1},{8,14},{9,15},{10,... | collective-permute-start | bytes 860168 | tf_op jit(solution)/shard_map/ppermute | solution.py:88
  100.9 51.7 %collective-permute-start.25 = (bf16[224,640]{1,0:T(8,128)(2,1)}, bf16[224,640]{1,0:T(8,128)(2,1)}, u32[]{:S(2)}, u32[]{:S(2)}) collective-permute-start(bf16[224,640]{1,0:T(8,128)(2,1)} %get-tuple-element.94), channel_id=1, source_target_pairs={{0,7},{1,6},{2,5},{3,4},{4,3},{5,2},{6,1},{7,0},{8,15},{9,14},{10,... | collective-permute-start | bytes 860168 | tf_op jit(solution)/shard_map/ppermute | solution.py:88
  112.5 40.4 %collective-permute-start.13 = (bf16[128,1024]{1,0:T(8,128)(2,1)}, bf16[128,1024]{1,0:T(8,128)(2,1)S(1)}, u32[]{:S(2)}, u32[]{:S(2)}) collective-permute-start(bf16[128,1024]{1,0:T(8,128)(2,1)} %get-tuple-element.92.r_0_.r_1_), channel_id=1, source_target_pairs={{0,8},{8,0},{16,24},{24,16},{1,9},{9,1},{17,25},{25,17},{2,10},{10... | collective-permute-start | bytes 786440 | tf_op jit(solution)/shard_map/ppermute | solution.py:88
  227.5 42.0 %collective-permute-start.52 = (bf16[8,32,1024]{2,1,0:T(8,128)(2,1)}, bf16[8,32,1024]{2,1,0:T(8,128)(2,1)S(1)}, u32[]{:S(2)}, u32[]{:S(2)}) collective-permute-start(bf16[8,32,1024]{2,1,0:T(8,128)(2,1)} %get-tuple-element.176), channel_id=1, source_target_pairs={{0,8},{8,0},{16,24},{24,16},{1,9},{9,1},{17,25},{25,17},{2,10},{10... | collective-permute-start | bytes 1572872 | tf_op jit(solution)/shard_map/ppermute | solution.py:88
  228.9 43.0 %collective-permute-start.53 = (bf16[8,32,1024]{2,1,0:T(8,128)(2,1)}, bf16[8,32,1024]{2,1,0:T(8,128)(2,1)S(1)}, u32[]{:S(2)}, u32[]{:S(2)}) collective-permute-start(bf16[8,32,1024]{2,1,0:T(8,128)(2,1)} %get-tuple-element.175), channel_id=1, source_target_pairs={{0,16},{8,24},{16,0},{24,8},{1,17},{9,25},{17,1},{25,9},{2,18},{10... | collective-permute-start | bytes 1572872 | tf_op jit(solution)/shard_map/ppermute | solution.py:88
  229.2 42.7 %collective-permute-start.54 = (bf16[8,32,1024]{2,1,0:T(8,128)(2,1)}, bf16[8,32,1024]{2,1,0:T(8,128)(2,1)}, u32[]{:S(2)}, u32[]{:S(2)}) collective-permute-start(bf16[8,32,1024]{2,1,0:T(8,128)(2,1)} %get-tuple-element.174), channel_id=1, source_target_pairs={{0,24},{8,16},{16,8},{24,0},{1,25},{9,17},{17,9},{25,1},{2,26},{10... | collective-permute-start | bytes 1572872 | tf_op jit(solution)/shard_map/ppermute | solution.py:88
  231.1 38.3 %collective-permute-start.61 = (bf16[224,640]{1,0:T(8,128)(2,1)}, bf16[224,640]{1,0:T(8,128)(2,1)}, u32[]{:S(2)}, u32[]{:S(2)}) collective-permute-start(bf16[224,640]{1,0:T(8,128)(2,1)} %get-tuple-element.133), channel_id=1, source_target_pairs={{0,4},{1,5},{2,6},{3,7},{4,0},{5,1},{6,2},{7,3},{8,12},{9,13},{10,... | collective-permute-start | bytes 860168 | tf_op jit(solution)/shard_map/ppermute | solution.py:88
  258.1 66.3 %collective-permute-start.34 = (bf16[4,128,1024]{2,1,0:T(8,128)(2,1)}, bf16[4,128,1024]{2,1,0:T(8,128)(2,1)S(1)}, u32[]{:S(2)}, u32[]{:S(2)}) collective-permute-start(bf16[4,128,1024]{2,1,0:T(8,128)(2,1)} %down.3), channel_id=1, source_target_pairs={{0,1},{1,0},{2,3},{3,2},{4,5},{5,4},{6,7},{7,6},{8,9},{9,8},{10,11... | collective-permute-start | bytes 3145736 | tf_op jit(solution)/shard_map/ppermute | solution.py:88
  269.3 78.4 %collective-permute-start.42 = (bf16[4,128,1024]{2,1,0:T(8,128)(2,1)}, bf16[4,128,1024]{2,1,0:T(8,128)(2,1)S(1)}, u32[]{:S(2)}, u32[]{:S(2)}) collective-permute-start(bf16[4,128,1024]{2,1,0:T(8,128)(2,1)} %first_grad.3), channel_id=1, source_target_pairs={{0,1},{1,0},{2,3},{3,2},{4,5},{5,4},{6,7},{7,6},{8,9},{9,8},{10,11... | collective-permute-start | bytes 3145736 | tf_op jit(solution)/shard_map/ppermute | solution.py:88
  269.6 33.5 %collective-permute-start.62 = (bf16[224,640]{1,0:T(8,128)(2,1)}, bf16[224,640]{1,0:T(8,128)(2,1)}, u32[]{:S(2)}, u32[]{:S(2)}) collective-permute-start(bf16[224,640]{1,0:T(8,128)(2,1)} %get-tuple-element.134), channel_id=1, source_target_pairs={{0,5},{1,4},{2,7},{3,6},{4,1},{5,0},{6,3},{7,2},{8,13},{9,12},{10,... | collective-permute-start | bytes 860168 | tf_op jit(solution)/shard_map/ppermute | solution.py:88
  271.9 37.4 %collective-permute-start.63 = (bf16[224,640]{1,0:T(8,128)(2,1)}, bf16[224,640]{1,0:T(8,128)(2,1)}, u32[]{:S(2)}, u32[]{:S(2)}) collective-permute-start(bf16[224,640]{1,0:T(8,128)(2,1)} %get-tuple-element.135), channel_id=1, source_target_pairs={{0,6},{1,7},{2,4},{3,5},{4,2},{5,3},{6,0},{7,1},{8,14},{9,15},{10,... | collective-permute-start | bytes 860168 | tf_op jit(solution)/shard_map/ppermute | solution.py:88
  271.9 43.4 %collective-permute-start.64 = (bf16[224,640]{1,0:T(8,128)(2,1)}, bf16[224,640]{1,0:T(8,128)(2,1)}, u32[]{:S(2)}, u32[]{:S(2)}) collective-permute-start(bf16[224,640]{1,0:T(8,128)(2,1)} %get-tuple-element.136), channel_id=1, source_target_pairs={{0,7},{1,6},{2,5},{3,4},{4,3},{5,2},{6,1},{7,0},{8,15},{9,14},{10,... | collective-permute-start | bytes 860168 | tf_op jit(solution)/shard_map/ppermute | solution.py:88
  276.0 77.2 %all-to-all-start.5 = ((bf16[8,32,1024]{2,1,0:T(8,128)(2,1)}), bf16[8,32,1024]{2,1,0:T(8,128)(2,1)S(1)}, u32[]{:S(2)}, u32[]{:S(2)}) async-start(bf16[8,32,1024]{2,1,0:T(8,128)(2,1)} %rep_sum.3), calls=%async_computation.5 | async-start | bytes 1048576 | tf_op jit(solution)/shard_map/all_to_all | solution.py:92
  318.7 27.5 %collective-permute-start.66 = (bf16[2,224,640]{2,1,0:T(8,128)(2,1)}, bf16[2,224,640]{2,1,0:T(8,128)(2,1)S(1)}, u32[]{:S(2)}, u32[]{:S(2)}) collective-permute-start(bf16[2,224,640]{2,1,0:T(8,128)(2,1)} %core_sums.1.r_2_), channel_id=1, source_target_pairs={{0,16},{8,24},{16,0},{24,8},{1,17},{9,25},{17,1},{25,9},{2,18},{10... | collective-permute-start | bytes 1720328 | tf_op jit(solution)/shard_map/ppermute | solution.py:88
  328.0 30.3 %collective-permute-start.35 = (bf16[128,1024]{1,0:T(8,128)(2,1)}, bf16[128,1024]{1,0:T(8,128)(2,1)S(1)}, u32[]{:S(2)}, u32[]{:S(2)}) collective-permute-start(bf16[128,1024]{1,0:T(8,128)(2,1)} %get-tuple-element.100), channel_id=1, source_target_pairs={{0,8},{8,0},{16,24},{24,16},{1,9},{9,1},{17,25},{25,17},{2,10},{10... | collective-permute-start | bytes 786440 | tf_op jit(solution)/shard_map/ppermute | solution.py:88
  360.3 33.8 %collective-permute-start.43 = (bf16[128,1024]{1,0:T(8,128)(2,1)}, bf16[128,1024]{1,0:T(8,128)(2,1)S(1)}, u32[]{:S(2)}, u32[]{:S(2)}) collective-permute-start(bf16[128,1024]{1,0:T(8,128)(2,1)} %get-tuple-element.116), channel_id=1, source_target_pairs={{0,2},{1,3},{2,0},{3,1},{4,6},{5,7},{6,4},{7,5},{8,10},{9,11},{10,... | collective-permute-start | bytes 786440 | tf_op jit(solution)/shard_map/ppermute | solution.py:88
  362.0 32.2 %collective-permute-start.44 = (bf16[128,1024]{1,0:T(8,128)(2,1)}, bf16[128,1024]{1,0:T(8,128)(2,1)S(1)}, u32[]{:S(2)}, u32[]{:S(2)}) collective-permute-start(bf16[128,1024]{1,0:T(8,128)(2,1)} %get-tuple-element.117), channel_id=1, source_target_pairs={{0,4},{1,5},{2,6},{3,7},{4,0},{5,1},{6,2},{7,3},{8,12},{9,13},{10,... | collective-permute-start | bytes 786440 | tf_op jit(solution)/shard_map/ppermute | solution.py:88
  364.3 29.8 %collective-permute-start.45 = (bf16[128,1024]{1,0:T(8,128)(2,1)}, bf16[128,1024]{1,0:T(8,128)(2,1)S(1)}, u32[]{:S(2)}, u32[]{:S(2)}) collective-permute-start(bf16[128,1024]{1,0:T(8,128)(2,1)} %get-tuple-element.118), channel_id=1, source_target_pairs={{0,6},{1,7},{2,4},{3,5},{4,2},{5,3},{6,0},{7,1},{8,14},{9,15},{10,... | collective-permute-start | bytes 786440 | tf_op jit(solution)/shard_map/ppermute | solution.py:88
  (116 other events, 1702.2 us)
where the time goes:
time: 406 us; the launch traced here: 400 us
  waiting for transfers between devices  152 us (37%)
  Pallas kernels  114 us (28%)
  starting transfers between devices  96.3 us (24%)
  local copies, waits for them, and re-layouts  31.4 us (8%)
  other arithmetic  4.99 us (1%)
    ppermute x68, waiting for transfers between devices, swap(): return lax.ppermute(block, axis, [(i, i ^ k) for i in range(count)])  152 us
    pallas_call x31, Pallas kernels, call(): pl.pallas_call(kernel, out_shape=[jax.ShapeDtypeStruct(shape, dtype) for...  114 us
    ppermute x68, starting transfers between devices, swap(): return lax.ppermute(block, axis, [(i, i ^ k) for i in range(count)])  65.4 us
    all_to_all x6, starting transfers between devices, exchange(): lax.all_to_all(block, 'shard', split_axis=0, concat_axis=0, tiled=True)  30.9 us
    unnamed x140, local copies, waits for them, and re-layouts  23.4 us
  transfers between devices with their start and end apart: 74, of which 22 were waited for; matrix products, arithmetic and copies ran while one was open for 6% of the time, Pallas kernels for 24%

commit v1 on v0

--- a/solution.py
+++ b/solution.py
@@ -96,12 +96,25 @@
     return [block] + [swap(block, axis, k) for k in range(step, lax.axis_size(axis), step)]
 
 
-def with_cores(parts):
-    return parts + [swap(part, "shard", 1) for part in parts]
-
-
 def deliver(blocks, axis, step):
     return [blocks[0]] + [swap(block, axis, i * step) for i, block in enumerate(blocks) if i]
+
+
+def exchange_z(blocks):
+    groups = [list(range(core, lax.axis_size("shard"), 2)) for core in range(2)]
+    return lax.all_to_all(
+        blocks, "shard", split_axis=0, concat_axis=0, axis_index_groups=groups, tiled=True
+    )
+
+
+def deliver_pairs(pairs):
+    parts = deliver(pairs, "shard", 2)
+    return [part[0] for part in parts], swap(jnp.stack([part[1] for part in parts]), "shard", 1)
+
+
+def both_cores(parts):
+    stacked = jnp.stack(parts)
+    return stacked, swap(stacked, "shard", 1)
 
 
 def call(kernel, name, outs, *operands, scalars=(), scratch=()):
@@ -145,13 +158,15 @@
 
 
 def blocks_kernel(n, in_ref, out_ref):
-    values = in_ref[...].astype(F32)
-    out_ref[...] = to_blocks(values, n, out_ref.shape[1]).astype(BF16)
-
-
-def attention_message_kernel(n, rep_ref, q_ref, k_ref, v_ref, out_ref, gain_ref, qkv_msg_ref, out_msg_ref):
+    values = to_blocks(in_ref[...].astype(F32), n, out_ref.shape[2]).astype(BF16)
+    for i in range(out_ref.shape[0]):
+        out_ref[i] = values
+
+
+def attention_message_kernel(n, rep_ref, me_ref, q_ref, k_ref, v_ref, out_ref, gain_ref, *refs):
+    msg_refs, (out_msg_ref, hold_ref) = refs[: n // 2], refs[n // 2 :]
     own = q_ref.shape[0]
-    piece, cols = qkv_msg_ref.shape[1:]
+    piece, cols = hold_ref.shape[1:]
     head_cols = cols // 3
     heads = head_cols // HD
     row = lax.broadcasted_iota(jnp.int32, (piece, own), 0) + rep_ref[0] * piece
@@ -169,25 +184,79 @@
         block = jnp.concatenate(parts, axis=1)
         for i in range(2):
             block = jnp.where(wide == own + i, gain_ref[i : i + 1, :], block)
-        qkv_msg_ref[s] = block.astype(BF16)
-    rows = to_blocks(dot(pick, out_ref[...]), n, out_msg_ref.shape[2]).astype(BF16)
-    for s in range(n):
-        out_msg_ref[s] = rows
-
-
-def join_kernel(reps, rep_ref, *refs):
+        hold_ref[s] = block.astype(BF16)
+    for i in range(n):
+        msg_refs[i // 2][i % 2] = hold_ref[me_ref[0] ^ i]
+    out_msg_ref[...] = to_blocks(dot(pick, out_ref[...]), n, out_msg_ref.shape[1]).astype(BF16)
+
+
+def join_kernel(n, reps, rep_ref, me_ref, *refs):
     for i in range(reps):
-        refs[reps][:, rep_ref[0] ^ i] = refs[i][...]
-
-
-def hidden_message_kernel(n, reps, block, rep_ref, core_ref, gate_ref, up_ref, down_ref, *msg_refs):
+        for s in range(n):
+            refs[reps][me_ref[0] ^ s, rep_ref[0] ^ i] = refs[i][s]
+
+
+def join_out_kernel(nz, reps, rep_ref, me_ref, mine_ref, other_ref, out_ref):
+    for core, ref in enumerate((mine_ref, other_ref)):
+        for i in range(reps):
+            for z in range(nz):
+                out_ref[me_ref[0] ^ (2 * z + core), rep_ref[0] ^ i] = ref[i, z]
+
+
+def fill_rows(values, rows):
+    if values.shape[0] == rows:
+        return values
+    return jnp.concatenate([values, jnp.zeros((rows - values.shape[0], values.shape[1]), F32)], axis=0)
+
+
+def fill_cols(values, cols):
+    if values.shape[1] == cols:
+        return values
+    return jnp.concatenate([values, jnp.zeros((values.shape[0], cols - values.shape[1]), F32)], axis=1)
+
+
+def message_plan(own, each, cols):
+    top, rows = round_up(own, 8), round_up(each, 8)
+    rest = D % cols
+    halved = rest and 2 * rest <= cols
+    first = round_up(rows // 2, 8) if halved else rows
+    total = top + D // cols * rows + (first if rest else 0)
+    return top, rows, rest, halved, first, total
+
+
+def pack_message(both, down, cols):
+    top, rows, rest, halved, first, _ = message_plan(both.shape[0], down.shape[0], cols)
+    down = fill_rows(down, rows)
+    parts = [fill_rows(both, top)]
+    parts += [down[:, j * cols : (j + 1) * cols] for j in range(D // cols)]
+    if rest:
+        tail = down[:, D - rest :]
+        if halved:
+            tail = jnp.concatenate([tail[:first], fill_rows(tail[first:], first)], axis=1)
+        parts.append(fill_cols(tail, cols))
+    return jnp.concatenate(parts, axis=0)
+
+
+def unpack_message(message, own, each):
+    cols = message.shape[1]
+    top, rows, rest, halved, first, _ = message_plan(own, each, cols)
+    parts = [message[top + j * rows : top + (j + 1) * rows] for j in range(D // cols)]
+    if rest:
+        tail = message[top + D // cols * rows :][:first]
+        if halved:
+            tail = jnp.concatenate([tail[:, :rest], tail[: rows - first, rest : 2 * rest]], axis=0)
+        parts.append(tail[:, :rest])
+    return message[:own], jnp.concatenate(parts, axis=1)[:each]
+
+
+def hidden_message_kernel(n, reps, rep_ref, core_ref, gate_ref, up_ref, down_ref, out_ref):
     own, units = gate_ref.shape
     held = down_ref.shape[0]
     each = held // (2 * reps)
     cols = n * each
-    padded = round_up(each, 16)
     place = lax.broadcasted_iota(jnp.int32, (1, cols), 1)
-    for i, msg_ref in enumerate(msg_refs):
+    row = lax.broadcasted_iota(jnp.int32, (round_up(each, 8), held), 0)
+    for i in range(2):
         begin = each * (2 * rep_ref[0] + (core_ref[0] ^ i))
         unit = place + begin
         for s in range(1, n):
@@ -195,44 +264,30 @@
         pick = jnp.where(lax.broadcasted_iota(jnp.int32, (units, cols), 0) == unit, 1.0, 0.0)
         pick = pick.astype(BF16)
         both = jnp.concatenate([dot(gate_ref[...], pick), dot(up_ref[...], pick)], axis=1)
-        both = jnp.concatenate([both, jnp.zeros((block - own, 2 * cols), F32)], axis=0)
-        msg_ref[pl.ds(0, block), :] = both.astype(BF16)
-        row = lax.broadcasted_iota(jnp.int32, (padded, held), 0)
-        take = (lax.broadcasted_iota(jnp.int32, (padded, held), 1) == row + begin) & (row < each)
-        down = to_blocks(dot(jnp.where(take, 1.0, 0.0).astype(BF16), down_ref[...]), n, n * block)
-        for j, part in enumerate(chunks(down, 2 * cols)):
-            msg_ref[pl.ds(block + j * padded, padded), :] = part.astype(BF16)
-
-
-def chunks(values, cols):
-    rows, width = values.shape
-    parts = []
-    for begin in range(0, width, cols):
-        part = values[:, begin : begin + cols]
-        if part.shape[1] < cols:
-            part = jnp.concatenate([part, jnp.zeros((rows, cols - part.shape[1]), F32)], axis=1)
-        parts.append(part)
-    return parts
-
-
-def hidden_weights_in_kernel(n, each, me_ref, *refs):
-    parts, (w_ref, down_ref, rows_ref) = refs[:n], refs[n:]
-    block, cols = w_ref.shape[1:]
-    width = down_ref.shape[1]
-    padded = rows_ref.shape[1]
-    for i, part in enumerate(parts):
-        s = me_ref[0] ^ i
-        w_ref[s] = part[pl.ds(0, block), :]
-        for j, begin in enumerate(range(0, width, cols)):
-            size = min(cols, width - begin)
-            rows = part[pl.ds(block + j * padded, padded), :].astype(F32)
-            rows_ref[s, :, begin : begin + size] = rows[:, :size]
-    down_ref[...] = jnp.concatenate([rows_ref[s][:each] for s in range(n)], axis=0).astype(BF16)
-
-
-def attend_kernel(rows, n, me_ref, *refs):
-    tokens, refs = refs[:n], refs[n:]
-    w_ref, cos_ref, sin_ref, start_ref, first_ref, q_ref, k_ref, v_ref, mixed_ref, gains_ref = refs
+        take = (lax.broadcasted_iota(jnp.int32, row.shape, 1) == row + begin) & (row < each)
+        down = dot(jnp.where(take, 1.0, 0.0).astype(BF16), down_ref[...])
+        message = pack_message(both, down[:each], 2 * cols).astype(BF16)
+        for z in range(out_ref.shape[0]):
+            out_ref[z, i] = message
+
+
+def hidden_weights_in_kernel(n, own, each, core_ref, mine_ref, other_ref, w_ref, down_ref, rows_ref):
+    block = w_ref.shape[1]
+    for side in range(2):
+        for z in range(n // 2):
+            s = 2 * z + (core_ref[0] ^ side)
+            message = other_ref[z] if side else mine_ref[z, 0]
+            both, down = unpack_message(message.astype(F32), own, each)
+            w_ref[s] = fill_rows(both, block).astype(BF16)
+            rows_ref[s, :each, :] = down
+    down = jnp.concatenate([rows_ref[s, :each, :] for s in range(n)], axis=0)
+    down_ref[...] = to_blocks(down, n, down_ref.shape[1]).astype(BF16)
+
+
+def attend_kernel(rows, n, me_ref, mine_ref, other_ref, *refs):
+    w_ref, cos_ref, sin_ref, start_ref, first_ref, q_ref, k_ref, v_ref, gains_ref = refs[:9]
+    pair_refs, mixed_ref = refs[9:-1], refs[-1]
+    core = me_ref[0] % 2
     length, head_cols = q_ref.shape
     heads = head_cols // HD
     width = first_ref.shape[1]
@@ -249,10 +304,11 @@
             parts += [spread_row, gap]
         gains.append(jnp.concatenate(parts, axis=1))
         gains_ref[i : i + 1, :] = gains[i]
-    for i, ref in enumerate(tokens):
-        inputs = ref[...].astype(F32)
-        normed = inputs * inverse_rms(inputs) * gains[0]
-        first_ref[rows_at(me_ref[0] ^ i, rows), :] = normed.astype(BF16)
+    for side, ref in enumerate((mine_ref, other_ref)):
+        for z in range(n // 2):
+            inputs = ref[z].astype(F32)
+            normed = inputs * inverse_rms(inputs) * gains[0]
+            first_ref[rows_at(2 * z + (core ^ side), rows), :] = normed.astype(BF16)
     block = min(256, length)
     for i in range(length // block):
         span = pl.ds(i * block, block)
@@ -272,11 +328,18 @@
             mixed = head_of(dot(probs.astype(BF16), v_ref[past, :]), h, heads)
             total = mixed if total is None else total + mixed
         mixed_ref[span, :] = total.astype(BF16)
-
-
-def attend_back_kernel(
-    first_ref, q_ref, k_ref, v_ref, g_ref, cos_ref, sin_ref, start_ref, dqkv_ref, piece_ref, dk_ref, dv_ref
-):
+    for i in range(n):
+        pair_refs[i // 2][i % 2] = mixed_ref[rows_at(me_ref[0] ^ i, rows), :]
+
+
+def attend_back_kernel(nz, reps, rep_ref, me_ref, *refs):
+    mines, refs = refs[:nz], refs[nz:]
+    other_ref, first_ref, q_ref, k_ref, v_ref, cos_ref, sin_ref, start_ref, dqkv_ref = refs[:9]
+    piece_refs, (g_ref, dk_ref, dv_ref, hold_ref) = refs[9 : 9 + reps], refs[9 + reps :]
+    rows = other_ref.shape[1]
+    for z in range(nz):
+        g_ref[rows_at(me_ref[0] ^ (2 * z), rows), :] = mines[z][...]
+        g_ref[rows_at(me_ref[0] ^ (2 * z + 1), rows), :] = other_ref[z]
     length, head_cols = q_ref.shape
     heads = head_cols // HD
     block = min(256, length)
@@ -306,15 +369,18 @@
         back = total * cos_ref[span, :] - turned(total) * sin_ref[span, :]
         dqkv_ref[span, head_cols : 2 * head_cols] = back.astype(BF16)
         dqkv_ref[span, 2 * head_cols :] = dv_ref[span, :].astype(BF16)
-    store_pieces(piece_ref, contract_rows(first_ref[...], dqkv_ref[...]))
-
-
-def store_pieces(piece_ref, grad):
-    reps, n, piece, cols = piece_ref.shape
+    store_pieces(rep_ref, piece_refs, hold_ref, contract_rows(first_ref[...], dqkv_ref[...]))
+
+
+def store_pieces(rep_ref, piece_refs, hold_ref, grad):
+    n, reps, piece, _ = hold_ref.shape
     for s in range(n):
         for r in range(reps):
             begin = (s * reps + r) * piece
-            piece_ref[r, s] = grad[begin : begin + piece].astype(BF16)
+            hold_ref[s, r] = grad[begin : begin + piece].astype(BF16)
+    for i, ref in enumerate(piece_refs):
+        for s in range(n):
+            ref[s] = hold_ref[s, rep_ref[0] ^ i]
 
 
 def first_grad_kernel(rows, side, me_ref, dqkv_ref, w_ref, out_ref):
@@ -328,30 +394,34 @@
         ref[...] = (mine_ref[i].astype(F32) + other_ref[i].astype(F32)).astype(BF16)
 
 
-def middle_kernel(n, tokens_ref, mixed_ref, w_ref, gains_ref, middle_ref, second_ref, attended_ref):
-    width = tokens_ref.shape[1]
-    attended = jnp.concatenate([mixed_ref[s] for s in range(n)], axis=1)[:, :D]
+def middle_kernel(n, me_ref, tokens_ref, *refs):
+    mines, refs = refs[: n // 2], refs[n // 2 :]
+    other_ref, w_ref, gains_ref, middle_ref, second_ref, attended_ref, hold_ref = refs
+    width = tokens_ref.shape[2]
+    for z in range(n // 2):
+        hold_ref[me_ref[0] ^ (2 * z)] = mines[z][...]
+        hold_ref[me_ref[0] ^ (2 * z + 1)] = other_ref[z]
+    attended = jnp.concatenate([hold_ref[s] for s in range(n)], axis=1)[:, :D]
     attended = to_blocks(attended.astype(F32), n, width).astype(BF16)
     attended_ref[...] = attended
-    middle = tokens_ref[...].astype(F32) + dot(attended, w_ref[...])
+    middle = tokens_ref[0].astype(F32) + dot(attended, w_ref[...])
     middle_ref[...] = middle
     second_ref[...] = (middle * inverse_rms(middle) * gains_ref[1:2, :]).astype(BF16)
 
 
-def stacked(refs):
-    return jnp.concatenate([ref[...] for ref in refs], axis=0)
-
-
-def hidden_kernel(reps, *refs):
-    seconds, cots = refs[:reps], refs[reps : 2 * reps]
-    w_ref, down_ref, grad_ref, grads_ref, hidden_ref = refs[2 * reps :]
-    rows = seconds[0].shape[0]
+def stacked(ref, begin=0, count=None):
+    count = ref.shape[0] if count is None else count
+    return jnp.concatenate([ref[begin + i] for i in range(count)], axis=0)
+
+
+def hidden_kernel(second_ref, cot_ref, w_ref, down_ref, grad_ref, grads_ref, hidden_ref):
+    reps, rows, _ = second_ref.shape
     units = down_ref.shape[0]
     for i in range(0, reps, 2):
         span = pl.ds(i * rows, 2 * rows)
-        both = dot(stacked(seconds[i : i + 2]), w_ref[...])
+        both = dot(stacked(second_ref, i, 2), w_ref[...])
         gate, up = both[:, :units], both[:, units:]
-        grad_hidden = contract_cols(stacked(cots[i : i + 2]), down_ref[...])
+        grad_hidden = contract_cols(stacked(cot_ref, i, 2), down_ref[...])
         sigmoid = 1.0 / (1.0 + jnp.exp(-gate))
         silu = gate * sigmoid
         hidden_ref[span, :] = (silu * up).astype(BF16)
@@ -363,61 +433,50 @@
             grad_ref[i + j] = grad[j * rows : (j + 1) * rows]
 
 
-def hidden_weights_kernel(reps, n, each, me_ref, *refs):
-    seconds, cots = refs[: 2 * reps], refs[2 * reps : 4 * reps]
-    (grads_a, grads_b, hidden_a, hidden_b), refs = refs[4 * reps : 4 * reps + 4], refs[4 * reps + 4 :]
-    msg_refs, (grad_ref, rows_ref) = refs[:n], refs[n:]
-    block, cols = grad_ref.shape[1:]
-    padded = rows_ref.shape[1]
-    grad = contract_rows(stacked(seconds[:reps]), grads_a[...])
-    grad = grad + contract_rows(stacked(seconds[reps:]), grads_b[...])
-    down = contract_rows(hidden_a[...], stacked(cots[:reps]))
-    down = down + contract_rows(hidden_b[...], stacked(cots[reps:]))
-    gap = jnp.zeros((padded - each, down.shape[1]), F32)
+def hidden_weights_kernel(n, own, each, core_ref, *refs):
+    second_a, second_b, cot_a, cot_b, grads_a, grads_b, hidden_a, hidden_b, msg_ref, hold_ref = refs
+    cols = hold_ref.shape[2]
+    grad = contract_rows(stacked(second_a), grads_a[...])
+    grad = grad + contract_rows(stacked(second_b), grads_b[...])
+    down = contract_rows(hidden_a[...], stacked(cot_a)) + contract_rows(hidden_b[...], stacked(cot_b))
+    down = from_blocks(down, n, own)
+    block = grad.shape[0] // n
     for s in range(n):
-        grad_ref[s] = grad[s * block : (s + 1) * block].astype(BF16)
-        rows_ref[s] = jnp.concatenate([down[s * each : (s + 1) * each], gap], axis=0)
-    for i, msg_ref in enumerate(msg_refs):
-        s = me_ref[0] ^ i
-        msg_ref[pl.ds(0, block), :] = grad_ref[s]
-        for j, part in enumerate(chunks(rows_ref[s], cols)):
-            msg_ref[pl.ds(block + j * padded, padded), :] = part.astype(BF16)
-
-
-def core_sums_kernel(n, *refs):
-    for core in range(2):
-        total = sum(refs[i][...].astype(F32) for i in range(core, n, 2))
-        refs[n][core] = total.astype(BF16)
+        both = grad[s * block : s * block + own]
+        hold_ref[s] = pack_message(both, down[s * each : (s + 1) * each], cols).astype(BF16)
+    for z in range(n // 2):
+        for i in range(2):
+            msg_ref[z, i] = hold_ref[2 * z + (core_ref[0] ^ i)]
+
+
+def core_sums_kernel(in_ref, mine_ref, other_ref):
+    for core, ref in enumerate((mine_ref, other_ref)):
+        ref[...] = sum(in_ref[z, core].astype(F32) for z in range(in_ref.shape[0])).astype(BF16)
 
 
 def hidden_out_kernel(n, reps, each, rep_ref, core_ref, *refs):
     parts, refs = refs[:reps], refs[reps:]
     gate_w_ref, up_w_ref, gain_ref, gate_ref, up_ref, down_ref, norm_ref, hold_ref = refs
     own = gate_ref.shape[0]
+    units = 2 * reps * each
     for i, part in enumerate(parts):
         for core in range(2):
             hold_ref[2 * (rep_ref[0] ^ i) + (core_ref[0] ^ core)] = part[core]
     cols = hold_ref.shape[2]
-    block = round_up(own + 2, 16)
-    padded = round_up(each, 16)
+    boths = []
+    for f in range(2 * reps):
+        both, down = unpack_message(hold_ref[f].astype(F32), own, each)
+        boths.append(both)
+        down_ref[f * each : (f + 1) * each, :] = down
     total = jnp.zeros((own, 1), F32)
     for begin, w_ref, out_ref in ((0, gate_w_ref, gate_ref), (cols // 2, up_w_ref, up_ref)):
-        held = [hold_ref[f, pl.ds(0, block), :].astype(F32)[:own] for f in range(2 * reps)]
         for s in range(n):
             place = begin + s * each
-            rows = jnp.concatenate([part[:, place : place + each] for part in held], axis=1)
-            span = slice(s * 2 * reps * each, (s + 1) * 2 * reps * each)
+            rows = jnp.concatenate([part[:, place : place + each] for part in boths], axis=1)
+            span = slice(s * units, (s + 1) * units)
             out_ref[:, span] = rows
             total = total + jnp.sum(rows * w_ref[:, span].astype(F32), axis=1, keepdims=True)
     norm_ref[...] = total / gain_ref[...]
-    width = n * block
-    for f in range(2 * reps):
-        rows = []
-        for j, start in enumerate(range(0, width, cols)):
-            part = hold_ref[f, pl.ds(block + j * padded, padded), :].astype(F32)[:each]
-            rows.append(part[:, : min(cols, width - start)])
-        rows = from_blocks(jnp.concatenate(rows, axis=1), n, own)
-        down_ref[f * each : (f + 1) * each, :] = rows
 
 
 def down_kernel(hidden_ref, w_ref, out_ref):
@@ -435,28 +494,31 @@
     refs[-1][...] = from_blocks(total, n, own).astype(BF16)
 
 
-def middle_grad_kernel(n, own, reps, *refs):
+def middle_grad_kernel(n, own, reps, me_ref, *refs):
     parts, refs = refs[:reps], refs[reps:]
-    cot_ref, middle_ref, gains_ref, w_ref, grad_ref, branch_ref, heads_ref = refs
-    rows = cot_ref.shape[0]
+    cot_ref, middle_ref, gains_ref, w_ref, grad_ref, branch_ref = refs[:6]
+    pair_refs, hold_ref = refs[6:-1], refs[-1]
+    rows = middle_ref.shape[0]
     middle = middle_ref[...]
     grad_second = sum(ref[...].astype(F32) for ref in parts)
-    grad = cot_ref[...].astype(F32) + norm_backward(
+    grad = cot_ref[0].astype(F32) + norm_backward(
         middle, inverse_rms(middle), gains_ref[1:2, :], grad_second
     )
     grad_ref[...] = grad
     branch = grad.astype(BF16)
     branch_ref[...] = branch
     attended = from_blocks(contract_cols(branch, w_ref[...]), n, own)
-    head_cols = heads_ref.shape[2]
+    head_cols = hold_ref.shape[2]
     if n * head_cols > D:
         attended = jnp.concatenate([attended, jnp.zeros((rows, n * head_cols - D), F32)], axis=1)
     for s in range(n):
-        heads_ref[s] = attended[:, s * head_cols : (s + 1) * head_cols].astype(BF16)
-
-
-def out_weights_kernel(attended_ref, branch_ref, piece_ref):
-    store_pieces(piece_ref, contract_rows(attended_ref[...], branch_ref[...]))
+        hold_ref[s] = attended[:, s * head_cols : (s + 1) * head_cols].astype(BF16)
+    for i in range(n):
+        pair_refs[i // 2][i % 2] = hold_ref[me_ref[0] ^ i]
+
+
+def out_weights_kernel(rep_ref, attended_ref, branch_ref, *refs):
+    store_pieces(rep_ref, refs[:-1], refs[-1], contract_rows(attended_ref[...], branch_ref[...]))
 
 
 def rep_sum_kernel(reps, *refs):
@@ -509,7 +571,7 @@
 
 def input_grad_kernel(n, own, nz, *refs):
     parts, (tokens_ref, gains_ref, grad_ref, out_ref) = refs[:nz], refs[nz:]
-    inputs = tokens_ref[...].astype(F32)
+    inputs = tokens_ref[0].astype(F32)
     grad_first = sum(ref[...].astype(F32) for ref in parts)
     total = grad_ref[...] + norm_backward(inputs, inverse_rms(inputs), gains_ref[0:1, :], grad_first)
     out_ref[...] = from_blocks(total, n, own)
@@ -544,63 +606,80 @@
     qkv_cols = 3 * head_cols
     each = held // (2 * reps)
     units = n * each
-    padded = round_up(each, 16)
-    msg_rows = block + -(-width // (2 * units)) * padded
+    msg_rows = message_plan(own, each, 2 * units)[-1]
     shard_index = lax.axis_index("shard").astype(jnp.int32)
     me = shard_index.reshape(1)
     core = (shard_index % 2).reshape(1)
     rep = lax.axis_index("rep").astype(jnp.int32).reshape(1)
     own_block = (rows, width)
 
-    (tokens_in,) = call(lambda *r: blocks_kernel(n, *r), "tokens_blocks", [(own_block, BF16)], tokens)
-    tokens_all = spread(tokens_in, "shard", 2)
-    tokens_all = [part for pair in zip(tokens_all, [swap(p, "shard", 1) for p in tokens_all]) for part in pair]
+    (tokens_in,) = call(
+        lambda *r: blocks_kernel(n, *r), "tokens_blocks", [((nz,) + own_block, BF16)], tokens
+    )
+    tokens_mine = exchange_z(tokens_in)
+    tokens_other = swap(tokens_mine, "shard", 1)
     gains_own = jnp.pad(jnp.stack([norm_one, norm_two]), ((0, 0), (0, qkv_cols - own))).astype(F32)
-    qkv_message, out_message = call(
+    *qkv_messages, out_message = call(
         lambda *r: attention_message_kernel(n, *r),
         "attention_message",
-        [((n, piece, qkv_cols), BF16), ((n, piece, width), BF16)],
+        [((2, piece, qkv_cols), BF16)] * nz + [((piece, width), BF16)],
         w_query,
         w_key,
         w_value,
         w_out,
         gains_own,
-        scalars=(rep,),
-    )
-
-    def joined(arrived, name):
-        cols = arrived.shape[2]
-        parts = spread(arrived, "rep", 1)
-        (whole,) = call(
-            lambda *r: join_kernel(reps, *r), name, [((n, reps, piece, cols), BF16)], *parts, scalars=(rep,)
-        )
-        return whole.reshape(width, cols)
-
-    w_qkv = joined(exchange(qkv_message), "join_qkv")
-
-    (cot_in,) = call(lambda *r: blocks_kernel(n, *r), "cot_blocks", [(own_block, BF16)], cotangent)
-    cots = with_cores(spread(cot_in, "rep", 1))
-    messages = call(
-        lambda *r: hidden_message_kernel(n, reps, block, *r),
+        scalars=(rep, me),
+        scratch=[((n, piece, qkv_cols), BF16)],
+    )
+    qkv_mine, qkv_other = deliver_pairs(qkv_messages)
+    qkv_piece = jnp.stack([block for z in range(nz) for block in (qkv_mine[z], qkv_other[z])])
+    (w_qkv,) = call(
+        lambda *r: join_kernel(n, reps, *r),
+        "join_qkv",
+        [((n, reps, piece, qkv_cols), BF16)],
+        *spread(qkv_piece, "rep", 1),
+        scalars=(rep, me),
+    )
+    w_qkv = w_qkv.reshape(width, qkv_cols)
+
+    (messages,) = call(
+        lambda *r: hidden_message_kernel(n, reps, *r),
         "hidden_message",
-        [((msg_rows, 2 * units), BF16)] * 2,
+        [((nz, 2, msg_rows, 2 * units), BF16)],
         w_gate,
         w_up,
         w_down,
         scalars=(rep, core),
     )
-    out_message, messages, tokens_all = lax.optimization_barrier((out_message, messages, tokens_all))
-    out_full = joined(exchange(out_message), "join_out")
-    arrived = [messages[0]] + [swap(messages[k % 2], "shard", k) for k in range(1, n)]
+    out_message, messages, tokens_mine = lax.optimization_barrier((out_message, messages, tokens_mine))
+    out_mine, out_other = both_cores(
+        spread(jnp.stack(spread(out_message, "shard", 2)), "rep", 1)
+    )
+    (out_full,) = call(
+        lambda *r: join_out_kernel(nz, reps, *r),
+        "join_out",
+        [((n, reps, piece, width), BF16)],
+        out_mine,
+        out_other,
+        scalars=(rep, me),
+    )
+    out_full = out_full.reshape(width, width)
+    messages = exchange_z(messages)
     w_hidden, w_down_in = call(
-        lambda *r: hidden_weights_in_kernel(n, each, *r),
+        lambda *r: hidden_weights_in_kernel(n, own, each, *r),
         "hidden_weights_in",
         [((n, block, 2 * units), BF16), ((units, width), BF16)],
-        *arrived,
-        scalars=(me,),
-        scratch=[((n, padded, width), F32)],
+        messages,
+        swap(messages[:, 1], "shard", 1),
+        scalars=(core,),
+        scratch=[((n, round_up(each, 8), D), F32)],
     )
     w_hidden = w_hidden.reshape(width, 2 * units)
+    (cot_in,) = call(
+        lambda *r: blocks_kernel(n, *r), "cot_blocks", [((1,) + own_block, BF16)], cotangent
+    )
+    cot_in, w_qkv = lax.optimization_barrier((cot_in, w_qkv))
+    cot_mine, cot_other = both_cores(spread(cot_in[0], "rep", 1))
 
     doc_start, position = doc_layout(lengths[0], length)
     cosines, sines = rope_tables(position)
@@ -608,98 +687,109 @@
     sines = jnp.tile(sines, (1, 2 * heads))
     start = doc_start[:, None]
     head_shape = (length, head_cols)
-    first_all, query, key, value, mixed, gains = call(
+    first_all, query, key, value, gains, *mixed = call(
         lambda *r: attend_kernel(rows, n, *r),
         "attend",
-        [((length, width), BF16)] + [(head_shape, BF16)] * 4 + [((2, width), F32)],
-        *tokens_all,
+        [((length, width), BF16)]
+        + [(head_shape, BF16)] * 3
+        + [((2, width), F32)]
+        + [((2, rows, head_cols), BF16)] * nz,
+        tokens_mine,
+        tokens_other,
         w_qkv,
         cosines,
         sines,
         start,
         scalars=(me,),
-    )
-    mixed = exchange(mixed.reshape(n, rows, head_cols))
+        scratch=[(head_shape, BF16)],
+    )
+    mixed_mine, mixed_other = deliver_pairs(mixed)
 
     middle, second, attended = call(
         lambda *r: middle_kernel(n, *r),
         "middle",
         [(own_block, F32), (own_block, BF16), (own_block, BF16)],
         tokens_in,
-        mixed,
+        *mixed_mine,
+        mixed_other,
         out_full,
         gains,
-    )
-
-    seconds = with_cores(spread(second, "rep", 1))
+        scalars=(me,),
+        scratch=[((n, rows, head_cols), BF16)],
+    )
+
+    second_mine, second_other = both_cores(spread(second, "rep", 1))
     side_outs = [
         ((reps, rows, width), BF16),
         ((reps * rows, 2 * units), BF16),
         ((reps * rows, units), BF16),
     ]
 
-    def hidden_side(side, name):
-        span = slice(side * reps, (side + 1) * reps)
-        return call(
-            lambda *r: hidden_kernel(reps, *r),
-            name,
-            side_outs,
-            *seconds[span],
-            *cots[span],
-            w_hidden,
-            w_down_in,
-        )
+    def hidden_side(seconds, cots, name):
+        return call(hidden_kernel, name, side_outs, seconds, cots, w_hidden, w_down_in)
 
     def plane_sums(mine, other):
         sums = call(pair_sum_kernel, "pair_sum", [(own_block, BF16)] * reps, mine, swap(other, "shard", 1))
         return deliver(sums, "rep", 1)
 
-    grad_other, grads_other, hidden_other = hidden_side(1, "hidden_other")
-    grad_mine, grads_mine, hidden_mine = hidden_side(0, "hidden_mine")
+    grad_mine, grads_mine, hidden_mine = hidden_side(second_mine, cot_mine, "hidden_mine")
+    grad_other, grads_other, hidden_other = hidden_side(second_other, cot_other, "hidden_other")
     grad_second = plane_sums(grad_mine, grad_other)
-    hidden_messages = call(
-        lambda *r: hidden_weights_kernel(reps, n, each, *r),
+    (hidden_messages,) = call(
+        lambda *r: hidden_weights_kernel(n, own, each, *r),
         "hidden_weights",
-        [((msg_rows, 2 * units), BF16)] * n,
-        *seconds,
-        *cots,
+        [((nz, 2, msg_rows, 2 * units), BF16)],
+        second_mine,
+        second_other,
+        cot_mine,
+        cot_other,
         grads_mine,
         grads_other,
         hidden_mine,
         hidden_other,
-        scalars=(me,),
-        scratch=[((n, block, 2 * units), BF16), ((n, padded, width), F32)],
-    )
-    hidden_messages = deliver(hidden_messages, "shard", 1)
-
-    grad_middle, grad_branch, grad_heads = call(
+        scalars=(core,),
+        scratch=[((n, msg_rows, 2 * units), BF16)],
+    )
+    hidden_messages = exchange_z(hidden_messages)
+
+    grad_middle, grad_branch, *grad_heads = call(
         lambda *r: middle_grad_kernel(n, own, reps, *r),
         "middle_grad",
-        [(own_block, F32), (own_block, BF16), ((n, rows, head_cols), BF16)],
+        [(own_block, F32), (own_block, BF16)] + [((2, rows, head_cols), BF16)] * nz,
         *grad_second,
         cot_in,
         middle,
         gains,
         out_full,
-    )
-    grad_heads = exchange(grad_heads).reshape(head_shape)
-    (out_pieces,) = call(
-        out_weights_kernel, "out_weights", [((reps, n, piece, width), BF16)], attended, grad_branch
-    )
-
-    grad_qkv, attention_pieces = call(
-        attend_back_kernel,
+        scalars=(me,),
+        scratch=[((n, rows, head_cols), BF16)],
+    )
+    heads_mine, heads_other = deliver_pairs(grad_heads)
+    out_pieces = call(
+        out_weights_kernel,
+        "out_weights",
+        [((n, piece, width), BF16)] * reps,
+        attended,
+        grad_branch,
+        scalars=(rep,),
+        scratch=[((n, reps, piece, width), BF16)],
+    )
+
+    grad_qkv, *attention_pieces = call(
+        lambda *r: attend_back_kernel(nz, reps, *r),
         "attend_back",
-        [((length, qkv_cols), BF16), ((reps, n, piece, qkv_cols), BF16)],
+        [((length, qkv_cols), BF16)] + [((n, piece, qkv_cols), BF16)] * reps,
+        *heads_mine,
+        heads_other,
         first_all,
         query,
         key,
         value,
-        grad_heads,
         cosines,
         sines,
         start,
-        scratch=[(head_shape, F32)] * 2,
+        scalars=(rep, me),
+        scratch=[(head_shape, BF16)] + [(head_shape, F32)] * 2 + [((n, reps, piece, qkv_cols), BF16)],
     )
     first_sides = [
         call(
@@ -726,10 +816,9 @@
     )
 
     def owner_pieces(pieces):
-        blocks = [lax.dynamic_index_in_dim(pieces, rep[0] ^ k, 0, keepdims=False) for k in range(reps)]
-        parts = deliver(blocks, "rep", 1)
+        parts = deliver(pieces, "rep", 1)
         (summed,) = call(
-            lambda *r: rep_sum_kernel(reps, *r), "rep_sum", [(pieces.shape[1:], BF16)], *parts
+            lambda *r: rep_sum_kernel(reps, *r), "rep_sum", [(pieces[0].shape, BF16)], *parts
         )
         return exchange(summed)
 
@@ -758,9 +847,10 @@
         scratch=[((reps, piece, width), F32)],
     )
 
-    (core_sums,) = call(
-        lambda *r: core_sums_kernel(n, *r), "core_sums", [((2, msg_rows, 2 * units), BF16)], *hidden_messages
-    )
+    sum_mine, sum_other = call(
+        core_sums_kernel, "core_sums", [((msg_rows, 2 * units), BF16)] * 2, hidden_messages
+    )
+    core_sums = jnp.stack([sum_mine, swap(sum_other, "shard", 1)])
     grad_w_gate, grad_w_up, grad_w_down, grad_norm_two = call(
         lambda *r: hidden_out_kernel(n, reps, each, *r),
         "hidden_out",

time: 406 us -> 415 us (1.022)
  starting transfers between devices: 96.3 us -> 84.1 us
  local copies, waits for them, and re-layouts: 31.4 us -> 43.2 us
    all_to_all x6 -> x2, starting transfers between devices: 30.9 us -> 11.7 us  [exchange(): lax.all_to_all(block, 'shard', split_axis=0, concat_axis=0, tiled=True)]
    all_to_all x0 -> x3, starting transfers between devices: none -> 18.4 us  [exchange_z(): lax.all_to_all(blocks, 'shard', split_axis=0, concat_axis=0, axis_index_g...]
    all_to_all x0 -> x3, waiting for transfers between devices: none -> 15.5 us  [exchange_z(): lax.all_to_all(blocks, 'shard', split_axis=0, concat_axis=0, axis_index_g...]
    ppermute x68 -> x60, waiting for transfers between devices: 152 us -> 138 us  [swap(): return lax.ppermute(block, axis, [(i, i ^ k) for i in range(count)])]
    ppermute x68 -> x60, starting transfers between devices: 65.4 us -> 54 us  [swap(): return lax.ppermute(block, axis, [(i, i ^ k) for i in range(count)])]
    slice x0 -> x12, local copies, waits for them, and re-layouts: none -> 7.08 us  [deliver_pairs(): part[1]]
    unnamed x140 -> x112, local copies, waits for them, and re-layouts: 23.4 us -> 28 us
  transfers between devices with their start and end apart: 74 -> 65, of which waited for: 22 -> 28; matrix products, arithmetic and copies ran while one was open for 6% -> 8% of each run, Pallas kernels for 24% -> 20%
where the time goes in v1:
time: 415 us; the launch traced here: 408 us
  waiting for transfers between devices  154 us (37%)
  Pallas kernels  117 us (28%)
  starting transfers between devices  84.1 us (20%)
  local copies, waits for them, and re-layouts  43.2 us (10%)
  other arithmetic  9.07 us (2%)
    ppermute x60, waiting for transfers between devices, swap(): return lax.ppermute(block, axis, [(i, i ^ k) for i in range(count)])  138 us
    pallas_call x31, Pallas kernels, call(): pl.pallas_call(kernel, out_shape=[jax.ShapeDtypeStruct(shape, dtype) for...  117 us
    ppermute x60, starting transfers between devices, swap(): return lax.ppermute(block, axis, [(i, i ^ k) for i in range(count)])  54 us
    unnamed x112, local copies, waits for them, and re-layouts  28 us
    all_to_all x3, starting transfers between devices, exchange_z(): lax.all_to_all(blocks, 'shard', split_axis=0, concat_axis=0, axis_index_g...  18.4 us
    all_to_all x3, waiting for transfers between devices, exchange_z(): lax.all_to_all(blocks, 'shard', split_axis=0, concat_axis=0, axis_index_g...  15.5 us
    all_to_all x2, starting transfers between devices, exchange(): lax.all_to_all(block, 'shard', split_axis=0, concat_axis=0, tiled=True)  11.7 us
  transfers between devices with their start and end apart: 65, of which 28 were waited for; matrix products, arithmetic and copies ran while one was open for 8% of the time, Pallas kernels for 20%

profile of v1, /device:TPU:10, one launch (start us, length us, event | category | flops | bytes accessed | tf_op | source)
XLA Modules:
  0.0 407.9 jit_solution(3312382753280678119)
XLA Ops:
  14.8 6.2 %all-to-all-start = ((bf16[4,128,1024]{2,1,0:T(8,128)(2,1)}), bf16[4,128,1024]{2,1,0:T(8,128)(2,1)S(1)}, u32[]{:S(2)}, u32[]{:S(2)}) async-start(bf16[4,128,1024]{2,1,0:T(8,128)(2,1)} %tokens_blocks.1.r_1_.r_4_), calls=%async_computation | async-start | bytes 2097152 | tf_op jit(solution)/shard_map/all_to_all | solution.py:105
  21.8 5.0 %hidden_message.1 = bf16[4,2,184,640]{3,2,1,0:T(8,128)(2,1)} custom-call(s32[1]{0:T(128)} %bitcast.1.r_0_.rep_ref, s32[1]{0:T(128)} %bitcast.4.r_1_.r_0_, bf16[120,2560]{1,0:T(8,128)(2,1)} %r_6_.2, bf16[120,2560]{1,0:T(8,128)(2,1)} %r_7_.2, bf16[320,960]{1,0:T(8,128)(2,1)} %r_4_.2), custom_call_target="tpu_custom_call" | custom-call | tf_op jit(solution)/shard_map/hidden_message/pallas_call | solution.py:123
  31.3 11.3 %all-to-all-done.r_1_ = bf16[4,128,1024]{2,1,0:T(8,128)(2,1)S(1)} async-done(((bf16[4,128,1024]{2,1,0:T(8,128)(2,1)}), bf16[4,128,1024]{2,1,0:T(8,128)(2,1)S(1)}, u32[]{:S(2)}, u32[]{:S(2)}) %all-to-all-start) | async-done | bytes 1048608 | tf_op jit(solution)/shard_map/all_to_all | solution.py:105
  42.6 7.1 %all-to-all-start.1 = ((bf16[4,2,184,640]{3,2,1,0:T(8,128)(2,1)}), bf16[4,2,184,640]{3,2,1,0:T(8,128)(2,1)S(1)}, u32[]{:S(2)}, u32[]{:S(2)}) async-start(bf16[4,2,184,640]{3,2,1,0:T(8,128)(2,1)} %hidden_message.1), calls=%async_computation.1 | async-start | bytes 3768320 | tf_op jit(solution)/shard_map/all_to_all | solution.py:105
  55.0 27.8 %collective-permute-done.12 = bf16[32,1024]{1,0:T(8,128)(2,1)S(1)} collective-permute-done((bf16[32,1024]{1,0:T(8,128)(2,1)S(1)}, bf16[32,1024]{1,0:T(8,128)(2,1)S(1)}, u32[]{:S(2)}, u32[]{:S(2)}) %collective-permute-start.12) | collective-permute-done | bytes 65568 | tf_op jit(solution)/shard_map/ppermute | solution.py:88
  84.4 9.9 %collective-permute-done.13 = bf16[32,1024]{1,0:T(8,128)(2,1)S(1)} collective-permute-done((bf16[32,1024]{1,0:T(8,128)(2,1)S(1)}, bf16[32,1024]{1,0:T(8,128)(2,1)S(1)}, u32[]{:S(2)}, u32[]{:S(2)}) %collective-permute-start.13) | collective-permute-done | bytes 65568 | tf_op jit(solution)/shard_map/ppermute | solution.py:88
  122.8 9.3 %attend.1 = (bf16[1024,1024]{1,0:T(8,128)(2,1)}, bf16[1024,128]{1,0:T(8,128)(2,1)}, bf16[1024,128]{1,0:T(8,128)(2,1)}, bf16[1024,128]{1,0:T(8,128)(2,1)}, f32[2,...) custom-call(s32[1]{0:T(128)} %bitcast.r_1_.r_0_, ...), custom_call_target="tpu_custom_call" | custom-call | tf_op jit(solution)/shard_map/attend/pallas_call | solution.py:123
  137.3 4.8 %collective-permute-done.9 = bf16[2,128,128]{2,1,0:T(8,128)(2,1)S(1)} collective-permute-done((bf16[2,128,128]{2,1,0:T(8,128)(2,1)}, bf16[2,128,128]{2,1,0:T(8,128)(2,1)S(1)}, u32[]{:S(2)}, u32[]{:S(2)}) %collective-permute-start.9) | collective-permute-done | bytes 65568 | tf_op jit(solution)/shard_map/ppermute | solution.py:88
  159.2 5.6 %collective-permute-done.19 = bf16[128,1024]{1,0:T(8,128)(2,1)S(1)} collective-permute-done((bf16[128,1024]{1,0:T(8,128)(2,1)}, bf16[128,1024]{1,0:T(8,128)(2,1)S(1)}, u32[]{:S(2)}, u32[]{:S(2)}) %collective-permute-start.19) | collective-permute-done | bytes 262176 | tf_op jit(solution)/shard_map/ppermute | solution.py:88
  164.8 5.6 %collective-permute-done.20 = bf16[128,1024]{1,0:T(8,128)(2,1)S(1)} collective-permute-done((bf16[128,1024]{1,0:T(8,128)(2,1)}, bf16[128,1024]{1,0:T(8,128)(2,1)S(1)}, u32[]{:S(2)}, u32[]{:S(2)}) %collective-permute-start.20) | collective-permute-done | bytes 262176 | tf_op jit(solution)/shard_map/ppermute | solution.py:88
  180.0 5.9 %hidden_other.1 = (bf16[4,128,1024]{2,1,0:T(8,128)(2,1)}, bf16[512,640]{1,0:T(8,128)(2,1)}, bf16[512,320]{1,0:T(8,128)(2,1)}) custom-call(bf16[4,128,1024]{2,1,0:T(8,128)(2,1)} %collective-permute-done.26.second_ref.r_2_, bf16[4,128,1024]{2,1,0:T(8,128)(2,1)} %collective-permute-done.27.cot_ref.r_4_, bf16[1024,640]{1,0:T(8,128)(2,1)} %bitcast.64, ...), custom_call_target="tpu_custom_call" | custom-call | tf_op jit(solution)/shard_map/hidden_other/pallas_call | solution.py:123
  186.0 5.7 %hidden_mine.1 = (bf16[4,128,1024]{2,1,0:T(8,128)(2,1)}, bf16[512,640]{1,0:T(8,128)(2,1)}, bf16[512,320]{1,0:T(8,128)(2,1)}) custom-call(bf16[4,128,1024]{2,1,0:T(8,128)(2,1)} %pad_maximum_fusion.1.second_ref.r_1_, bf16[4,128,1024]{2,1,0:T(8,128)(2,1)} %copy-done.1, bf16[1024,640]{1,0:T(8,128)(2,1)} %bitcast.65, ...), custom_call_target="tpu_custom_call" | custom-call | tf_op jit(solution)/shard_map/hidden_mine/pallas_call | solution.py:123
  198.7 5.8 %collective-permute-done.33.r_2_ = bf16[128,1024]{1,0:T(8,128)(2,1)S(1)} collective-permute-done((bf16[128,1024]{1,0:T(8,128)(2,1)}, bf16[128,1024]{1,0:T(8,128)(2,1)S(1)}, u32[]{:S(2)}, u32[]{:S(2)}) %collective-permute-start.33) | collective-permute-done | bytes 262176 | tf_op jit(solution)/shard_map/ppermute | solution.py:88
  204.6 6.2 %collective-permute-done.34.r_3_ = bf16[128,1024]{1,0:T(8,128)(2,1)S(1)} collective-permute-done((bf16[128,1024]{1,0:T(8,128)(2,1)}, bf16[128,1024]{1,0:T(8,128)(2,1)S(1)}, u32[]{:S(2)}, u32[]{:S(2)}) %collective-permute-start.34) | collective-permute-done | bytes 262176 | tf_op jit(solution)/shard_map/ppermute | solution.py:88
  227.2 11.7 %attend_back.1 = (bf16[1024,384]{1,0:T(8,128)(2,1)}, bf16[8,32,384]{2,1,0:T(8,128)(2,1)}, bf16[8,32,384]{2,1,0:T(8,128)(2,1)}, bf16[8,32,384]{2,1,0:T(8,128)(2,1)}, bf16[8,32,384]{2,1,0:T(8,128)(2,1)}) custom-call(s32[1]{0:T(128)} %bitcast.1.r_0_.rep_ref, s32[1]{0:T(128)} %bitcast.r_1_.r_0_, bf16[128,128]{1,0:T(8,128)(2,1)} %get-tuple-element.192.r_2_, ...), custom_call_target="tpu_custom_call" | custom-call | tf_op jit(solution)/shard_map/attend_back/pallas_call | solution.py:123
  253.7 4.8 %all-to-all-start.2 = ((bf16[8,32,384]{2,1,0:T(8,128)(2,1)}), bf16[8,32,384]{2,1,0:T(8,128)(2,1)S(1)}, u32[]{:S(2)}, u32[]{:S(2)}) async-start(bf16[8,32,384]{2,1,0:T(8,128)(2,1)} %rep_sum.2), calls=%async_computation.2 | async-start | bytes 393216 | tf_op jit(solution)/shard_map/all_to_all | solution.py:92
  258.6 6.8 %hidden_weights.1 = bf16[4,2,184,640]{3,2,1,0:T(8,128)(2,1)} custom-call(s32[1]{0:T(128)} %bitcast.4.r_1_.r_0_, bf16[4,128,1024]{2,1,0:T(8,128)(2,1)} %pad_maximum_fusion.1.second_ref.r_1_, bf16[4,128,1024]{2,1,0:T(8,128)(2,1)} %collective-permute-done.26.second_ref.r_2_, bf16[4,128,1024]{2,1,0:T(8,128)(2,1)} %copy-done.1, ...), custom_call_target="tpu_custom_call" | custom-call | tf_op jit(solution)/shard_map/hidden_weights/pallas_call | solution.py:123
  266.0 5.1 %all-to-all-start.4 = ((bf16[4,2,184,640]{3,2,1,0:T(8,128)(2,1)}), bf16[4,2,184,640]{3,2,1,0:T(8,128)(2,1)S(1)}, u32[]{:S(2)}, u32[]{:S(2)}) async-start(bf16[4,2,184,640]{3,2,1,0:T(8,128)(2,1)} %hidden_weights.1), calls=%async_computation.4 | async-start | bytes 3768320 | tf_op jit(solution)/shard_map/all_to_all | solution.py:105
  284.1 8.0 %collective-permute-done.50.r_1_ = bf16[8,32,1024]{2,1,0:T(8,128)(2,1)S(1)} collective-permute-done((bf16[8,32,1024]{2,1,0:T(8,128)(2,1)}, bf16[8,32,1024]{2,1,0:T(8,128)(2,1)S(1)}, u32[]{:S(2)}, u32[]{:S(2)}) %collective-permute-start.50) | collective-permute-done | bytes 524320 | tf_op jit(solution)/shard_map/ppermute | solution.py:88
  292.1 12.0 %collective-permute-done.51.r_2_ = bf16[8,32,1024]{2,1,0:T(8,128)(2,1)S(1)} collective-permute-done((bf16[8,32,1024]{2,1,0:T(8,128)(2,1)}, bf16[8,32,1024]{2,1,0:T(8,128)(2,1)S(1)}, u32[]{:S(2)}, u32[]{:S(2)}) %collective-permute-start.51) | collective-permute-done | bytes 524320 | tf_op jit(solution)/shard_map/ppermute | solution.py:88
  311.8 6.9 %all-to-all-start.3 = ((bf16[8,32,1024]{2,1,0:T(8,128)(2,1)}), bf16[8,32,1024]{2,1,0:T(8,128)(2,1)S(1)}, u32[]{:S(2)}, u32[]{:S(2)}) async-start(bf16[8,32,1024]{2,1,0:T(8,128)(2,1)} %rep_sum.3), calls=%async_computation.3 | async-start | bytes 1048576 | tf_op jit(solution)/shard_map/all_to_all | solution.py:92
  345.6 6.0 %collective-permute-done.48.r_3_ = bf16[8,32,384]{2,1,0:T(8,128)(2,1)S(1)} collective-permute-done((bf16[8,32,384]{2,1,0:T(8,128)(2,1)S(1)}, bf16[8,32,384]{2,1,0:T(8,128)(2,1)S(1)}, u32[]{:S(2)}, u32[]{:S(2)}) %collective-permute-start.48) | collective-permute-done | bytes 196640 | tf_op jit(solution)/shard_map/ppermute | solution.py:88
  365.3 9.0 %collective-permute-done.53.r_2_ = bf16[32,1024]{1,0:T(8,128)(2,1)S(1)} collective-permute-done((bf16[32,1024]{1,0:T(8,128)(2,1)}, bf16[32,1024]{1,0:T(8,128)(2,1)S(1)}, u32[]{:S(2)}, u32[]{:S(2)}) %collective-permute-start.53) | collective-permute-done | bytes 65568 | tf_op jit(solution)/shard_map/ppermute | solution.py:88
  399.1 7.1 %hidden_out.1 = (f32[120,2560]{1,0:T(8,128)}, f32[120,2560]{1,0:T(8,128)}, f32[320,960]{1,0:T(8,128)}, f32[120,1]{1,0:T(8,128)}) custom-call(s32[1]{0:T(128)} %bitcast.1.r_0_.rep_ref, s32[1]{0:T(128)} %bitcast.4.r_1_.r_0_, bf16[2,184,640]{2,1,0:T(8,128)(2,1)} %copy-done.7, bf16[2,184,640]{2,1,0:T(8,128)(2,1)} %copy-done.18, bf16[2,184,640]{2,1,0:T(8,128)(2,1)} %copy-done.19, ...), custom_call_target="tpu_custom_call" | custom-call | tf_op jit(solution)/shard_map/hidden_out/pallas_call | solution.py:123
  (288 shorter events, 213.0 us)
Async XLA Ops:
  14.8 27.8 %all-to-all-start = ((bf16[4,128,1024]{2,1,0:T(8,128)(2,1)}), bf16[4,128,1024]{2,1,0:T(8,128)(2,1)S(1)}, u32[]{:S(2)}, u32[]{:S(2)}) async-start(bf16[4,128,1024]{2,1,0:T(8,128)(2,1)} %tokens_blocks.1.r_1_.r_4_), calls=%async_computation | async-start | bytes 2097152 | tf_op jit(solution)/shard_map/all_to_all | solution.py:105
  42.6 128.8 %all-to-all-start.1 = ((bf16[4,2,184,640]{3,2,1,0:T(8,128)(2,1)}), bf16[4,2,184,640]{3,2,1,0:T(8,128)(2,1)S(1)}, u32[]{:S(2)}, u32[]{:S(2)}) async-start(bf16[4,2,184,640]{3,2,1,0:T(8,128)(2,1)} %hidden_message.1), calls=%async_computation.1 | async-start | bytes 3768320 | tf_op jit(solution)/shard_map/all_to_all | solution.py:105
  50.4 72.5 %collective-permute-start = (bf16[4,128,1024]{2,1,0:T(8,128)(2,1)S(1)}, bf16[4,128,1024]{2,1,0:T(8,128)(2,1)}, u32[]{:S(2)}, u32[]{:S(2)}) collective-permute-start(bf16[4,128,1024]{2,1,0:T(8,128)(2,1)S(1)} %all-to-all-done.r_1_), channel_id=1, source_target_pairs={{0,1},{1,0},{2,3},{3,2},{4,5},{5,4},{6,7},{7,6},{8,9},{9,8},{10,11... | collective-permute-start | bytes 3145736 | tf_op jit(solution)/shard_map/ppermute | solution.py:88
  51.0 48.8 %collective-permute-start.5 = (bf16[8,32,384]{2,1,0:T(8,128)(2,1)}, bf16[8,32,384]{2,1,0:T(8,128)(2,1)}, u32[]{:S(2)}, u32[]{:S(2)}) collective-permute-start(bf16[8,32,384]{2,1,0:T(8,128)(2,1)} %slice_dynamic-update-slice_fusion.r_2_), channel_id=1, source_target_pairs={{0,8},{8,0},{16,24},{24,16},{1,9},{9,1},{17,25},{25,17},{2,10},{10... | collective-permute-start | bytes 589832 | tf_op jit(solution)/shard_map/ppermute | solution.py:88
  51.5 31.3 %collective-permute-start.12 = (bf16[32,1024]{1,0:T(8,128)(2,1)S(1)}, bf16[32,1024]{1,0:T(8,128)(2,1)S(1)}, u32[]{:S(2)}, u32[]{:S(2)}) collective-permute-start(bf16[32,1024]{1,0:T(8,128)(2,1)S(1)} %copy-done.41), channel_id=1, source_target_pairs={{0,2},{1,3},{2,0},{3,1},{4,6},{5,7},{6,4},{7,5},{8,10},{9,11},{10,... | collective-permute-start | bytes 196616 | tf_op jit(solution)/shard_map/ppermute | solution.py:88
  51.6 42.7 %collective-permute-start.13 = (bf16[32,1024]{1,0:T(8,128)(2,1)S(1)}, bf16[32,1024]{1,0:T(8,128)(2,1)S(1)}, u32[]{:S(2)}, u32[]{:S(2)}) collective-permute-start(bf16[32,1024]{1,0:T(8,128)(2,1)S(1)} %copy-done.41), channel_id=1, source_target_pairs={{0,4},{1,5},{2,6},{3,7},{4,0},{5,1},{6,2},{7,3},{8,12},{9,13},{10,... | collective-permute-start | bytes 196616 | tf_op jit(solution)/shard_map/ppermute | solution.py:88
  54.4 42.4 %collective-permute-start.14 = (bf16[32,1024]{1,0:T(8,128)(2,1)S(1)}, bf16[32,1024]{1,0:T(8,128)(2,1)S(1)}, u32[]{:S(2)}, u32[]{:S(2)}) collective-permute-start(bf16[32,1024]{1,0:T(8,128)(2,1)S(1)} %copy-done.41), channel_id=1, source_target_pairs={{0,6},{1,7},{2,4},{3,5},{4,2},{5,3},{6,0},{7,1},{8,14},{9,15},{10,... | collective-permute-start | bytes 196616 | tf_op jit(solution)/shard_map/ppermute | solution.py:88
  82.9 21.1 %collective-permute-start.6 = (bf16[8,32,384]{2,1,0:T(8,128)(2,1)}, bf16[8,32,384]{2,1,0:T(8,128)(2,1)S(1)}, u32[]{:S(2)}, u32[]{:S(2)}) collective-permute-start(bf16[8,32,384]{2,1,0:T(8,128)(2,1)} %slice_dynamic-update-slice_fusion.r_2_), channel_id=1, source_target_pairs={{0,16},{8,24},{16,0},{24,8},{1,17},{9,25},{17,1},{25,9},{2,18},{10... | collective-permute-start | bytes 589832 | tf_op jit(solution)/shard_map/ppermute | solution.py:88
  97.7 20.9 %collective-permute-start.15 = (bf16[4,32,1024]{2,1,0:T(8,128)(2,1)}, bf16[4,32,1024]{2,1,0:T(8,128)(2,1)}, u32[]{:S(2)}, u32[]{:S(2)}) collective-permute-start(bf16[4,32,1024]{2,1,0:T(8,128)(2,1)} %get-tuple-element.190), channel_id=1, source_target_pairs={{0,8},{8,0},{16,24},{24,16},{1,9},{9,1},{17,25},{25,17},{2,10},{10... | collective-permute-start | bytes 786440 | tf_op jit(solution)/shard_map/ppermute | solution.py:88
  99.8 21.7 %collective-permute-start.17 = (bf16[4,32,1024]{2,1,0:T(8,128)(2,1)}, bf16[4,32,1024]{2,1,0:T(8,128)(2,1)}, u32[]{:S(2)}, u32[]{:S(2)}) collective-permute-start(bf16[4,32,1024]{2,1,0:T(8,128)(2,1)} %get-tuple-element.190), channel_id=1, source_target_pairs={{0,24},{8,16},{16,8},{24,0},{1,25},{9,17},{17,9},{25,1},{2,26},{10... | collective-permute-start | bytes 786440 | tf_op jit(solution)/shard_map/ppermute | solution.py:88
  118.0 38.6 %collective-permute-start.22 = (bf16[128,1024]{1,0:T(8,128)(2,1)S(1)}, bf16[128,1024]{1,0:T(8,128)(2,1)S(1)}, u32[]{:S(2)}, u32[]{:S(2)}) collective-permute-start(bf16[128,1024]{1,0:T(8,128)(2,1)S(1)} %bitcast.66), channel_id=1, source_target_pairs={{0,8},{8,0},{16,24},{24,16},{1,9},{9,1},{17,25},{25,17},{2,10},{10... | collective-permute-start | bytes 786440 | tf_op jit(solution)/shard_map/ppermute | solution.py:88
  118.6 40.3 %collective-permute-start.23 = (bf16[128,1024]{1,0:T(8,128)(2,1)S(1)}, bf16[128,1024]{1,0:T(8,128)(2,1)S(1)}, u32[]{:S(2)}, u32[]{:S(2)}) collective-permute-start(bf16[128,1024]{1,0:T(8,128)(2,1)S(1)} %bitcast.67), channel_id=1, source_target_pairs={{0,16},{8,24},{16,0},{24,8},{1,17},{9,25},{17,1},{25,9},{2,18},{10... | collective-permute-start | bytes 786440 | tf_op jit(solution)/shard_map/ppermute | solution.py:88
  119.2 39.8 %collective-permute-start.24 = (bf16[128,1024]{1,0:T(8,128)(2,1)S(1)}, bf16[128,1024]{1,0:T(8,128)(2,1)S(1)}, u32[]{:S(2)}, u32[]{:S(2)}) collective-permute-start(bf16[128,1024]{1,0:T(8,128)(2,1)S(1)} %bitcast.68), channel_id=1, source_target_pairs={{0,24},{8,16},{16,8},{24,0},{1,25},{9,17},{17,9},{25,1},{2,26},{10... | collective-permute-start | bytes 786440 | tf_op jit(solution)/shard_map/ppermute | solution.py:88
  122.8 24.5 %collective-permute-start.18 = (bf16[4,4,32,1024]{3,2,1,0:T(8,128)(2,1)S(1)}, bf16[4,4,32,1024]{3,2,1,0:T(8,128)(2,1)S(1)}, u32[]{:S(2)}, u32[]{:S(2)}) collective-permute-start(bf16[4,4,32,1024]{3,2,1,0:T(8,128)(2,1)S(1)} %pad_maximum_fusion.r_2_), channel_id=1, source_target_pairs={{0,1},{1,0},{2,3},{3,2},{4,5},{5,4},{6,7},{7,6},{8,9},{9,8},{10,11... | collective-permute-start | bytes 3145736 | tf_op jit(solution)/shard_map/ppermute | solution.py:88
  266.0 45.8 %all-to-all-start.4 = ((bf16[4,2,184,640]{3,2,1,0:T(8,128)(2,1)}), bf16[4,2,184,640]{3,2,1,0:T(8,128)(2,1)S(1)}, u32[]{:S(2)}, u32[]{:S(2)}) async-start(bf16[4,2,184,640]{3,2,1,0:T(8,128)(2,1)} %hidden_weights.1), calls=%async_computation.4 | async-start | bytes 3768320 | tf_op jit(solution)/shard_map/all_to_all | solution.py:105
  274.0 47.6 %collective-permute-start.28 = (bf16[4,128,1024]{2,1,0:T(8,128)(2,1)}, bf16[4,128,1024]{2,1,0:T(8,128)(2,1)}, u32[]{:S(2)}, u32[]{:S(2)}) collective-permute-start(bf16[4,128,1024]{2,1,0:T(8,128)(2,1)} %down.3), channel_id=1, source_target_pairs={{0,1},{1,0},{2,3},{3,2},{4,5},{5,4},{6,7},{7,6},{8,9},{9,8},{10,11... | collective-permute-start | bytes 3145736 | tf_op jit(solution)/shard_map/ppermute | solution.py:88
  278.5 25.5 %collective-permute-start.51 = (bf16[8,32,1024]{2,1,0:T(8,128)(2,1)}, bf16[8,32,1024]{2,1,0:T(8,128)(2,1)S(1)}, u32[]{:S(2)}, u32[]{:S(2)}) collective-permute-start(bf16[8,32,1024]{2,1,0:T(8,128)(2,1)} %get-tuple-element.135), channel_id=1, source_target_pairs={{0,16},{8,24},{16,0},{24,8},{1,17},{9,25},{17,1},{25,9},{2,18},{10... | collective-permute-start | bytes 1572872 | tf_op jit(solution)/shard_map/ppermute | solution.py:88
  279.1 24.9 %collective-permute-start.52 = (bf16[8,32,1024]{2,1,0:T(8,128)(2,1)}, bf16[8,32,1024]{2,1,0:T(8,128)(2,1)S(1)}, u32[]{:S(2)}, u32[]{:S(2)}) collective-permute-start(bf16[8,32,1024]{2,1,0:T(8,128)(2,1)} %get-tuple-element.136), channel_id=1, source_target_pairs={{0,24},{8,16},{16,8},{24,0},{1,25},{9,17},{17,9},{25,1},{2,26},{10... | collective-permute-start | bytes 1572872 | tf_op jit(solution)/shard_map/ppermute | solution.py:88
  284.1 47.4 %collective-permute-start.40 = (bf16[4,128,1024]{2,1,0:T(8,128)(2,1)}, bf16[4,128,1024]{2,1,0:T(8,128)(2,1)S(1)}, u32[]{:S(2)}, u32[]{:S(2)}) collective-permute-start(bf16[4,128,1024]{2,1,0:T(8,128)(2,1)} %first_grad.3), channel_id=1, source_target_pairs={{0,1},{1,0},{2,3},{3,2},{4,5},{5,4},{6,7},{7,6},{8,9},{9,8},{10,11... | collective-permute-start | bytes 3145736 | tf_op jit(solution)/shard_map/ppermute | solution.py:88
  311.8 43.4 %all-to-all-start.3 = ((bf16[8,32,1024]{2,1,0:T(8,128)(2,1)}), bf16[8,32,1024]{2,1,0:T(8,128)(2,1)S(1)}, u32[]{:S(2)}, u32[]{:S(2)}) async-start(bf16[8,32,1024]{2,1,0:T(8,128)(2,1)} %rep_sum.3), calls=%async_computation.3 | async-start | bytes 1048576 | tf_op jit(solution)/shard_map/all_to_all | solution.py:92
  351.6 45.7 %collective-permute-start.57 = (bf16[2,184,640]{2,1,0:T(8,128)(2,1)S(1)}, bf16[2,184,640]{2,1,0:T(8,128)(2,1)S(1)}, u32[]{:S(2)}, u32[]{:S(2)}) collective-permute-start(bf16[2,184,640]{2,1,0:T(8,128)(2,1)S(1)} %pad_maximum_fusion.3.r_2_), channel_id=1, source_target_pairs={{0,8},{8,0},{16,24},{24,16},{1,9},{9,1},{17,25},{25,17},{2,10},{10... | collective-permute-start | bytes 1413128 | tf_op jit(solution)/shard_map/ppermute | solution.py:88
  352.3 45.1 %collective-permute-start.58 = (bf16[2,184,640]{2,1,0:T(8,128)(2,1)S(1)}, bf16[2,184,640]{2,1,0:T(8,128)(2,1)S(1)}, u32[]{:S(2)}, u32[]{:S(2)}) collective-permute-start(bf16[2,184,640]{2,1,0:T(8,128)(2,1)S(1)} %pad_maximum_fusion.3.r_2_), channel_id=1, source_target_pairs={{0,16},{8,24},{16,0},{24,8},{1,17},{9,25},{17,1},{25,9},{2,18},{10... | collective-permute-start | bytes 1413128 | tf_op jit(solution)/shard_map/ppermute | solution.py:88
  353.6 43.8 %collective-permute-start.59 = (bf16[2,184,640]{2,1,0:T(8,128)(2,1)S(1)}, bf16[2,184,640]{2,1,0:T(8,128)(2,1)S(1)}, u32[]{:S(2)}, u32[]{:S(2)}) collective-permute-start(bf16[2,184,640]{2,1,0:T(8,128)(2,1)S(1)} %pad_maximum_fusion.3.r_2_), channel_id=1, source_target_pairs={{0,24},{8,16},{16,8},{24,0},{1,25},{9,17},{17,9},{25,1},{2,26},{10... | collective-permute-start | bytes 1413128 | tf_op jit(solution)/shard_map/ppermute | solution.py:88
  364.7 29.4 %collective-permute-start.54 = (bf16[32,1024]{1,0:T(8,128)(2,1)}, bf16[32,1024]{1,0:T(8,128)(2,1)S(1)}, u32[]{:S(2)}, u32[]{:S(2)}) collective-permute-start(bf16[32,1024]{1,0:T(8,128)(2,1)} %owner_sum.1.r_1_), channel_id=1, source_target_pairs={{0,16},{8,24},{16,0},{24,8},{1,17},{9,25},{17,1},{25,9},{2,18},{10... | collective-permute-start | bytes 196616 | tf_op jit(solution)/shard_map/ppermute | solution.py:88
  (90 other events, 1008.6 us)

commit v2 on v1

--- a/solution.py
+++ b/solution.py
@@ -100,16 +100,8 @@
     return [blocks[0]] + [swap(block, axis, i * step) for i, block in enumerate(blocks) if i]
 
 
-def exchange_z(blocks):
-    groups = [list(range(core, lax.axis_size("shard"), 2)) for core in range(2)]
-    return lax.all_to_all(
-        blocks, "shard", split_axis=0, concat_axis=0, axis_index_groups=groups, tiled=True
-    )
-
-
-def deliver_pairs(pairs):
-    parts = deliver(pairs, "shard", 2)
-    return [part[0] for part in parts], swap(jnp.stack([part[1] for part in parts]), "shard", 1)
+def after(value, *earlier):
+    return lax.optimization_barrier((value,) + earlier)[0]
 
 
 def both_cores(parts):
@@ -157,16 +149,19 @@
     return raised * (1.0 / jnp.sum(raised, axis=-1, keepdims=True))
 
 
-def blocks_kernel(n, in_ref, out_ref):
-    values = to_blocks(in_ref[...].astype(F32), n, out_ref.shape[2]).astype(BF16)
-    for i in range(out_ref.shape[0]):
-        out_ref[i] = values
-
-
-def attention_message_kernel(n, rep_ref, me_ref, q_ref, k_ref, v_ref, out_ref, gain_ref, *refs):
-    msg_refs, (out_msg_ref, hold_ref) = refs[: n // 2], refs[n // 2 :]
+def blocks_kernel(n, in_ref, *out_refs):
+    values = to_blocks(in_ref[...].astype(F32), n, out_refs[0].shape[1]).astype(BF16)
+    out_refs[0][...] = values
+    for ref in out_refs[1:]:
+        for i in range(ref.shape[0]):
+            ref[i] = values
+
+
+def attention_message_kernel(n, rep_ref, q_ref, k_ref, v_ref, out_ref, gain_ref, msg_ref):
     own = q_ref.shape[0]
-    piece, cols = hold_ref.shape[1:]
+    piece = msg_ref.shape[1]
+    cols = gain_ref.shape[1]
+    half = msg_ref.shape[2] - cols
     head_cols = cols // 3
     heads = head_cols // HD
     row = lax.broadcasted_iota(jnp.int32, (piece, own), 0) + rep_ref[0] * piece
@@ -184,23 +179,24 @@
         block = jnp.concatenate(parts, axis=1)
         for i in range(2):
             block = jnp.where(wide == own + i, gain_ref[i : i + 1, :], block)
-        hold_ref[s] = block.astype(BF16)
-    for i in range(n):
-        msg_refs[i // 2][i % 2] = hold_ref[me_ref[0] ^ i]
-    out_msg_ref[...] = to_blocks(dot(pick, out_ref[...]), n, out_msg_ref.shape[1]).astype(BF16)
-
-
-def join_kernel(n, reps, rep_ref, me_ref, *refs):
+        msg_ref[s, :, :cols] = block.astype(BF16)
+    rows = to_blocks(dot(pick, out_ref[...]), n, 2 * half).astype(BF16)
+    for s in range(n):
+        msg_ref[s, :, cols:] = rows[:, s % 2 * half : (s % 2 + 1) * half]
+
+
+def join_kernel(reps, rep_ref, *refs):
     for i in range(reps):
-        for s in range(n):
-            refs[reps][me_ref[0] ^ s, rep_ref[0] ^ i] = refs[i][s]
-
-
-def join_out_kernel(nz, reps, rep_ref, me_ref, mine_ref, other_ref, out_ref):
-    for core, ref in enumerate((mine_ref, other_ref)):
-        for i in range(reps):
-            for z in range(nz):
-                out_ref[me_ref[0] ^ (2 * z + core), rep_ref[0] ^ i] = ref[i, z]
+        refs[reps][:, rep_ref[0] ^ i] = refs[i][...]
+
+
+def join_out_kernel(reps, rep_ref, core_ref, mine_ref, other_ref, out_ref):
+    first = core_ref[0] == 0
+    half = mine_ref.shape[3]
+    for i in range(reps):
+        mine, other = mine_ref[i], other_ref[i]
+        out_ref[:, rep_ref[0] ^ i, :, :half] = jnp.where(first, mine, other)
+        out_ref[:, rep_ref[0] ^ i, :, half:] = jnp.where(first, other, mine)
 
 
 def fill_rows(values, rows):
@@ -249,7 +245,7 @@
     return message[:own], jnp.concatenate(parts, axis=1)[:each]
 
 
-def hidden_message_kernel(n, reps, rep_ref, core_ref, gate_ref, up_ref, down_ref, out_ref):
+def hidden_message_kernel(n, reps, rep_ref, gate_ref, up_ref, down_ref, *out_refs):
     own, units = gate_ref.shape
     held = down_ref.shape[0]
     each = held // (2 * reps)
@@ -257,7 +253,7 @@
     place = lax.broadcasted_iota(jnp.int32, (1, cols), 1)
     row = lax.broadcasted_iota(jnp.int32, (round_up(each, 8), held), 0)
     for i in range(2):
-        begin = each * (2 * rep_ref[0] + (core_ref[0] ^ i))
+        begin = each * (2 * rep_ref[0] + i)
         unit = place + begin
         for s in range(1, n):
             unit = unit + jnp.where(place >= each * s, held - each, 0)
@@ -267,27 +263,33 @@
         take = (lax.broadcasted_iota(jnp.int32, row.shape, 1) == row + begin) & (row < each)
         down = dot(jnp.where(take, 1.0, 0.0).astype(BF16), down_ref[...])
         message = pack_message(both, down[:each], 2 * cols).astype(BF16)
-        for z in range(out_ref.shape[0]):
-            out_ref[z, i] = message
-
-
-def hidden_weights_in_kernel(n, own, each, core_ref, mine_ref, other_ref, w_ref, down_ref, rows_ref):
+        for z in range(n // 2):
+            split_rows([ref.at[2 * z + i] for ref in out_refs], message)
+
+
+def split_rows(refs, values):
+    begin = 0
+    for ref in refs:
+        rows = ref.shape[0]
+        ref[...] = values[begin : begin + rows]
+        begin += rows
+
+
+def hidden_weights_in_kernel(n, own, each, *refs):
+    parts, (w_ref, down_ref) = refs[:-2], refs[-2:]
     block = w_ref.shape[1]
-    for side in range(2):
-        for z in range(n // 2):
-            s = 2 * z + (core_ref[0] ^ side)
-            message = other_ref[z] if side else mine_ref[z, 0]
-            both, down = unpack_message(message.astype(F32), own, each)
-            w_ref[s] = fill_rows(both, block).astype(BF16)
-            rows_ref[s, :each, :] = down
-    down = jnp.concatenate([rows_ref[s, :each, :] for s in range(n)], axis=0)
-    down_ref[...] = to_blocks(down, n, down_ref.shape[1]).astype(BF16)
+    downs = []
+    for s in range(n):
+        message = jnp.concatenate([part[s].astype(F32) for part in parts], axis=0)
+        both, down = unpack_message(message, own, each)
+        w_ref[s] = fill_rows(both, block).astype(BF16)
+        downs.append(down)
+    down_ref[...] = to_blocks(jnp.concatenate(downs, axis=0), n, down_ref.shape[1]).astype(BF16)
 
 
 def attend_kernel(rows, n, me_ref, mine_ref, other_ref, *refs):
     w_ref, cos_ref, sin_ref, start_ref, first_ref, q_ref, k_ref, v_ref, gains_ref = refs[:9]
-    pair_refs, mixed_ref = refs[9:-1], refs[-1]
-    core = me_ref[0] % 2
+    part_refs, mixed_ref = refs[9:-1], refs[-1]
     length, head_cols = q_ref.shape
     heads = head_cols // HD
     width = first_ref.shape[1]
@@ -308,7 +310,7 @@
         for z in range(n // 2):
             inputs = ref[z].astype(F32)
             normed = inputs * inverse_rms(inputs) * gains[0]
-            first_ref[rows_at(2 * z + (core ^ side), rows), :] = normed.astype(BF16)
+            first_ref[rows_at(me_ref[0] ^ (2 * z + side), rows), :] = normed.astype(BF16)
     block = min(256, length)
     for i in range(length // block):
         span = pl.ds(i * block, block)
@@ -328,18 +330,16 @@
             mixed = head_of(dot(probs.astype(BF16), v_ref[past, :]), h, heads)
             total = mixed if total is None else total + mixed
         mixed_ref[span, :] = total.astype(BF16)
-    for i in range(n):
-        pair_refs[i // 2][i % 2] = mixed_ref[rows_at(me_ref[0] ^ i, rows), :]
-
-
-def attend_back_kernel(nz, reps, rep_ref, me_ref, *refs):
-    mines, refs = refs[:nz], refs[nz:]
-    other_ref, first_ref, q_ref, k_ref, v_ref, cos_ref, sin_ref, start_ref, dqkv_ref = refs[:9]
-    piece_refs, (g_ref, dk_ref, dv_ref, hold_ref) = refs[9 : 9 + reps], refs[9 + reps :]
-    rows = other_ref.shape[1]
-    for z in range(nz):
-        g_ref[rows_at(me_ref[0] ^ (2 * z), rows), :] = mines[z][...]
-        g_ref[rows_at(me_ref[0] ^ (2 * z + 1), rows), :] = other_ref[z]
+    for i, ref in enumerate(part_refs):
+        ref[...] = mixed_ref[rows_at(me_ref[0] ^ i, rows), :]
+
+
+def attend_back_kernel(n, reps, rep_ref, me_ref, *refs):
+    parts, refs = refs[:n], refs[n:]
+    first_ref, q_ref, k_ref, v_ref, cos_ref, sin_ref, start_ref, dqkv_ref = refs[:8]
+    piece_refs, (g_ref, dk_ref, dv_ref, hold_ref) = refs[8 : 8 + reps], refs[8 + reps :]
+    for i, ref in enumerate(parts):
+        g_ref[rows_at(me_ref[0] ^ i, ref.shape[0]), :] = ref[...]
     length, head_cols = q_ref.shape
     heads = head_cols // HD
     block = min(256, length)
@@ -395,16 +395,15 @@
 
 
 def middle_kernel(n, me_ref, tokens_ref, *refs):
-    mines, refs = refs[: n // 2], refs[n // 2 :]
-    other_ref, w_ref, gains_ref, middle_ref, second_ref, attended_ref, hold_ref = refs
-    width = tokens_ref.shape[2]
-    for z in range(n // 2):
-        hold_ref[me_ref[0] ^ (2 * z)] = mines[z][...]
-        hold_ref[me_ref[0] ^ (2 * z + 1)] = other_ref[z]
+    parts, refs = refs[:n], refs[n:]
+    w_ref, gains_ref, middle_ref, second_ref, attended_ref, hold_ref = refs
+    width = tokens_ref.shape[1]
+    for i, ref in enumerate(parts):
+        hold_ref[me_ref[0] ^ i] = ref[...]
     attended = jnp.concatenate([hold_ref[s] for s in range(n)], axis=1)[:, :D]
     attended = to_blocks(attended.astype(F32), n, width).astype(BF16)
     attended_ref[...] = attended
-    middle = tokens_ref[0].astype(F32) + dot(attended, w_ref[...])
+    middle = tokens_ref[...].astype(F32) + dot(attended, w_ref[...])
     middle_ref[...] = middle
     second_ref[...] = (middle * inverse_rms(middle) * gains_ref[1:2, :]).astype(BF16)
 
@@ -414,14 +413,15 @@
     return jnp.concatenate([ref[begin + i] for i in range(count)], axis=0)
 
 
-def hidden_kernel(second_ref, cot_ref, w_ref, down_ref, grad_ref, grads_ref, hidden_ref):
+def hidden_kernel(rep_ref, second_ref, cot_ref, w_ref, down_ref, grad_ref, grads_ref, hidden_ref):
     reps, rows, _ = second_ref.shape
     units = down_ref.shape[0]
     for i in range(0, reps, 2):
         span = pl.ds(i * rows, 2 * rows)
         both = dot(stacked(second_ref, i, 2), w_ref[...])
         gate, up = both[:, :units], both[:, units:]
-        grad_hidden = contract_cols(stacked(cot_ref, i, 2), down_ref[...])
+        cots = jnp.concatenate([cot_ref[rep_ref[0] ^ (i + j)] for j in range(2)], axis=0)
+        grad_hidden = contract_cols(cots, down_ref[...])
         sigmoid = 1.0 / (1.0 + jnp.exp(-gate))
         silu = gate * sigmoid
         hidden_ref[span, :] = (silu * up).astype(BF16)
@@ -433,35 +433,40 @@
             grad_ref[i + j] = grad[j * rows : (j + 1) * rows]
 
 
-def hidden_weights_kernel(n, own, each, core_ref, *refs):
-    second_a, second_b, cot_a, cot_b, grads_a, grads_b, hidden_a, hidden_b, msg_ref, hold_ref = refs
-    cols = hold_ref.shape[2]
+def hidden_weights_kernel(n, own, each, rep_ref, *refs):
+    second_a, second_b, cot_a, cot_b, grads_a, grads_b, hidden_a, hidden_b, *msg_refs = refs
+    cols = msg_refs[0].shape[2]
     grad = contract_rows(stacked(second_a), grads_a[...])
     grad = grad + contract_rows(stacked(second_b), grads_b[...])
-    down = contract_rows(hidden_a[...], stacked(cot_a)) + contract_rows(hidden_b[...], stacked(cot_b))
+    cots = [
+        jnp.concatenate([ref[rep_ref[0] ^ i] for i in range(ref.shape[0])], axis=0) for ref in (cot_a, cot_b)
+    ]
+    down = contract_rows(hidden_a[...], cots[0]) + contract_rows(hidden_b[...], cots[1])
     down = from_blocks(down, n, own)
     block = grad.shape[0] // n
     for s in range(n):
         both = grad[s * block : s * block + own]
-        hold_ref[s] = pack_message(both, down[s * each : (s + 1) * each], cols).astype(BF16)
-    for z in range(n // 2):
-        for i in range(2):
-            msg_ref[z, i] = hold_ref[2 * z + (core_ref[0] ^ i)]
-
-
-def core_sums_kernel(in_ref, mine_ref, other_ref):
-    for core, ref in enumerate((mine_ref, other_ref)):
-        ref[...] = sum(in_ref[z, core].astype(F32) for z in range(in_ref.shape[0])).astype(BF16)
-
-
-def hidden_out_kernel(n, reps, each, rep_ref, core_ref, *refs):
+        message = pack_message(both, down[s * each : (s + 1) * each], cols).astype(BF16)
+        split_rows([ref.at[s] for ref in msg_refs], message)
+
+
+def core_sums_kernel(*refs):
+    out_ref = refs[-1]
+    for core in range(2):
+        sums = [
+            sum(part[s].astype(F32) for s in range(core, part.shape[0], 2)) for part in refs[:-1]
+        ]
+        out_ref[core] = jnp.concatenate(sums, axis=0).astype(BF16)
+
+
+def hidden_out_kernel(n, reps, each, rep_ref, *refs):
     parts, refs = refs[:reps], refs[reps:]
     gate_w_ref, up_w_ref, gain_ref, gate_ref, up_ref, down_ref, norm_ref, hold_ref = refs
     own = gate_ref.shape[0]
     units = 2 * reps * each
     for i, part in enumerate(parts):
         for core in range(2):
-            hold_ref[2 * (rep_ref[0] ^ i) + (core_ref[0] ^ core)] = part[core]
+            hold_ref[2 * (rep_ref[0] ^ i) + core] = part[core]
     cols = hold_ref.shape[2]
     boths = []
     for f in range(2 * reps):
@@ -497,11 +502,11 @@
 def middle_grad_kernel(n, own, reps, me_ref, *refs):
     parts, refs = refs[:reps], refs[reps:]
     cot_ref, middle_ref, gains_ref, w_ref, grad_ref, branch_ref = refs[:6]
-    pair_refs, hold_ref = refs[6:-1], refs[-1]
+    part_refs, hold_ref = refs[6:-1], refs[-1]
     rows = middle_ref.shape[0]
     middle = middle_ref[...]
     grad_second = sum(ref[...].astype(F32) for ref in parts)
-    grad = cot_ref[0].astype(F32) + norm_backward(
+    grad = cot_ref[...].astype(F32) + norm_backward(
         middle, inverse_rms(middle), gains_ref[1:2, :], grad_second
     )
     grad_ref[...] = grad
@@ -513,8 +518,8 @@
         attended = jnp.concatenate([attended, jnp.zeros((rows, n * head_cols - D), F32)], axis=1)
     for s in range(n):
         hold_ref[s] = attended[:, s * head_cols : (s + 1) * head_cols].astype(BF16)
-    for i in range(n):
-        pair_refs[i // 2][i % 2] = hold_ref[me_ref[0] ^ i]
+    for i, ref in enumerate(part_refs):
+        ref[...] = hold_ref[me_ref[0] ^ i]
 
 
 def out_weights_kernel(rep_ref, attended_ref, branch_ref, *refs):
@@ -571,7 +576,7 @@
 
 def input_grad_kernel(n, own, nz, *refs):
     parts, (tokens_ref, gains_ref, grad_ref, out_ref) = refs[:nz], refs[nz:]
-    inputs = tokens_ref[0].astype(F32)
+    inputs = tokens_ref[...].astype(F32)
     grad_first = sum(ref[...].astype(F32) for ref in parts)
     total = grad_ref[...] + norm_backward(inputs, inverse_rms(inputs), gains_ref[0:1, :], grad_first)
     out_ref[...] = from_blocks(total, n, own)
@@ -613,73 +618,51 @@
     rep = lax.axis_index("rep").astype(jnp.int32).reshape(1)
     own_block = (rows, width)
 
-    (tokens_in,) = call(
-        lambda *r: blocks_kernel(n, *r), "tokens_blocks", [((nz,) + own_block, BF16)], tokens
-    )
-    tokens_mine = exchange_z(tokens_in)
-    tokens_other = swap(tokens_mine, "shard", 1)
+    (tokens_in,) = call(lambda *r: blocks_kernel(n, *r), "tokens_blocks", [(own_block, BF16)], tokens)
+    tokens_mine, tokens_other = both_cores(spread(tokens_in, "shard", 2))
     gains_own = jnp.pad(jnp.stack([norm_one, norm_two]), ((0, 0), (0, qkv_cols - own))).astype(F32)
-    *qkv_messages, out_message = call(
+    (message,) = call(
         lambda *r: attention_message_kernel(n, *r),
         "attention_message",
-        [((2, piece, qkv_cols), BF16)] * nz + [((piece, width), BF16)],
-        w_query,
+        [((n, piece, qkv_cols + width // 2), BF16)],
+        after(w_query, tokens_in),
         w_key,
         w_value,
         w_out,
         gains_own,
-        scalars=(rep, me),
-        scratch=[((n, piece, qkv_cols), BF16)],
-    )
-    qkv_mine, qkv_other = deliver_pairs(qkv_messages)
-    qkv_piece = jnp.stack([block for z in range(nz) for block in (qkv_mine[z], qkv_other[z])])
+        scalars=(rep,),
+    )
+    arrived = exchange(message)
     (w_qkv,) = call(
-        lambda *r: join_kernel(n, reps, *r),
+        lambda *r: join_kernel(reps, *r),
         "join_qkv",
         [((n, reps, piece, qkv_cols), BF16)],
-        *spread(qkv_piece, "rep", 1),
-        scalars=(rep, me),
+        *spread(arrived[:, :, :qkv_cols], "rep", 1),
+        scalars=(rep,),
     )
     w_qkv = w_qkv.reshape(width, qkv_cols)
-
-    (messages,) = call(
+    cot_in, cot_tiled = call(
+        lambda *r: blocks_kernel(n, *r),
+        "cot_blocks",
+        [(own_block, BF16), ((reps,) + own_block, BF16)],
+        after(cotangent, message),
+    )
+    cot_mine = lax.all_to_all(after(cot_tiled, arrived), "rep", split_axis=0, concat_axis=0, tiled=True)
+
+    split = msg_rows // 2 // 16 * 16 + 16
+    part_rows = (split, msg_rows - split) if split < msg_rows else (msg_rows,)
+    messages = call(
         lambda *r: hidden_message_kernel(n, reps, *r),
         "hidden_message",
-        [((nz, 2, msg_rows, 2 * units), BF16)],
-        w_gate,
+        [((n, part, 2 * units), BF16) for part in part_rows],
+        after(w_gate, cot_in),
         w_up,
         w_down,
-        scalars=(rep, core),
-    )
-    out_message, messages, tokens_mine = lax.optimization_barrier((out_message, messages, tokens_mine))
-    out_mine, out_other = both_cores(
-        spread(jnp.stack(spread(out_message, "shard", 2)), "rep", 1)
-    )
-    (out_full,) = call(
-        lambda *r: join_out_kernel(nz, reps, *r),
-        "join_out",
-        [((n, reps, piece, width), BF16)],
-        out_mine,
-        out_other,
-        scalars=(rep, me),
-    )
-    out_full = out_full.reshape(width, width)
-    messages = exchange_z(messages)
-    w_hidden, w_down_in = call(
-        lambda *r: hidden_weights_in_kernel(n, own, each, *r),
-        "hidden_weights_in",
-        [((n, block, 2 * units), BF16), ((units, width), BF16)],
-        messages,
-        swap(messages[:, 1], "shard", 1),
-        scalars=(core,),
-        scratch=[((n, round_up(each, 8), D), F32)],
-    )
-    w_hidden = w_hidden.reshape(width, 2 * units)
-    (cot_in,) = call(
-        lambda *r: blocks_kernel(n, *r), "cot_blocks", [((1,) + own_block, BF16)], cotangent
-    )
-    cot_in, w_qkv = lax.optimization_barrier((cot_in, w_qkv))
-    cot_mine, cot_other = both_cores(spread(cot_in[0], "rep", 1))
+        scalars=(rep,),
+    )
+    hidden_first = exchange(after(messages[0], tokens_mine, cot_mine))
+
+    out_mine, out_other = both_cores(spread(after(arrived, w_qkv)[:, :, qkv_cols:], "rep", 1))
 
     doc_start, position = doc_layout(lengths[0], length)
     cosines, sines = rope_tables(position)
@@ -693,7 +676,7 @@
         [((length, width), BF16)]
         + [(head_shape, BF16)] * 3
         + [((2, width), F32)]
-        + [((2, rows, head_cols), BF16)] * nz,
+        + [((rows, head_cols), BF16)] * n,
         tokens_mine,
         tokens_other,
         w_qkv,
@@ -703,20 +686,38 @@
         scalars=(me,),
         scratch=[(head_shape, BF16)],
     )
-    mixed_mine, mixed_other = deliver_pairs(mixed)
+    mixed = deliver([after(mixed[0], hidden_first)] + mixed[1:], "shard", 1)
+    hidden_rest = [exchange(after(message, *mixed)) for message in messages[1:]]
+    (out_full,) = call(
+        lambda *r: join_out_kernel(reps, *r),
+        "join_out",
+        [((n, reps, piece, width), BF16)],
+        after(out_mine, gains),
+        out_other,
+        scalars=(rep, core),
+    )
+    out_full = out_full.reshape(width, width)
 
     middle, second, attended = call(
         lambda *r: middle_kernel(n, *r),
         "middle",
         [(own_block, F32), (own_block, BF16), (own_block, BF16)],
         tokens_in,
-        *mixed_mine,
-        mixed_other,
+        *mixed,
         out_full,
         gains,
         scalars=(me,),
         scratch=[((n, rows, head_cols), BF16)],
     )
+    w_hidden, w_down_in = call(
+        lambda *r: hidden_weights_in_kernel(n, own, each, *r),
+        "hidden_weights_in",
+        [((n, block, 2 * units), BF16), ((units, width), BF16)],
+        after(hidden_first, second),
+        *hidden_rest,
+    )
+    w_hidden = w_hidden.reshape(width, 2 * units)
+    cot_other = swap(cot_mine, "shard", 1)
 
     second_mine, second_other = both_cores(spread(second, "rep", 1))
     side_outs = [
@@ -726,45 +727,47 @@
     ]
 
     def hidden_side(seconds, cots, name):
-        return call(hidden_kernel, name, side_outs, seconds, cots, w_hidden, w_down_in)
+        return call(hidden_kernel, name, side_outs, seconds, cots, w_hidden, w_down_in, scalars=(rep,))
 
     def plane_sums(mine, other):
         sums = call(pair_sum_kernel, "pair_sum", [(own_block, BF16)] * reps, mine, swap(other, "shard", 1))
-        return deliver(sums, "rep", 1)
-
-    grad_mine, grads_mine, hidden_mine = hidden_side(second_mine, cot_mine, "hidden_mine")
+        return sums, deliver(sums, "rep", 1)
+
     grad_other, grads_other, hidden_other = hidden_side(second_other, cot_other, "hidden_other")
-    grad_second = plane_sums(grad_mine, grad_other)
-    (hidden_messages,) = call(
+    grad_mine, grads_mine, hidden_mine = hidden_side(
+        after(second_mine, grad_other), cot_mine, "hidden_mine"
+    )
+    sums, grad_second = plane_sums(grad_mine, grad_other)
+    hidden_messages = call(
         lambda *r: hidden_weights_kernel(n, own, each, *r),
         "hidden_weights",
-        [((nz, 2, msg_rows, 2 * units), BF16)],
+        [((n, part, 2 * units), BF16) for part in part_rows],
         second_mine,
         second_other,
         cot_mine,
         cot_other,
         grads_mine,
         grads_other,
-        hidden_mine,
+        after(hidden_mine, sums[0]),
         hidden_other,
-        scalars=(core,),
-        scratch=[((n, msg_rows, 2 * units), BF16)],
-    )
-    hidden_messages = exchange_z(hidden_messages)
+        scalars=(rep,),
+    )
+    hidden_sums = [exchange(hidden_messages[0])]
 
     grad_middle, grad_branch, *grad_heads = call(
         lambda *r: middle_grad_kernel(n, own, reps, *r),
         "middle_grad",
-        [(own_block, F32), (own_block, BF16)] + [((2, rows, head_cols), BF16)] * nz,
+        [(own_block, F32), (own_block, BF16)] + [((rows, head_cols), BF16)] * n,
         *grad_second,
         cot_in,
-        middle,
+        after(middle, hidden_messages[0]),
         gains,
         out_full,
         scalars=(me,),
         scratch=[((n, rows, head_cols), BF16)],
     )
-    heads_mine, heads_other = deliver_pairs(grad_heads)
+    grad_heads = deliver(grad_heads, "shard", 1)
+    hidden_sums += [exchange(after(message, *grad_heads)) for message in hidden_messages[1:]]
     out_pieces = call(
         out_weights_kernel,
         "out_weights",
@@ -774,56 +777,63 @@
         scalars=(rep,),
         scratch=[((n, reps, piece, width), BF16)],
     )
+    down_other, down_mine = [
+        call(down_kernel, "down", [((reps, rows, width), BF16)], after(hidden, out_pieces[0]), w_down_in)[0]
+        for hidden in (hidden_other, hidden_mine)
+    ]
 
     grad_qkv, *attention_pieces = call(
-        lambda *r: attend_back_kernel(nz, reps, *r),
+        lambda *r: attend_back_kernel(n, reps, *r),
         "attend_back",
         [((length, qkv_cols), BF16)] + [((n, piece, qkv_cols), BF16)] * reps,
-        *heads_mine,
-        heads_other,
+        *grad_heads,
         first_all,
         query,
         key,
         value,
         cosines,
         sines,
-        start,
+        after(start, down_mine, down_other),
         scalars=(rep, me),
         scratch=[(head_shape, BF16)] + [(head_shape, F32)] * 2 + [((n, reps, piece, qkv_cols), BF16)],
     )
-    first_sides = [
-        call(
-            lambda *r, side=side: first_grad_kernel(rows, side, *r),
+
+    def first_side(grads, side):
+        return call(
+            lambda *r: first_grad_kernel(rows, side, *r),
             "first_grad",
             [((nz, rows, width), BF16)],
-            grad_qkv,
+            grads,
             w_qkv,
             scalars=(me,),
         )[0]
-        for side in (1, 0)
-    ]
+
+    first_other = first_side(grad_qkv, 1)
+    first_mine = first_side(after(grad_qkv, first_other), 0)
     first_sums = call(
-        pair_sum_kernel, "pair_sum", [(own_block, BF16)] * nz, first_sides[1], swap(first_sides[0], "shard", 1)
-    )
+        pair_sum_kernel, "pair_sum", [(own_block, BF16)] * nz, first_mine, swap(first_other, "shard", 1)
+    )
+    first_parts = deliver(first_sums, "shard", 2)
     (input_grad,) = call(
         lambda *r: input_grad_kernel(n, own, nz, *r),
         "input_grad",
         [((rows, D), F32)],
-        *deliver(first_sums, "shard", 2),
+        *first_parts,
         tokens_in,
         gains,
         grad_middle,
     )
 
-    def owner_pieces(pieces):
+    def owner_pieces(pieces, *earlier):
         parts = deliver(pieces, "rep", 1)
+        parts[0] = after(parts[0], *earlier)
         (summed,) = call(
             lambda *r: rep_sum_kernel(reps, *r), "rep_sum", [(pieces[0].shape, BF16)], *parts
         )
         return exchange(summed)
 
     gain_cols = [gain.astype(F32)[:, None] for gain in (norm_one, norm_two)]
-    attention_parts = spread(owner_pieces(attention_pieces), "rep", 1)
+    attention_parts = spread(owner_pieces(attention_pieces, first_sums[0]), "rep", 1)
     grad_w_query, grad_w_key, grad_w_value, grad_norm_one = call(
         lambda *r: attention_out_kernel(n, reps, *r),
         "attention_out",
@@ -837,7 +847,7 @@
         scratch=[((reps, n, piece, qkv_cols), F32)],
     )
 
-    (out_piece,) = call(owner_sum_kernel, "owner_sum", [((piece, width), BF16)], owner_pieces(out_pieces))
+    (out_piece,) = call(owner_sum_kernel, "owner_sum", [((piece, width), BF16)], owner_pieces(out_pieces, first_sums[0]))
     (grad_w_out,) = call(
         lambda *r: out_out_kernel(n, reps, *r),
         "out_out",
@@ -847,10 +857,7 @@
         scratch=[((reps, piece, width), F32)],
     )
 
-    sum_mine, sum_other = call(
-        core_sums_kernel, "core_sums", [((msg_rows, 2 * units), BF16)] * 2, hidden_messages
-    )
-    core_sums = jnp.stack([sum_mine, swap(sum_other, "shard", 1)])
+    (core_sums,) = call(core_sums_kernel, "core_sums", [((2, msg_rows, 2 * units), BF16)], *hidden_sums)
     grad_w_gate, grad_w_up, grad_w_down, grad_norm_two = call(
         lambda *r: hidden_out_kernel(n, reps, each, *r),
         "hidden_out",
@@ -859,20 +866,16 @@
         w_gate,
         w_up,
         gain_cols[1],
-        scalars=(rep, core),
+        scalars=(rep,),
         scratch=[((2 * reps, msg_rows, 2 * units), BF16)],
     )
 
-    down_parts = [
-        call(down_kernel, "down", [((reps, rows, width), BF16)], hidden, w_down_in)[0]
-        for hidden in (hidden_other, hidden_mine)
-    ]
     (output,) = call(
         lambda *r: output_kernel(n, own, *r),
         "output",
         [((rows, D), BF16)],
         middle,
-        *plane_sums(down_parts[1], down_parts[0]),
+        *plane_sums(after(down_mine, first_sums[0]), down_other)[1],
     )
     return (
         output,

time: 415 us -> 415 us (level)
  blocking collectives: 0 us -> 13.7 us
  starting transfers between devices: 84.1 us -> 95.2 us
  local copies, waits for them, and re-layouts: 43.2 us -> 33.8 us
  waiting for transfers between devices: 154 us -> 145 us
    all_to_all x2 -> x6, waiting for transfers between devices: 0.01 us -> 29.7 us  [exchange(): lax.all_to_all(block, 'shard', split_axis=0, concat_axis=0, tiled=True)]
    ppermute x60 -> x57, waiting for transfers between devices: 138 us -> 115 us  [swap(): return lax.ppermute(block, axis, [(i, i ^ k) for i in range(count)])]
    all_to_all x2 -> x6, starting transfers between devices: 11.7 us -> 32.5 us  [exchange(): lax.all_to_all(block, 'shard', split_axis=0, concat_axis=0, tiled=True)]
    all_to_all x3 -> x1, waiting for transfers between devices: 15.5 us -> 0.01 us  [shards(): lax.all_to_all(after(cot_tiled, arrived), 'rep', split_axis=0, concat_axi...]
    all_to_all x3 -> x1, starting transfers between devices: 18.4 us -> 4.25 us  [shards(): lax.all_to_all(after(cot_tiled, arrived), 'rep', split_axis=0, concat_axi...]
    all_to_all x0 -> x1, blocking collectives: none -> 13.7 us  [exchange(): lax.all_to_all(block, 'shard', split_axis=0, concat_axis=0, tiled=True)]
    slice x12 -> x1, local copies, waits for them, and re-layouts: 7.08 us -> 0.02 us  [shards(): arrived[:, :, :qkv_cols]]
    unnamed x112 -> x131, local copies, waits for them, and re-layouts: 28 us -> 23.4 us
  transfers between devices with their start and end apart: 65 -> 64, of which waited for: 28 -> 25; matrix products, arithmetic and copies ran while one was open for 8% -> 5% of each run, Pallas kernels for 20% -> 18%
where the time goes in v2:
time: 415 us; the launch traced here: 409 us
  waiting for transfers between devices  145 us (35%)
  Pallas kernels  115 us (28%)
  starting transfers between devices  95.2 us (23%)
  local copies, waits for them, and re-layouts  33.8 us (8%)
  blocking collectives  13.7 us (3%)
  other arithmetic  5.66 us (1%)
    pallas_call x31, Pallas kernels, call(): pl.pallas_call(kernel, out_shape=[jax.ShapeDtypeStruct(shape, dtype) for...  115 us
    ppermute x57, waiting for transfers between devices, swap(): return lax.ppermute(block, axis, [(i, i ^ k) for i in range(count)])  115 us
    ppermute x57, starting transfers between devices, swap(): return lax.ppermute(block, axis, [(i, i ^ k) for i in range(count)])  58.5 us
    all_to_all x6, starting transfers between devices, exchange(): lax.all_to_all(block, 'shard', split_axis=0, concat_axis=0, tiled=True)  32.5 us
    all_to_all x6, waiting for transfers between devices, exchange(): lax.all_to_all(block, 'shard', split_axis=0, concat_axis=0, tiled=True)  29.7 us
    unnamed x131, local copies, waits for them, and re-layouts  23.4 us
    all_to_all x1, blocking collectives, exchange(): lax.all_to_all(block, 'shard', split_axis=0, concat_axis=0, tiled=True)  13.7 us
  transfers between devices with their start and end apart: 64, of which 25 were waited for; matrix products, arithmetic and copies ran while one was open for 5% of the time, Pallas kernels for 18%

profile of v2, /device:TPU:10, one launch (start us, length us, event | category | flops | bytes accessed | tf_op | source)
XLA Modules:
  0.0 409.5 jit_solution(15481909685511574670)
XLA Ops:
  10.5 5.3 %all-to-all-start = ((bf16[8,32,896]{2,1,0:T(8,128)(2,1)}), bf16[8,32,896]{2,1,0:T(8,128)(2,1)S(1)}, u32[]{:S(2)}, u32[]{:S(2)}) async-start(bf16[8,32,896]{2,1,0:T(8,128)(2,1)} %attention_message.1), calls=%async_computation | async-start | bytes 917504 | tf_op jit(solution)/shard_map/all_to_all | solution.py:92
  18.9 7.9 %all-to-all-done = bf16[8,32,896]{2,1,0:T(8,128)(2,1)S(1)} async-done(((bf16[8,32,896]{2,1,0:T(8,128)(2,1)}), bf16[8,32,896]{2,1,0:T(8,128)(2,1)S(1)}, u32[]{:S(2)}, u32[]{:S(2)}) %all-to-all-start) | async-done | bytes 458784 | tf_op jit(solution)/shard_map/all_to_all | solution.py:92
  44.6 7.4 %collective-permute-done.1 = bf16[128,1024]{1,0:T(8,128)(2,1)S(1)} collective-permute-done((bf16[128,1024]{1,0:T(8,128)(2,1)S(1)}, bf16[128,1024]{1,0:T(8,128)(2,1)S(1)}, u32[]{:S(2)}, u32[]{:S(2)}) %collective-permute-start.1) | collective-permute-done | bytes 262176 | tf_op jit(solution)/shard_map/ppermute | solution.py:88
  52.0 5.7 %collective-permute-done.2 = bf16[128,1024]{1,0:T(8,128)(2,1)S(1)} collective-permute-done((bf16[128,1024]{1,0:T(8,128)(2,1)S(1)}, bf16[128,1024]{1,0:T(8,128)(2,1)S(1)}, u32[]{:S(2)}, u32[]{:S(2)}) %collective-permute-start.2) | collective-permute-done | bytes 262176 | tf_op jit(solution)/shard_map/ppermute | solution.py:88
  68.8 5.7 %collective-permute-done.14 = bf16[8,32,512]{2,1,0:T(8,128)(2,1)S(1)} collective-permute-done((bf16[8,32,512]{2,1,0:T(8,128)(2,1)S(1)}, bf16[8,32,512]{2,1,0:T(8,128)(2,1)S(1)}, u32[]{:S(2)}, u32[]{:S(2)}) %collective-permute-start.14) | collective-permute-done | bytes 262176 | tf_op jit(solution)/shard_map/ppermute | solution.py:88
  87.6 9.1 %attend.1 = (bf16[1024,1024]{1,0:T(8,128)(2,1)}, bf16[1024,128]{1,0:T(8,128)(2,1)}, bf16[1024,128]{1,0:T(8,128)(2,1)}, bf16[1024,128]{1,0:T(8,128)(2,1)}, f32[2,...) custom-call(s32[1]{0:T(128)} %bitcast.r_0_.r_1_, ...), custom_call_target="tpu_custom_call" | custom-call | tf_op jit(solution)/shard_map/attend/pallas_call | solution.py:115
  109.1 5.4 %all-to-all-start.3 = ((bf16[8,88,640]{2,1,0:T(8,128)(2,1)}), bf16[8,88,640]{2,1,0:T(8,128)(2,1)}, u32[]{:S(2)}, u32[]{:S(2)}) async-start(bf16[8,88,640]{2,1,0:T(8,128)(2,1)} %get-tuple-element.125), calls=%async_computation.3 | async-start | bytes 1802240 | tf_op jit(solution)/shard_map/all_to_all | solution.py:92
  124.2 5.9 %collective-permute-done.18 = bf16[128,1024]{1,0:T(8,128)(2,1)S(1)} collective-permute-done((bf16[128,1024]{1,0:T(8,128)(2,1)}, bf16[128,1024]{1,0:T(8,128)(2,1)S(1)}, u32[]{:S(2)}, u32[]{:S(2)}) %collective-permute-start.18) | collective-permute-done | bytes 262176 | tf_op jit(solution)/shard_map/ppermute | solution.py:88
  130.1 5.4 %collective-permute-done.19 = bf16[128,1024]{1,0:T(8,128)(2,1)S(1)} collective-permute-done((bf16[128,1024]{1,0:T(8,128)(2,1)}, bf16[128,1024]{1,0:T(8,128)(2,1)S(1)}, u32[]{:S(2)}, u32[]{:S(2)}) %collective-permute-start.19) | collective-permute-done | bytes 262176 | tf_op jit(solution)/shard_map/ppermute | solution.py:88
  141.2 5.6 %hidden_other.1 = (bf16[4,128,1024]{2,1,0:T(8,128)(2,1)}, bf16[512,640]{1,0:T(8,128)(2,1)}, bf16[512,320]{1,0:T(8,128)(2,1)}) custom-call(s32[1]{0:T(128)} %bitcast.5.r_0_.rep_ref, bf16[4,128,1024]{2,1,0:T(8,128)(2,1)} %collective-permute-done.21.second_ref.r_2_, bf16[4,128,1024]{2,1,0:T(8,128)(2,1)} %copy-done.4, bf16[1024,640]{1,0:T(8,128)(2,1)} %bitcast.38, ...), custom_call_target="tpu_custom_call" | custom-call | tf_op jit(solution)/shard_map/hidden_other/pallas_call | solution.py:115
  147.0 5.7 %hidden_mine.1 = (bf16[4,128,1024]{2,1,0:T(8,128)(2,1)}, bf16[512,640]{1,0:T(8,128)(2,1)}, bf16[512,320]{1,0:T(8,128)(2,1)}) custom-call(s32[1]{0:T(128)} %bitcast.5.r_0_.rep_ref, bf16[4,128,1024]{2,1,0:T(8,128)(2,1)} %copy-done.1, bf16[4,128,1024]{2,1,0:T(8,128)(2,1)} %copy-done, bf16[1024,640]{1,0:T(8,128)(2,1)} %bitcast.39, ...), custom_call_target="tpu_custom_call" | custom-call | tf_op jit(solution)/shard_map/hidden_mine/pallas_call | solution.py:115
  159.7 6.6 %hidden_weights.1 = (bf16[8,96,640]{2,1,0:T(8,128)(2,1)}, bf16[8,88,640]{2,1,0:T(8,128)(2,1)}) custom-call(s32[1]{0:T(128)} %bitcast.5.r_0_.rep_ref, bf16[4,128,1024]{2,1,0:T(8,128)(2,1)} %copy-done.1, bf16[4,128,1024]{2,1,0:T(8,128)(2,1)} %collective-permute-done.21.second_ref.r_2_, bf16[4,128,1024]{2,1,0:T(8,128)(2,1)} %copy-done, ...), custom_call_target="tpu_custom_call" | custom-call | tf_op jit(solution)/shard_map/hidden_weights/pallas_call | solution.py:115
  193.6 11.3 %attend_back.1 = (bf16[1024,384]{1,0:T(8,128)(2,1)}, bf16[8,32,384]{2,1,0:T(8,128)(2,1)}, bf16[8,32,384]{2,1,0:T(8,128)(2,1)}, bf16[8,32,384]{2,1,0:T(8,128)(2,1)}, bf16[8,32,384]{2,1,0:T(8,128)(2,1)}) custom-call(s32[1]{0:T(128)} %bitcast.5.r_0_.rep_ref, s32[1]{0:T(128)} %bitcast.r_0_.r_1_, bf16[128,128]{1,0:T(8,128)(2,1)} %get-tuple-element.146.r_2_, ...), custom_call_target="tpu_custom_call" | custom-call | tf_op jit(solution)/shard_map/attend_back/pallas_call | solution.py:115
  224.6 13.7 %all_to_all.40.r_1_ = bf16[8,32,384]{2,1,0:T(8,128)(2,1)} all-to-all(bf16[8,32,384]{2,1,0:T(8,128)(2,1)} %rep_sum.2), channel_id=1, replica_groups=mesh['rep'=4,'shard'=8] {'shard'}, dimensions={0} | all-to-all | bytes 393216 | tf_op jit(solution)/shard_map/all_to_all | solution.py:92
  243.5 21.7 %all-to-all-done.6.refs_0_ = bf16[8,96,640]{2,1,0:T(8,128)(2,1)S(1)} async-done(((bf16[8,96,640]{2,1,0:T(8,128)(2,1)}), bf16[8,96,640]{2,1,0:T(8,128)(2,1)S(1)}, u32[]{:S(2)}, u32[]{:S(2)}) %all-to-all-start.6) | async-done | bytes 983072 | tf_op jit(solution)/shard_map/all_to_all | solution.py:92
  265.2 7.0 %all-to-all-start.7 = ((bf16[8,88,640]{2,1,0:T(8,128)(2,1)}), bf16[8,88,640]{2,1,0:T(8,128)(2,1)S(1)}, u32[]{:S(2)}, u32[]{:S(2)}) async-start(bf16[8,88,640]{2,1,0:T(8,128)(2,1)} %get-tuple-element.186), calls=%async_computation.7 | async-start | bytes 1802240 | tf_op jit(solution)/shard_map/all_to_all | solution.py:92
  275.6 11.5 %collective-permute-done.48.r_1_ = bf16[8,32,1024]{2,1,0:T(8,128)(2,1)S(1)} collective-permute-done((bf16[8,32,1024]{2,1,0:T(8,128)(2,1)}, bf16[8,32,1024]{2,1,0:T(8,128)(2,1)S(1)}, u32[]{:S(2)}, u32[]{:S(2)}) %collective-permute-start.48) | collective-permute-done | bytes 524320 | tf_op jit(solution)/shard_map/ppermute | solution.py:88
  287.1 11.4 %collective-permute-done.50.r_3_ = bf16[8,32,1024]{2,1,0:T(8,128)(2,1)S(1)} collective-permute-done((bf16[8,32,1024]{2,1,0:T(8,128)(2,1)S(1)}, bf16[8,32,1024]{2,1,0:T(8,128)(2,1)S(1)}, u32[]{:S(2)}, u32[]{:S(2)}) %collective-permute-start.50) | collective-permute-done | bytes 524320 | tf_op jit(solution)/shard_map/ppermute | solution.py:88
  301.9 5.3 %all-to-all-start.5 = ((bf16[8,32,1024]{2,1,0:T(8,128)(2,1)}), bf16[8,32,1024]{2,1,0:T(8,128)(2,1)S(1)}, u32[]{:S(2)}, u32[]{:S(2)}) async-start(bf16[8,32,1024]{2,1,0:T(8,128)(2,1)} %rep_sum.3), calls=%async_computation.5 | async-start | bytes 1048576 | tf_op jit(solution)/shard_map/all_to_all | solution.py:92
  316.5 9.4 %collective-permute-done.39.r_1_ = bf16[128,1024]{1,0:T(8,128)(2,1)S(1)} collective-permute-done((bf16[128,1024]{1,0:T(8,128)(2,1)}, bf16[128,1024]{1,0:T(8,128)(2,1)S(1)}, u32[]{:S(2)}, u32[]{:S(2)}) %collective-permute-start.39) | collective-permute-done | bytes 262176 | tf_op jit(solution)/shard_map/ppermute | solution.py:88
  328.5 7.5 %collective-permute-done.40.r_2_ = bf16[128,1024]{1,0:T(8,128)(2,1)S(1)} collective-permute-done((bf16[128,1024]{1,0:T(8,128)(2,1)}, bf16[128,1024]{1,0:T(8,128)(2,1)S(1)}, u32[]{:S(2)}, u32[]{:S(2)}) %collective-permute-start.40) | collective-permute-done | bytes 262176 | tf_op jit(solution)/shard_map/ppermute | solution.py:88
  337.7 6.0 %collective-permute-done.41.r_3_ = bf16[128,1024]{1,0:T(8,128)(2,1)S(1)} collective-permute-done((bf16[128,1024]{1,0:T(8,128)(2,1)}, bf16[128,1024]{1,0:T(8,128)(2,1)S(1)}, u32[]{:S(2)}, u32[]{:S(2)}) %collective-permute-start.41) | collective-permute-done | bytes 262176 | tf_op jit(solution)/shard_map/ppermute | solution.py:88
  355.8 19.1 %collective-permute-done.47.r_4_ = bf16[8,32,384]{2,1,0:T(8,128)(2,1)S(1)} collective-permute-done((bf16[8,32,384]{2,1,0:T(8,128)(2,1)S(1)}, bf16[8,32,384]{2,1,0:T(8,128)(2,1)S(1)}, u32[]{:S(2)}, u32[]{:S(2)}) %collective-permute-start.47) | collective-permute-done | bytes 196640 | tf_op jit(solution)/shard_map/ppermute | solution.py:88
  400.7 7.1 %hidden_out.1 = (f32[120,2560]{1,0:T(8,128)}, f32[120,2560]{1,0:T(8,128)}, f32[320,960]{1,0:T(8,128)}, f32[120,1]{1,0:T(8,128)}) custom-call(s32[1]{0:T(128)} %bitcast.5.r_0_.rep_ref, bf16[2,184,640]{2,1,0:T(8,128)(2,1)} %core_sums.1.r_1_, bf16[2,184,640]{2,1,0:T(8,128)(2,1)} %copy-done.17, bf16[2,184,640]{2,1,0:T(8,128)(2,1)} %copy-done.18, ...), custom_call_target="tpu_custom_call" | custom-call | tf_op jit(solution)/shard_map/hidden_out/pallas_call | solution.py:115
  (291 shorter events, 201.2 us)
Async XLA Ops:
  26.9 31.0 %all-to-all-start.1 = ((bf16[4,128,1024]{2,1,0:T(8,128)(2,1)}), bf16[4,128,1024]{2,1,0:T(8,128)(2,1)S(1)}, u32[]{:S(2)}, u32[]{:S(2)}) async-start(bf16[4,128,1024]{2,1,0:T(8,128)(2,1)} %get-tuple-element.108), calls=%async_computation.1 | async-start | bytes 2097152 | tf_op jit(solution)/shard_map/all_to_all | solution.py:650
  34.0 23.7 %collective-permute-start.2 = (bf16[128,1024]{1,0:T(8,128)(2,1)S(1)}, bf16[128,1024]{1,0:T(8,128)(2,1)S(1)}, u32[]{:S(2)}, u32[]{:S(2)}) collective-permute-start(bf16[128,1024]{1,0:T(8,128)(2,1)S(1)} %copy-done.5), channel_id=1, source_target_pairs={{0,6},{1,7},{2,4},{3,5},{4,2},{5,3},{6,0},{7,1},{8,14},{9,15},{10,... | collective-permute-start | bytes 786440 | tf_op jit(solution)/shard_map/ppermute | solution.py:88
  40.5 21.8 %collective-permute-start.4 = (bf16[8,32,384]{2,1,0:T(8,128)(2,1)S(1)}, bf16[8,32,384]{2,1,0:T(8,128)(2,1)S(1)}, u32[]{:S(2)}, u32[]{:S(2)}) collective-permute-start(bf16[8,32,384]{2,1,0:T(8,128)(2,1)S(1)} %slice.8.r_1_), channel_id=1, source_target_pairs={{0,8},{8,0},{16,24},{24,16},{1,9},{9,1},{17,25},{25,17},{2,10},{10... | collective-permute-start | bytes 589832 | tf_op jit(solution)/shard_map/ppermute | solution.py:88
  40.6 21.7 %collective-permute-start.5 = (bf16[8,32,384]{2,1,0:T(8,128)(2,1)S(1)}, bf16[8,32,384]{2,1,0:T(8,128)(2,1)S(1)}, u32[]{:S(2)}, u32[]{:S(2)}) collective-permute-start(bf16[8,32,384]{2,1,0:T(8,128)(2,1)S(1)} %slice.8.r_1_), channel_id=1, source_target_pairs={{0,16},{8,24},{16,0},{24,8},{1,17},{9,25},{17,1},{25,9},{2,18},{10... | collective-permute-start | bytes 589832 | tf_op jit(solution)/shard_map/ppermute | solution.py:88
  57.9 47.7 %all-to-all-start.2 = ((bf16[8,96,640]{2,1,0:T(8,128)(2,1)}), bf16[8,96,640]{2,1,0:T(8,128)(2,1)}, u32[]{:S(2)}, u32[]{:S(2)}) async-start(bf16[8,96,640]{2,1,0:T(8,128)(2,1)} %get-tuple-element.109), calls=%async_computation.2 | async-start | bytes 1966080 | tf_op jit(solution)/shard_map/all_to_all | solution.py:92
  79.7 34.8 %collective-permute-start.17 = (bf16[4,8,32,512]{3,2,1,0:T(8,128)(2,1)S(1)}, bf16[4,8,32,512]{3,2,1,0:T(8,128)(2,1)}, u32[]{:S(2)}, u32[]{:S(2)}) collective-permute-start(bf16[4,8,32,512]{3,2,1,0:T(8,128)(2,1)S(1)} %pad_maximum_fusion.1.r_2_), channel_id=1, source_target_pairs={{0,1},{1,0},{2,3},{3,2},{4,5},{5,4},{6,7},{7,6},{8,9},{9,8},{10,11... | collective-permute-start | bytes 3145736 | tf_op jit(solution)/shard_map/ppermute | solution.py:88
  109.1 27.6 %all-to-all-start.3 = ((bf16[8,88,640]{2,1,0:T(8,128)(2,1)}), bf16[8,88,640]{2,1,0:T(8,128)(2,1)}, u32[]{:S(2)}, u32[]{:S(2)}) async-start(bf16[8,88,640]{2,1,0:T(8,128)(2,1)} %get-tuple-element.125), calls=%async_computation.3 | async-start | bytes 1802240 | tf_op jit(solution)/shard_map/all_to_all | solution.py:92
  238.4 26.8 %all-to-all-start.6 = ((bf16[8,96,640]{2,1,0:T(8,128)(2,1)}), bf16[8,96,640]{2,1,0:T(8,128)(2,1)S(1)}, u32[]{:S(2)}, u32[]{:S(2)}) async-start(bf16[8,96,640]{2,1,0:T(8,128)(2,1)} %get-tuple-element.141), calls=%async_computation.6 | async-start | bytes 1966080 | tf_op jit(solution)/shard_map/all_to_all | solution.py:92
  265.2 36.7 %all-to-all-start.7 = ((bf16[8,88,640]{2,1,0:T(8,128)(2,1)}), bf16[8,88,640]{2,1,0:T(8,128)(2,1)S(1)}, u32[]{:S(2)}, u32[]{:S(2)}) async-start(bf16[8,88,640]{2,1,0:T(8,128)(2,1)} %get-tuple-element.186), calls=%async_computation.7 | async-start | bytes 1802240 | tf_op jit(solution)/shard_map/all_to_all | solution.py:92
  274.1 24.3 %collective-permute-start.50 = (bf16[8,32,1024]{2,1,0:T(8,128)(2,1)S(1)}, bf16[8,32,1024]{2,1,0:T(8,128)(2,1)S(1)}, u32[]{:S(2)}, u32[]{:S(2)}) collective-permute-start(bf16[8,32,1024]{2,1,0:T(8,128)(2,1)S(1)} %copy-done.58), channel_id=1, source_target_pairs={{0,24},{8,16},{16,8},{24,0},{1,25},{9,17},{17,9},{25,1},{2,26},{10... | collective-permute-start | bytes 1572872 | tf_op jit(solution)/shard_map/ppermute | solution.py:88
  275.6 35.2 %collective-permute-start.35 = (bf16[4,128,1024]{2,1,0:T(8,128)(2,1)S(1)}, bf16[4,128,1024]{2,1,0:T(8,128)(2,1)}, u32[]{:S(2)}, u32[]{:S(2)}) collective-permute-start(bf16[4,128,1024]{2,1,0:T(8,128)(2,1)S(1)} %copy-done.9), channel_id=1, source_target_pairs={{0,1},{1,0},{2,3},{3,2},{4,5},{5,4},{6,7},{7,6},{8,9},{9,8},{10,11... | collective-permute-start | bytes 3145736 | tf_op jit(solution)/shard_map/ppermute | solution.py:88
  301.9 49.5 %all-to-all-start.5 = ((bf16[8,32,1024]{2,1,0:T(8,128)(2,1)}), bf16[8,32,1024]{2,1,0:T(8,128)(2,1)S(1)}, u32[]{:S(2)}, u32[]{:S(2)}) async-start(bf16[8,32,1024]{2,1,0:T(8,128)(2,1)} %rep_sum.3), calls=%async_computation.5 | async-start | bytes 1048576 | tf_op jit(solution)/shard_map/all_to_all | solution.py:92
  307.3 28.7 %collective-permute-start.40 = (bf16[128,1024]{1,0:T(8,128)(2,1)}, bf16[128,1024]{1,0:T(8,128)(2,1)S(1)}, u32[]{:S(2)}, u32[]{:S(2)}) collective-permute-start(bf16[128,1024]{1,0:T(8,128)(2,1)} %get-tuple-element.169), channel_id=1, source_target_pairs={{0,4},{1,5},{2,6},{3,7},{4,0},{5,1},{6,2},{7,3},{8,12},{9,13},{10,... | collective-permute-start | bytes 786440 | tf_op jit(solution)/shard_map/ppermute | solution.py:88
  310.2 33.4 %collective-permute-start.41 = (bf16[128,1024]{1,0:T(8,128)(2,1)}, bf16[128,1024]{1,0:T(8,128)(2,1)S(1)}, u32[]{:S(2)}, u32[]{:S(2)}) collective-permute-start(bf16[128,1024]{1,0:T(8,128)(2,1)} %get-tuple-element.170), channel_id=1, source_target_pairs={{0,6},{1,7},{2,4},{3,5},{4,2},{5,3},{6,0},{7,1},{8,14},{9,15},{10,... | collective-permute-start | bytes 786440 | tf_op jit(solution)/shard_map/ppermute | solution.py:88
  313.4 34.3 %collective-permute-start.36 = (bf16[128,1024]{1,0:T(8,128)(2,1)}, bf16[128,1024]{1,0:T(8,128)(2,1)S(1)}, u32[]{:S(2)}, u32[]{:S(2)}) collective-permute-start(bf16[128,1024]{1,0:T(8,128)(2,1)} %get-tuple-element.165), channel_id=1, source_target_pairs={{0,8},{8,0},{16,24},{24,16},{1,9},{9,1},{17,25},{25,17},{2,10},{10... | collective-permute-start | bytes 786440 | tf_op jit(solution)/shard_map/ppermute | solution.py:88
  315.0 34.2 %collective-permute-start.37 = (bf16[128,1024]{1,0:T(8,128)(2,1)}, bf16[128,1024]{1,0:T(8,128)(2,1)S(1)}, u32[]{:S(2)}, u32[]{:S(2)}) collective-permute-start(bf16[128,1024]{1,0:T(8,128)(2,1)} %get-tuple-element.166), channel_id=1, source_target_pairs={{0,16},{8,24},{16,0},{24,8},{1,17},{9,25},{17,1},{25,9},{2,18},{10... | collective-permute-start | bytes 786440 | tf_op jit(solution)/shard_map/ppermute | solution.py:88
  325.9 23.9 %collective-permute-start.38 = (bf16[128,1024]{1,0:T(8,128)(2,1)}, bf16[128,1024]{1,0:T(8,128)(2,1)S(1)}, u32[]{:S(2)}, u32[]{:S(2)}) collective-permute-start(bf16[128,1024]{1,0:T(8,128)(2,1)} %get-tuple-element.167), channel_id=1, source_target_pairs={{0,24},{8,16},{16,8},{24,0},{1,25},{9,17},{17,9},{25,1},{2,26},{10... | collective-permute-start | bytes 786440 | tf_op jit(solution)/shard_map/ppermute | solution.py:88
  347.7 51.2 %collective-permute-start.54 = (bf16[2,184,640]{2,1,0:T(8,128)(2,1)}, bf16[2,184,640]{2,1,0:T(8,128)(2,1)S(1)}, u32[]{:S(2)}, u32[]{:S(2)}) collective-permute-start(bf16[2,184,640]{2,1,0:T(8,128)(2,1)} %core_sums.1.r_1_), channel_id=1, source_target_pairs={{0,8},{8,0},{16,24},{24,16},{1,9},{9,1},{17,25},{25,17},{2,10},{10... | collective-permute-start | bytes 1413128 | tf_op jit(solution)/shard_map/ppermute | solution.py:88
  349.2 49.7 %collective-permute-start.55 = (bf16[2,184,640]{2,1,0:T(8,128)(2,1)}, bf16[2,184,640]{2,1,0:T(8,128)(2,1)S(1)}, u32[]{:S(2)}, u32[]{:S(2)}) collective-permute-start(bf16[2,184,640]{2,1,0:T(8,128)(2,1)} %core_sums.1.r_1_), channel_id=1, source_target_pairs={{0,16},{8,24},{16,0},{24,8},{1,17},{9,25},{17,1},{25,9},{2,18},{10... | collective-permute-start | bytes 1413128 | tf_op jit(solution)/shard_map/ppermute | solution.py:88
  349.9 49.1 %collective-permute-start.56 = (bf16[2,184,640]{2,1,0:T(8,128)(2,1)}, bf16[2,184,640]{2,1,0:T(8,128)(2,1)S(1)}, u32[]{:S(2)}, u32[]{:S(2)}) collective-permute-start(bf16[2,184,640]{2,1,0:T(8,128)(2,1)} %core_sums.1.r_1_), channel_id=1, source_target_pairs={{0,24},{8,16},{16,8},{24,0},{1,25},{9,17},{17,9},{25,1},{2,26},{10... | collective-permute-start | bytes 1413128 | tf_op jit(solution)/shard_map/ppermute | solution.py:88
  353.9 21.0 %collective-permute-start.47 = (bf16[8,32,384]{2,1,0:T(8,128)(2,1)S(1)}, bf16[8,32,384]{2,1,0:T(8,128)(2,1)S(1)}, u32[]{:S(2)}, u32[]{:S(2)}) collective-permute-start(bf16[8,32,384]{2,1,0:T(8,128)(2,1)S(1)} %copy-done.12), channel_id=1, source_target_pairs={{0,24},{8,16},{16,8},{24,0},{1,25},{9,17},{17,9},{25,1},{2,26},{10... | collective-permute-start | bytes 589832 | tf_op jit(solution)/shard_map/ppermute | solution.py:88
  355.4 21.1 %collective-permute-start.51 = (bf16[32,1024]{1,0:T(8,128)(2,1)}, bf16[32,1024]{1,0:T(8,128)(2,1)S(1)}, u32[]{:S(2)}, u32[]{:S(2)}) collective-permute-start(bf16[32,1024]{1,0:T(8,128)(2,1)} %owner_sum.1.r_1_), channel_id=1, source_target_pairs={{0,8},{8,0},{16,24},{24,16},{1,9},{9,1},{17,25},{25,17},{2,10},{10... | collective-permute-start | bytes 196616 | tf_op jit(solution)/shard_map/ppermute | solution.py:88
  374.9 20.8 %collective-permute-start.52 = (bf16[32,1024]{1,0:T(8,128)(2,1)}, bf16[32,1024]{1,0:T(8,128)(2,1)S(1)}, u32[]{:S(2)}, u32[]{:S(2)}) collective-permute-start(bf16[32,1024]{1,0:T(8,128)(2,1)} %owner_sum.1.r_1_), channel_id=1, source_target_pairs={{0,16},{8,24},{16,0},{24,8},{1,17},{9,25},{17,1},{25,9},{2,18},{10... | collective-permute-start | bytes 196616 | tf_op jit(solution)/shard_map/ppermute | solution.py:88
  376.5 19.3 %collective-permute-start.53 = (bf16[32,1024]{1,0:T(8,128)(2,1)}, bf16[32,1024]{1,0:T(8,128)(2,1)S(1)}, u32[]{:S(2)}, u32[]{:S(2)}) collective-permute-start(bf16[32,1024]{1,0:T(8,128)(2,1)} %owner_sum.1.r_1_), channel_id=1, source_target_pairs={{0,24},{8,16},{16,8},{24,0},{1,25},{9,17},{17,9},{25,1},{2,26},{10... | collective-permute-start | bytes 196616 | tf_op jit(solution)/shard_map/ppermute | solution.py:88
  (102 other events, 1128.7 us)

commit v3 on v2

--- a/solution.py
+++ b/solution.py
@@ -100,8 +100,20 @@
     return [blocks[0]] + [swap(block, axis, i * step) for i, block in enumerate(blocks) if i]
 
 
+def exchange_z(blocks):
+    groups = [list(range(core, lax.axis_size("shard"), 2)) for core in range(2)]
+    return lax.all_to_all(
+        blocks, "shard", split_axis=0, concat_axis=0, axis_index_groups=groups, tiled=True
+    )
+
+
 def after(value, *earlier):
     return lax.optimization_barrier((value,) + earlier)[0]
+
+
+def later(values, *earlier):
+    values = tuple(values)
+    return list(lax.optimization_barrier(values + earlier)[: len(values)])
 
 
 def both_cores(parts):
@@ -132,6 +144,10 @@
     return jnp.concatenate(parts, axis=1)
 
 
+def widened(values, times):
+    return jnp.concatenate([values] * times, axis=1)
+
+
 def head_of(values, h, heads):
     if heads == 1:
         return values
@@ -150,7 +166,7 @@
 
 
 def blocks_kernel(n, in_ref, *out_refs):
-    values = to_blocks(in_ref[...].astype(F32), n, out_refs[0].shape[1]).astype(BF16)
+    values = to_blocks(in_ref[...].astype(F32).T, n, out_refs[0].shape[1]).astype(BF16)
     out_refs[0][...] = values
     for ref in out_refs[1:]:
         for i in range(ref.shape[0]):
@@ -166,7 +182,7 @@
     heads = head_cols // HD
     row = lax.broadcasted_iota(jnp.int32, (piece, own), 0) + rep_ref[0] * piece
     pick = jnp.where(row == lax.broadcasted_iota(jnp.int32, (piece, own), 1), 1.0, 0.0).astype(BF16)
-    query, key, value = (dot(pick, ref[...]) for ref in (q_ref, k_ref, v_ref))
+    query, key, value = dot(pick, q_ref[...]), contract_cols(pick, k_ref[...]), contract_cols(pick, v_ref[...])
     gap = jnp.zeros((piece, HD), F32)
     wide = lax.broadcasted_iota(jnp.int32, (piece, cols), 0) + rep_ref[0] * piece
     for s in range(n):
@@ -183,6 +199,10 @@
     rows = to_blocks(dot(pick, out_ref[...]), n, 2 * half).astype(BF16)
     for s in range(n):
         msg_ref[s, :, cols:] = rows[:, s % 2 * half : (s % 2 + 1) * half]
+
+
+def as_row(column):
+    return jnp.broadcast_to(column, (column.shape[0], 128)).T[0:1, :]
 
 
 def join_kernel(reps, rep_ref, *refs):
@@ -290,6 +310,7 @@
 def attend_kernel(rows, n, me_ref, mine_ref, other_ref, *refs):
     w_ref, cos_ref, sin_ref, start_ref, first_ref, q_ref, k_ref, v_ref, gains_ref = refs[:9]
     part_refs, mixed_ref = refs[9:-1], refs[-1]
+    core = me_ref[0] % 2
     length, head_cols = q_ref.shape
     heads = head_cols // HD
     width = first_ref.shape[1]
@@ -310,12 +331,12 @@
         for z in range(n // 2):
             inputs = ref[z].astype(F32)
             normed = inputs * inverse_rms(inputs) * gains[0]
-            first_ref[rows_at(me_ref[0] ^ (2 * z + side), rows), :] = normed.astype(BF16)
+            first_ref[rows_at(2 * z + (core ^ side), rows), :] = normed.astype(BF16)
     block = min(256, length)
     for i in range(length // block):
         span = pl.ds(i * block, block)
         raw = dot(first_ref[span, :], w_ref[...])
-        cosines, sines = cos_ref[span, :], sin_ref[span, :]
+        cosines, sines = widened(cos_ref[span, :], 2 * heads), widened(sin_ref[span, :], 2 * heads)
         query, key = raw[:, :head_cols], raw[:, head_cols : 2 * head_cols]
         q_ref[span, :] = (query * cosines + turned(query) * sines).astype(BF16)
         k_ref[span, :] = (key * cosines + turned(key) * sines).astype(BF16)
@@ -361,12 +382,14 @@
             dv_ref[past, :] += contract_rows(probs.astype(BF16), grad)
             dk_ref[past, :] += contract_rows(grad_logits, query)
         total = total * SCALE
-        back = total * cos_ref[span, :] - turned(total) * sin_ref[span, :]
+        cosines, sines = widened(cos_ref[span, :], 2 * heads), widened(sin_ref[span, :], 2 * heads)
+        back = total * cosines - turned(total) * sines
         dqkv_ref[span, :head_cols] = back.astype(BF16)
     for i in range(length // block):
         span = pl.ds(i * block, block)
         total = dk_ref[span, :] * SCALE
-        back = total * cos_ref[span, :] - turned(total) * sin_ref[span, :]
+        cosines, sines = widened(cos_ref[span, :], 2 * heads), widened(sin_ref[span, :], 2 * heads)
+        back = total * cosines - turned(total) * sines
         dqkv_ref[span, head_cols : 2 * head_cols] = back.astype(BF16)
         dqkv_ref[span, 2 * head_cols :] = dv_ref[span, :].astype(BF16)
     store_pieces(rep_ref, piece_refs, hold_ref, contract_rows(first_ref[...], dqkv_ref[...]))
@@ -413,15 +436,14 @@
     return jnp.concatenate([ref[begin + i] for i in range(count)], axis=0)
 
 
-def hidden_kernel(rep_ref, second_ref, cot_ref, w_ref, down_ref, grad_ref, grads_ref, hidden_ref):
+def hidden_kernel(second_ref, cot_ref, w_ref, down_ref, grad_ref, grads_ref, hidden_ref):
     reps, rows, _ = second_ref.shape
     units = down_ref.shape[0]
     for i in range(0, reps, 2):
         span = pl.ds(i * rows, 2 * rows)
         both = dot(stacked(second_ref, i, 2), w_ref[...])
         gate, up = both[:, :units], both[:, units:]
-        cots = jnp.concatenate([cot_ref[rep_ref[0] ^ (i + j)] for j in range(2)], axis=0)
-        grad_hidden = contract_cols(cots, down_ref[...])
+        grad_hidden = contract_cols(stacked(cot_ref, i, 2), down_ref[...])
         sigmoid = 1.0 / (1.0 + jnp.exp(-gate))
         silu = gate * sigmoid
         hidden_ref[span, :] = (silu * up).astype(BF16)
@@ -433,15 +455,12 @@
             grad_ref[i + j] = grad[j * rows : (j + 1) * rows]
 
 
-def hidden_weights_kernel(n, own, each, rep_ref, *refs):
+def hidden_weights_kernel(n, own, each, *refs):
     second_a, second_b, cot_a, cot_b, grads_a, grads_b, hidden_a, hidden_b, *msg_refs = refs
     cols = msg_refs[0].shape[2]
     grad = contract_rows(stacked(second_a), grads_a[...])
     grad = grad + contract_rows(stacked(second_b), grads_b[...])
-    cots = [
-        jnp.concatenate([ref[rep_ref[0] ^ i] for i in range(ref.shape[0])], axis=0) for ref in (cot_a, cot_b)
-    ]
-    down = contract_rows(hidden_a[...], cots[0]) + contract_rows(hidden_b[...], cots[1])
+    down = contract_rows(hidden_a[...], stacked(cot_a)) + contract_rows(hidden_b[...], stacked(cot_b))
     down = from_blocks(down, n, own)
     block = grad.shape[0] // n
     for s in range(n):
@@ -465,12 +484,11 @@
     own = gate_ref.shape[0]
     units = 2 * reps * each
     for i, part in enumerate(parts):
-        for core in range(2):
-            hold_ref[2 * (rep_ref[0] ^ i) + core] = part[core]
-    cols = hold_ref.shape[2]
+        hold_ref[rep_ref[0] ^ i] = part[...]
+    cols = hold_ref.shape[3]
     boths = []
     for f in range(2 * reps):
-        both, down = unpack_message(hold_ref[f].astype(F32), own, each)
+        both, down = unpack_message(hold_ref[f // 2, f % 2].astype(F32), own, each)
         boths.append(both)
         down_ref[f * each : (f + 1) * each, :] = down
     total = jnp.zeros((own, 1), F32)
@@ -481,7 +499,7 @@
             span = slice(s * units, (s + 1) * units)
             out_ref[:, span] = rows
             total = total + jnp.sum(rows * w_ref[:, span].astype(F32), axis=1, keepdims=True)
-    norm_ref[...] = total / gain_ref[...]
+    norm_ref[...] = as_row(total) / gain_ref[...]
 
 
 def down_kernel(hidden_ref, w_ref, out_ref):
@@ -496,7 +514,7 @@
     total = middle_ref[...]
     for ref in refs[:-1]:
         total = total + ref[...].astype(F32)
-    refs[-1][...] = from_blocks(total, n, own).astype(BF16)
+    refs[-1][...] = from_blocks(total, n, own).T.astype(BF16)
 
 
 def middle_grad_kernel(n, own, reps, me_ref, *refs):
@@ -565,12 +583,13 @@
     query = jnp.concatenate([slot(h, 0) for h in range(QH)], axis=1)
     q_ref[...] = query
     total = jnp.sum(query * q_w_ref[...].astype(F32), axis=1, keepdims=True)
+    total = as_row(total)
     for kind, w_ref, out_ref in ((1, k_w_ref, k_ref), (2, v_w_ref, v_ref)):
         wide = jnp.concatenate(
             [sum(slot(j * GROUP + g, kind) for g in range(GROUP)) for j in range(KVH)], axis=1
-        )
+        ).T
         out_ref[...] = wide
-        total = total + jnp.sum(wide * w_ref[...].astype(F32), axis=1, keepdims=True)
+        total = total + jnp.sum(wide * w_ref[...].astype(F32), axis=0, keepdims=True)
     norm_ref[...] = total / gain_ref[...]
 
 
@@ -579,7 +598,7 @@
     inputs = tokens_ref[...].astype(F32)
     grad_first = sum(ref[...].astype(F32) for ref in parts)
     total = grad_ref[...] + norm_backward(inputs, inverse_rms(inputs), gains_ref[0:1, :], grad_first)
-    out_ref[...] = from_blocks(total, n, own)
+    out_ref[...] = from_blocks(total, n, own).T
 
 
 def shards(
@@ -618,16 +637,20 @@
     rep = lax.axis_index("rep").astype(jnp.int32).reshape(1)
     own_block = (rows, width)
 
-    (tokens_in,) = call(lambda *r: blocks_kernel(n, *r), "tokens_blocks", [(own_block, BF16)], tokens)
-    tokens_mine, tokens_other = both_cores(spread(tokens_in, "shard", 2))
+    tokens_in, tokens_tiled = call(
+        lambda *r: blocks_kernel(n, *r),
+        "tokens_blocks",
+        [(own_block, BF16), ((nz,) + own_block, BF16)],
+        tokens.T,
+    )
     gains_own = jnp.pad(jnp.stack([norm_one, norm_two]), ((0, 0), (0, qkv_cols - own))).astype(F32)
     (message,) = call(
         lambda *r: attention_message_kernel(n, *r),
         "attention_message",
         [((n, piece, qkv_cols + width // 2), BF16)],
         after(w_query, tokens_in),
-        w_key,
-        w_value,
+        w_key.T,
+        w_value.T,
         w_out,
         gains_own,
         scalars=(rep,),
@@ -641,13 +664,15 @@
         scalars=(rep,),
     )
     w_qkv = w_qkv.reshape(width, qkv_cols)
-    cot_in, cot_tiled = call(
-        lambda *r: blocks_kernel(n, *r),
-        "cot_blocks",
-        [(own_block, BF16), ((reps,) + own_block, BF16)],
-        after(cotangent, message),
-    )
-    cot_mine = lax.all_to_all(after(cot_tiled, arrived), "rep", split_axis=0, concat_axis=0, tiled=True)
+    tokens_mine = exchange_z(after(tokens_tiled, arrived))
+    tokens_other = swap(tokens_mine, "shard", 1)
+    (cot_in,) = call(
+        lambda *r: blocks_kernel(n, *r), "cot_blocks", [(own_block, BF16)], after(cotangent.T, message)
+    )
+    cot_parts = spread(after(cot_in, w_qkv), "rep", 1)
+    doc_start, position = doc_layout(after(lengths, cot_in)[0], length)
+    cosines, sines = rope_tables(position)
+    start = doc_start[:, None]
 
     split = msg_rows // 2 // 16 * 16 + 16
     part_rows = (split, msg_rows - split) if split < msg_rows else (msg_rows,)
@@ -655,20 +680,15 @@
         lambda *r: hidden_message_kernel(n, reps, *r),
         "hidden_message",
         [((n, part, 2 * units), BF16) for part in part_rows],
-        after(w_gate, cot_in),
+        after(w_gate, cosines, sines, start),
         w_up,
         w_down,
         scalars=(rep,),
     )
-    hidden_first = exchange(after(messages[0], tokens_mine, cot_mine))
-
-    out_mine, out_other = both_cores(spread(after(arrived, w_qkv)[:, :, qkv_cols:], "rep", 1))
-
-    doc_start, position = doc_layout(lengths[0], length)
-    cosines, sines = rope_tables(position)
-    cosines = jnp.tile(cosines, (1, 2 * heads))
-    sines = jnp.tile(sines, (1, 2 * heads))
-    start = doc_start[:, None]
+    hidden_first = exchange(after(messages[0], tokens_mine))
+
+    out_parts = spread(after(arrived, w_qkv)[:, :, qkv_cols:], "rep", 1)
+
     head_shape = (length, head_cols)
     first_all, query, key, value, gains, *mixed = call(
         lambda *r: attend_kernel(rows, n, *r),
@@ -682,18 +702,17 @@
         w_qkv,
         cosines,
         sines,
-        start,
+        after(start, messages[0]),
         scalars=(me,),
         scratch=[(head_shape, BF16)],
     )
-    mixed = deliver([after(mixed[0], hidden_first)] + mixed[1:], "shard", 1)
+    mixed = deliver(later(mixed, hidden_first), "shard", 1)
     hidden_rest = [exchange(after(message, *mixed)) for message in messages[1:]]
     (out_full,) = call(
         lambda *r: join_out_kernel(reps, *r),
         "join_out",
         [((n, reps, piece, width), BF16)],
-        after(out_mine, gains),
-        out_other,
+        *both_cores([after(out_parts[0], gains)] + out_parts[1:]),
         scalars=(rep, core),
     )
     out_full = out_full.reshape(width, width)
@@ -717,7 +736,7 @@
         *hidden_rest,
     )
     w_hidden = w_hidden.reshape(width, 2 * units)
-    cot_other = swap(cot_mine, "shard", 1)
+    cot_mine, cot_other = both_cores([after(cot_parts[0], out_full)] + cot_parts[1:])
 
     second_mine, second_other = both_cores(spread(second, "rep", 1))
     side_outs = [
@@ -727,7 +746,7 @@
     ]
 
     def hidden_side(seconds, cots, name):
-        return call(hidden_kernel, name, side_outs, seconds, cots, w_hidden, w_down_in, scalars=(rep,))
+        return call(hidden_kernel, name, side_outs, seconds, cots, w_hidden, w_down_in)
 
     def plane_sums(mine, other):
         sums = call(pair_sum_kernel, "pair_sum", [(own_block, BF16)] * reps, mine, swap(other, "shard", 1))
@@ -750,9 +769,18 @@
         grads_other,
         after(hidden_mine, sums[0]),
         hidden_other,
-        scalars=(rep,),
     )
     hidden_sums = [exchange(hidden_messages[0])]
+    down_other, down_mine = [
+        call(
+            down_kernel,
+            "down",
+            [((reps, rows, width), BF16)],
+            after(hidden, hidden_messages[0]),
+            w_down_in,
+        )[0]
+        for hidden in (hidden_other, hidden_mine)
+    ]
 
     grad_middle, grad_branch, *grad_heads = call(
         lambda *r: middle_grad_kernel(n, own, reps, *r),
@@ -760,28 +788,24 @@
         [(own_block, F32), (own_block, BF16)] + [((rows, head_cols), BF16)] * n,
         *grad_second,
         cot_in,
-        after(middle, hidden_messages[0]),
+        after(middle, down_other, down_mine),
         gains,
         out_full,
         scalars=(me,),
         scratch=[((n, rows, head_cols), BF16)],
     )
     grad_heads = deliver(grad_heads, "shard", 1)
+    down_sums, down_parts = plane_sums(after(down_mine, grad_branch), down_other)
     hidden_sums += [exchange(after(message, *grad_heads)) for message in hidden_messages[1:]]
     out_pieces = call(
         out_weights_kernel,
         "out_weights",
         [((n, piece, width), BF16)] * reps,
         attended,
-        grad_branch,
+        after(grad_branch, down_sums[0]),
         scalars=(rep,),
         scratch=[((n, reps, piece, width), BF16)],
     )
-    down_other, down_mine = [
-        call(down_kernel, "down", [((reps, rows, width), BF16)], after(hidden, out_pieces[0]), w_down_in)[0]
-        for hidden in (hidden_other, hidden_mine)
-    ]
-
     grad_qkv, *attention_pieces = call(
         lambda *r: attend_back_kernel(n, reps, *r),
         "attend_back",
@@ -793,10 +817,19 @@
         value,
         cosines,
         sines,
-        after(start, down_mine, down_other),
+        after(start, out_pieces[0], hidden_sums[0]),
         scalars=(rep, me),
         scratch=[(head_shape, BF16)] + [(head_shape, F32)] * 2 + [((n, reps, piece, qkv_cols), BF16)],
     )
+
+    def rep_sum(parts, *earlier):
+        return call(
+            lambda *r: rep_sum_kernel(reps, *r),
+            "rep_sum",
+            [(parts[0].shape, BF16)],
+            after(parts[0], *earlier),
+            *parts[1:],
+        )[0]
 
     def first_side(grads, side):
         return call(
@@ -810,44 +843,71 @@
 
     first_other = first_side(grad_qkv, 1)
     first_mine = first_side(after(grad_qkv, first_other), 0)
+    (output,) = call(
+        lambda *r: output_kernel(n, own, *r),
+        "output",
+        [((D, rows), BF16)],
+        after(middle, first_mine),
+        *down_parts,
+    )
+    out_summed = rep_sum(deliver(out_pieces, "rep", 1), output)
+    attention_summed = rep_sum(deliver(attention_pieces, "rep", 1), out_summed)
     first_sums = call(
-        pair_sum_kernel, "pair_sum", [(own_block, BF16)] * nz, first_mine, swap(first_other, "shard", 1)
+        pair_sum_kernel,
+        "pair_sum",
+        [(own_block, BF16)] * nz,
+        after(first_mine, attention_summed, *hidden_sums),
+        swap(first_other, "shard", 1),
     )
     first_parts = deliver(first_sums, "shard", 2)
+    attention_moved = exchange(after(attention_summed, *hidden_sums))
+    (core_sums,) = call(
+        core_sums_kernel,
+        "core_sums",
+        [((2, msg_rows, 2 * units), BF16)],
+        after(hidden_sums[0], first_sums[0]),
+        *hidden_sums[1:],
+    )
+    out_moved = exchange(after(out_summed, attention_moved))
+
+    gain_rows = [gain.astype(F32)[None] for gain in (norm_one, norm_two)]
     (input_grad,) = call(
         lambda *r: input_grad_kernel(n, own, nz, *r),
         "input_grad",
-        [((rows, D), F32)],
+        [((D, rows), F32)],
         *first_parts,
         tokens_in,
         gains,
         grad_middle,
     )
 
-    def owner_pieces(pieces, *earlier):
-        parts = deliver(pieces, "rep", 1)
-        parts[0] = after(parts[0], *earlier)
-        (summed,) = call(
-            lambda *r: rep_sum_kernel(reps, *r), "rep_sum", [(pieces[0].shape, BF16)], *parts
-        )
-        return exchange(summed)
-
-    gain_cols = [gain.astype(F32)[:, None] for gain in (norm_one, norm_two)]
-    attention_parts = spread(owner_pieces(attention_pieces, first_sums[0]), "rep", 1)
+    grad_w_gate, grad_w_up, grad_w_down, grad_norm_two = call(
+        lambda *r: hidden_out_kernel(n, reps, each, *r),
+        "hidden_out",
+        [(w_gate.shape, F32), (w_up.shape, F32), (w_down.shape, F32), ((1, own), F32)],
+        *spread(core_sums, "rep", 1),
+        w_gate,
+        w_up,
+        after(gain_rows[1], input_grad),
+        scalars=(rep,),
+        scratch=[((reps, 2, msg_rows, 2 * units), BF16)],
+    )
+
+    attention_parts = spread(attention_moved, "rep", 1)
     grad_w_query, grad_w_key, grad_w_value, grad_norm_one = call(
         lambda *r: attention_out_kernel(n, reps, *r),
         "attention_out",
-        [(w_query.shape, F32), (w_key.shape, F32), (w_value.shape, F32), ((own, 1), F32)],
+        [(w_query.shape, F32), (w_key.shape[::-1], F32), (w_value.shape[::-1], F32), ((1, own), F32)],
         *attention_parts,
-        w_query,
-        w_key,
-        w_value,
-        gain_cols[0],
+        after(w_query, grad_norm_two),
+        w_key.T,
+        w_value.T,
+        gain_rows[0],
         scalars=(rep,),
         scratch=[((reps, n, piece, qkv_cols), F32)],
     )
 
-    (out_piece,) = call(owner_sum_kernel, "owner_sum", [((piece, width), BF16)], owner_pieces(out_pieces, first_sums[0]))
+    (out_piece,) = call(owner_sum_kernel, "owner_sum", [((piece, width), BF16)], after(out_moved, input_grad))
     (grad_w_out,) = call(
         lambda *r: out_out_kernel(n, reps, *r),
         "out_out",
@@ -857,35 +917,15 @@
         scratch=[((reps, piece, width), F32)],
     )
 
-    (core_sums,) = call(core_sums_kernel, "core_sums", [((2, msg_rows, 2 * units), BF16)], *hidden_sums)
-    grad_w_gate, grad_w_up, grad_w_down, grad_norm_two = call(
-        lambda *r: hidden_out_kernel(n, reps, each, *r),
-        "hidden_out",
-        [(w_gate.shape, F32), (w_up.shape, F32), (w_down.shape, F32), ((own, 1), F32)],
-        *spread(core_sums, "rep", 1),
-        w_gate,
-        w_up,
-        gain_cols[1],
-        scalars=(rep,),
-        scratch=[((2 * reps, msg_rows, 2 * units), BF16)],
-    )
-
-    (output,) = call(
-        lambda *r: output_kernel(n, own, *r),
-        "output",
-        [((rows, D), BF16)],
-        middle,
-        *plane_sums(after(down_mine, first_sums[0]), down_other)[1],
-    )
     return (
-        output,
-        input_grad,
-        grad_norm_one[:, 0],
+        output.T,
+        input_grad.T,
+        grad_norm_one[0],
         grad_w_query,
-        grad_w_key,
-        grad_w_value,
+        grad_w_key.T,
+        grad_w_value.T,
         grad_w_out,
-        grad_norm_two[:, 0],
+        grad_norm_two[0],
         grad_w_gate,
         grad_w_up,
         grad_w_down,

time: 415 us -> 361 us (0.87)
  waiting for transfers between devices: 145 us -> 84.6 us
  local copies, waits for them, and re-layouts: 33.8 us -> 17.4 us
  blocking collectives: 13.7 us -> 29.1 us
    ppermute x57, waiting for transfers between devices: 115 us -> 64.4 us  [swap(): return lax.ppermute(block, axis, [(i, i ^ k) for i in range(count)])]
    all_to_all x6 -> x5, waiting for transfers between devices: 29.7 us -> 0.01 us  [exchange(): lax.all_to_all(block, 'shard', split_axis=0, concat_axis=0, tiled=True)]
    all_to_all x1, waiting for transfers between devices: 0.01 us -> 20.2 us  [exchange_z(): lax.all_to_all(blocks, 'shard', split_axis=0, concat_axis=0, axis_index_g...]
    all_to_all x1 -> x2, blocking collectives: 13.7 us -> 29.1 us  [exchange(): lax.all_to_all(block, 'shard', split_axis=0, concat_axis=0, tiled=True)]
    unnamed x131 -> x140, local copies, waits for them, and re-layouts: 23.4 us -> 14.6 us
    another operation x5 -> x0, local copies, waits for them, and re-layouts: 5.92 us -> none  [the longest x2 2.94 us: shards(): sines = jnp.tile(sines, (1, 2 * heads))]
    all_to_all x6 -> x5, starting transfers between devices: 32.5 us -> 30.7 us  [exchange(): lax.all_to_all(block, 'shard', split_axis=0, concat_axis=0, tiled=True)]
  transfers between devices with their start and end apart: 64 -> 63, of which waited for: 25 -> 18; matrix products, arithmetic and copies ran while one was open for 5% -> 3% of each run, Pallas kernels for 18% -> 27%
where the time goes in v3:
time: 361 us; the launch traced here: 356 us
  Pallas kernels  117 us (32%)
  starting transfers between devices  97.8 us (27%)
  waiting for transfers between devices  84.6 us (23%)
  blocking collectives  29.1 us (8%)
  local copies, waits for them, and re-layouts  17.4 us (5%)
  other arithmetic  8.42 us (2%)
    pallas_call x31, Pallas kernels, call(): pl.pallas_call(kernel, out_shape=[jax.ShapeDtypeStruct(shape, dtype) for...  117 us
    ppermute x57, waiting for transfers between devices, swap(): return lax.ppermute(block, axis, [(i, i ^ k) for i in range(count)])  64.4 us
    ppermute x57, starting transfers between devices, swap(): return lax.ppermute(block, axis, [(i, i ^ k) for i in range(count)])  61.4 us
    all_to_all x5, starting transfers between devices, exchange(): lax.all_to_all(block, 'shard', split_axis=0, concat_axis=0, tiled=True)  30.7 us
    all_to_all x2, blocking collectives, exchange(): lax.all_to_all(block, 'shard', split_axis=0, concat_axis=0, tiled=True)  29.1 us
    all_to_all x1, waiting for transfers between devices, exchange_z(): lax.all_to_all(blocks, 'shard', split_axis=0, concat_axis=0, axis_index_g...  20.2 us
    unnamed x140, local copies, waits for them, and re-layouts  14.6 us
  transfers between devices with their start and end apart: 63, of which 18 were waited for; matrix products, arithmetic and copies ran while one was open for 3% of the time, Pallas kernels for 27%

profile of v3, /device:TPU:10, one launch (start us, length us, event | category | flops | bytes accessed | tf_op | source)
XLA Modules:
  0.0 355.8 jit_solution(16455141468849768153)
XLA Ops:
  6.6 17.2 %all_to_all.40 = bf16[8,32,896]{2,1,0:T(8,128)(2,1)S(1)} all-to-all(bf16[8,32,896]{2,1,0:T(8,128)(2,1)} %attention_message.1), channel_id=1, replica_groups=mesh['rep'=4,'shard'=8] {'shard'}, dimensions={0} | all-to-all | bytes 917504 | tf_op jit(solution)/shard_map/all_to_all | solution.py:92
  23.8 5.7 %all-to-all-start.1 = ((bf16[4,128,1024]{2,1,0:T(8,128)(2,1)}), bf16[4,128,1024]{2,1,0:T(8,128)(2,1)S(1)}, u32[]{:S(2)}, u32[]{:S(2)}) async-start(bf16[4,128,1024]{2,1,0:T(8,128)(2,1)} %get-tuple-element.124), calls=%async_computation.1 | async-start | bytes 2097152 | tf_op jit(solution)/shard_map/all_to_all | solution.py:105
  31.7 20.2 %all-to-all-done.1.r_1_ = bf16[4,128,1024]{2,1,0:T(8,128)(2,1)S(1)} async-done(((bf16[4,128,1024]{2,1,0:T(8,128)(2,1)}), bf16[4,128,1024]{2,1,0:T(8,128)(2,1)S(1)}, u32[]{:S(2)}, u32[]{:S(2)}) %all-to-all-start.1) | async-done | bytes 1048608 | tf_op jit(solution)/shard_map/all_to_all | solution.py:105
  55.0 5.0 %hidden_message.1 = (bf16[8,96,640]{2,1,0:T(8,128)(2,1)}, bf16[8,88,640]{2,1,0:T(8,128)(2,1)}) custom-call(s32[1]{0:T(128)} %bitcast.2.r_0_.rep_ref, bf16[120,2560]{1,0:T(8,128)(2,1)} %r_5_.1, bf16[120,2560]{1,0:T(8,128)(2,1)} %r_6_.1, bf16[320,960]{1,0:T(8,128)(2,1)} %r_3_.1), custom_call_target="tpu_custom_call" | custom-call | tf_op jit(solution)/shard_map/hidden_message/pallas_call | solution.py:127
  60.1 7.0 %all-to-all-start.2 = ((bf16[8,96,640]{2,1,0:T(8,128)(2,1)}), bf16[8,96,640]{2,1,0:T(8,128)(2,1)S(1)}, u32[]{:S(2)}, u32[]{:S(2)}) async-start(bf16[8,96,640]{2,1,0:T(8,128)(2,1)} %get-tuple-element.138), calls=%async_computation.2 | async-start | bytes 1966080 | tf_op jit(solution)/shard_map/all_to_all | solution.py:92
  70.7 4.3 %collective-permute-done.1.r_2_ = bf16[8,32,384]{2,1,0:T(8,128)(2,1)S(1)} collective-permute-done((bf16[8,32,384]{2,1,0:T(8,128)(2,1)S(1)}, bf16[8,32,384]{2,1,0:T(8,128)(2,1)S(1)}, u32[]{:S(2)}, u32[]{:S(2)}) %collective-permute-start.1) | collective-permute-done | bytes 196640 | tf_op jit(solution)/shard_map/ppermute | solution.py:88
  88.4 9.0 %attend.1 = (bf16[1024,1024]{1,0:T(8,128)(2,1)}, bf16[1024,128]{1,0:T(8,128)(2,1)}, bf16[1024,128]{1,0:T(8,128)(2,1)}, bf16[1024,128]{1,0:T(8,128)(2,1)}, f32[2,...) custom-call(s32[1]{0:T(128)} %bitcast.r_0_.r_1_, ...), custom_call_target="tpu_custom_call" | custom-call | tf_op jit(solution)/shard_map/attend/pallas_call | solution.py:127
  115.8 6.4 %all-to-all-start.3 = ((bf16[8,88,640]{2,1,0:T(8,128)(2,1)}), bf16[8,88,640]{2,1,0:T(8,128)(2,1)}, u32[]{:S(2)}, u32[]{:S(2)}) async-start(bf16[8,88,640]{2,1,0:T(8,128)(2,1)} %get-tuple-element.156), calls=%async_computation.3 | async-start | bytes 1802240 | tf_op jit(solution)/shard_map/all_to_all | solution.py:92
  134.2 4.5 %collective-permute-done.15 = bf16[128,1024]{1,0:T(8,128)(2,1)S(1)} collective-permute-done((bf16[128,1024]{1,0:T(8,128)(2,1)}, bf16[128,1024]{1,0:T(8,128)(2,1)S(1)}, u32[]{:S(2)}, u32[]{:S(2)}) %collective-permute-start.15) | collective-permute-done | bytes 262176 | tf_op jit(solution)/shard_map/ppermute | solution.py:88
  138.8 6.0 %collective-permute-done.16 = bf16[128,1024]{1,0:T(8,128)(2,1)S(1)} collective-permute-done((bf16[128,1024]{1,0:T(8,128)(2,1)}, bf16[128,1024]{1,0:T(8,128)(2,1)S(1)}, u32[]{:S(2)}, u32[]{:S(2)}) %collective-permute-start.16) | collective-permute-done | bytes 262176 | tf_op jit(solution)/shard_map/ppermute | solution.py:88
  149.6 5.7 %hidden_other.1 = (bf16[4,128,1024]{2,1,0:T(8,128)(2,1)}, bf16[512,640]{1,0:T(8,128)(2,1)}, bf16[512,320]{1,0:T(8,128)(2,1)}) custom-call(bf16[4,128,1024]{2,1,0:T(8,128)(2,1)} %collective-permute-done.18.second_ref.r_1_, bf16[4,128,1024]{2,1,0:T(8,128)(2,1)} %copy-done.4, bf16[1024,640]{1,0:T(8,128)(2,1)} %bitcast.41, ...), custom_call_target="tpu_custom_call" | custom-call | tf_op jit(solution)/shard_map/hidden_other/pallas_call | solution.py:127
  155.5 5.7 %hidden_mine.1 = (bf16[4,128,1024]{2,1,0:T(8,128)(2,1)}, bf16[512,640]{1,0:T(8,128)(2,1)}, bf16[512,320]{1,0:T(8,128)(2,1)}) custom-call(bf16[4,128,1024]{2,1,0:T(8,128)(2,1)} %copy-done.1, bf16[4,128,1024]{2,1,0:T(8,128)(2,1)} %copy-done, bf16[1024,640]{1,0:T(8,128)(2,1)} %bitcast.42, bf16[320,1024]{1,0:T(8,128)(2,1)} %get-tuple-element.158.down_ref.w_ref), custom_call_target="tpu_custom_call" | custom-call | tf_op jit(solution)/shard_map/hidden_mine/pallas_call | solution.py:127
  164.8 6.6 %hidden_weights.1 = (bf16[8,96,640]{2,1,0:T(8,128)(2,1)}, bf16[8,88,640]{2,1,0:T(8,128)(2,1)}) custom-call(bf16[4,128,1024]{2,1,0:T(8,128)(2,1)} %copy-done.1, bf16[4,128,1024]{2,1,0:T(8,128)(2,1)} %collective-permute-done.18.second_ref.r_1_, bf16[4,128,1024]{2,1,0:T(8,128)(2,1)} %copy-done, bf16[4,128,1024]{2,1,0:T(8,128)(2,1)} %copy-done.4, ...), custom_call_target="tpu_custom_call" | custom-call | tf_op jit(solution)/shard_map/hidden_weights/pallas_call | solution.py:127
  171.4 5.3 %all-to-all-start.4 = ((bf16[8,96,640]{2,1,0:T(8,128)(2,1)}), bf16[8,96,640]{2,1,0:T(8,128)(2,1)S(1)}, u32[]{:S(2)}, u32[]{:S(2)}) async-start(bf16[8,96,640]{2,1,0:T(8,128)(2,1)} %get-tuple-element.171), calls=%async_computation.4 | async-start | bytes 1966080 | tf_op jit(solution)/shard_map/all_to_all | solution.py:92
  186.0 5.0 %collective-permute-done.25.r_3_ = bf16[128,1024]{1,0:T(8,128)(2,1)S(1)} collective-permute-done((bf16[128,1024]{1,0:T(8,128)(2,1)S(1)}, bf16[128,1024]{1,0:T(8,128)(2,1)S(1)}, u32[]{:S(2)}, u32[]{:S(2)}) %collective-permute-start.25) | collective-permute-done | bytes 262176 | tf_op jit(solution)/shard_map/ppermute | solution.py:88
  206.7 7.1 %all-to-all-start.5 = ((bf16[8,88,640]{2,1,0:T(8,128)(2,1)}), bf16[8,88,640]{2,1,0:T(8,128)(2,1)S(1)}, u32[]{:S(2)}, u32[]{:S(2)}) async-start(bf16[8,88,640]{2,1,0:T(8,128)(2,1)} %get-tuple-element.210), calls=%async_computation.5 | async-start | bytes 1802240 | tf_op jit(solution)/shard_map/all_to_all | solution.py:92
  229.3 13.2 %attend_back.1 = (bf16[1024,384]{1,0:T(8,128)(2,1)}, bf16[8,32,384]{2,1,0:T(8,128)(2,1)}, bf16[8,32,384]{2,1,0:T(8,128)(2,1)}, bf16[8,32,384]{2,1,0:T(8,128)(2,1)}, bf16[8,32,384]{2,1,0:T(8,128)(2,1)}) custom-call(s32[1]{0:T(128)} %bitcast.2.r_0_.rep_ref, s32[1]{0:T(128)} %bitcast.r_0_.r_1_, bf16[128,128]{1,0:T(8,128)(2,1)} %get-tuple-element.175.r_2_, ...), custom_call_target="tpu_custom_call" | custom-call | tf_op jit(solution)/shard_map/attend_back/pallas_call | solution.py:127
  246.1 12.8 %collective-permute-done.36.r_3_ = bf16[128,1024]{1,0:T(8,128)(2,1)} collective-permute-done((bf16[128,1024]{1,0:T(8,128)(2,1)}, bf16[128,1024]{1,0:T(8,128)(2,1)}, u32[]{:S(2)}, u32[]{:S(2)}) %collective-permute-start.36) | collective-permute-done | bytes 262176 | tf_op jit(solution)/shard_map/ppermute | solution.py:88
  275.4 11.9 %all_to_all.41.r_1_ = bf16[8,32,384]{2,1,0:T(8,128)(2,1)S(1)} all-to-all(bf16[8,32,384]{2,1,0:T(8,128)(2,1)} %rep_sum.3), channel_id=1, replica_groups=mesh['rep'=4,'shard'=8] {'shard'}, dimensions={0} | all-to-all | bytes 393216 | tf_op jit(solution)/shard_map/all_to_all | solution.py:92
  287.3 5.0 %all-to-all-start.7 = ((bf16[8,32,1024]{2,1,0:T(8,128)(2,1)}), bf16[8,32,1024]{2,1,0:T(8,128)(2,1)S(1)}, u32[]{:S(2)}, u32[]{:S(2)}) async-start(bf16[8,32,1024]{2,1,0:T(8,128)(2,1)} %rep_sum.2), calls=%async_computation.7 | async-start | bytes 1048576 | tf_op jit(solution)/shard_map/all_to_all | solution.py:92
  304.8 6.4 %collective-permute-done.45.r_1_ = bf16[128,1024]{1,0:T(8,128)(2,1)S(1)} collective-permute-done((bf16[128,1024]{1,0:T(8,128)(2,1)}, bf16[128,1024]{1,0:T(8,128)(2,1)S(1)}, u32[]{:S(2)}, u32[]{:S(2)}) %collective-permute-start.45) | collective-permute-done | bytes 262176 | tf_op jit(solution)/shard_map/ppermute | solution.py:88
  311.6 9.5 %collective-permute-done.46.r_2_ = bf16[128,1024]{1,0:T(8,128)(2,1)S(1)} collective-permute-done((bf16[128,1024]{1,0:T(8,128)(2,1)}, bf16[128,1024]{1,0:T(8,128)(2,1)S(1)}, u32[]{:S(2)}, u32[]{:S(2)}) %collective-permute-start.46) | collective-permute-done | bytes 262176 | tf_op jit(solution)/shard_map/ppermute | solution.py:88
  323.1 5.6 %collective-permute-done.47.r_3_ = bf16[128,1024]{1,0:T(8,128)(2,1)S(1)} collective-permute-done((bf16[128,1024]{1,0:T(8,128)(2,1)S(1)}, bf16[128,1024]{1,0:T(8,128)(2,1)S(1)}, u32[]{:S(2)}, u32[]{:S(2)}) %collective-permute-start.47) | collective-permute-done | bytes 262176 | tf_op jit(solution)/shard_map/ppermute | solution.py:88
  341.3 7.1 %hidden_out.1 = (f32[120,2560]{1,0:T(8,128)}, f32[120,2560]{1,0:T(8,128)}, f32[320,960]{1,0:T(8,128)}, f32[1,120]{1,0:T(1,128)}) custom-call(s32[1]{0:T(128)} %bitcast.2.r_0_.rep_ref, bf16[2,184,640]{2,1,0:T(8,128)(2,1)} %core_sums.1.r_1_, bf16[2,184,640]{2,1,0:T(8,128)(2,1)} %copy-done.20, bf16[2,184,640]{2,1,0:T(8,128)(2,1)} %copy-done.21, ...), custom_call_target="tpu_custom_call" | custom-call | tf_op jit(solution)/shard_map/hidden_out/pallas_call | solution.py:127
  (290 shorter events, 162.1 us)
Async XLA Ops:
  23.8 28.1 %all-to-all-start.1 = ((bf16[4,128,1024]{2,1,0:T(8,128)(2,1)}), bf16[4,128,1024]{2,1,0:T(8,128)(2,1)S(1)}, u32[]{:S(2)}, u32[]{:S(2)}) async-start(bf16[4,128,1024]{2,1,0:T(8,128)(2,1)} %get-tuple-element.124), calls=%async_computation.1 | async-start | bytes 2097152 | tf_op jit(solution)/shard_map/all_to_all | solution.py:105
  51.9 35.5 %collective-permute-start = (bf16[4,128,1024]{2,1,0:T(8,128)(2,1)S(1)}, bf16[4,128,1024]{2,1,0:T(8,128)(2,1)S(1)}, u32[]{:S(2)}, u32[]{:S(2)}) collective-permute-start(bf16[4,128,1024]{2,1,0:T(8,128)(2,1)S(1)} %all-to-all-done.1.r_1_), channel_id=1, source_target_pairs={{0,1},{1,0},{2,3},{3,2},{4,5},{5,4},{6,7},{7,6},{8,9},{9,8},{10,11... | collective-permute-start | bytes 3145736 | tf_op jit(solution)/shard_map/ppermute | solution.py:88
  60.1 41.0 %all-to-all-start.2 = ((bf16[8,96,640]{2,1,0:T(8,128)(2,1)}), bf16[8,96,640]{2,1,0:T(8,128)(2,1)S(1)}, u32[]{:S(2)}, u32[]{:S(2)}) async-start(bf16[8,96,640]{2,1,0:T(8,128)(2,1)} %get-tuple-element.138), calls=%async_computation.2 | async-start | bytes 1966080 | tf_op jit(solution)/shard_map/all_to_all | solution.py:92
  99.4 22.8 %collective-permute-start.14 = (bf16[4,8,32,512]{3,2,1,0:T(8,128)(2,1)S(1)}, bf16[4,8,32,512]{3,2,1,0:T(8,128)(2,1)S(1)}, u32[]{:S(2)}, u32[]{:S(2)}) collective-permute-start(bf16[4,8,32,512]{3,2,1,0:T(8,128)(2,1)S(1)} %pad_maximum_fusion.r_2_), channel_id=1, source_target_pairs={{0,1},{1,0},{2,3},{3,2},{4,5},{5,4},{6,7},{7,6},{8,9},{9,8},{10,11... | collective-permute-start | bytes 3145736 | tf_op jit(solution)/shard_map/ppermute | solution.py:88
  99.5 31.9 %collective-permute-start.19 = (bf16[128,1024]{1,0:T(8,128)(2,1)S(1)}, bf16[128,1024]{1,0:T(8,128)(2,1)}, u32[]{:S(2)}, u32[]{:S(2)}) collective-permute-start(bf16[128,1024]{1,0:T(8,128)(2,1)S(1)} %copy-done.8), channel_id=1, source_target_pairs={{0,8},{8,0},{16,24},{24,16},{1,9},{9,1},{17,25},{25,17},{2,10},{10... | collective-permute-start | bytes 786440 | tf_op jit(solution)/shard_map/ppermute | solution.py:88
  111.7 21.2 %collective-permute-start.20 = (bf16[128,1024]{1,0:T(8,128)(2,1)S(1)}, bf16[128,1024]{1,0:T(8,128)(2,1)}, u32[]{:S(2)}, u32[]{:S(2)}) collective-permute-start(bf16[128,1024]{1,0:T(8,128)(2,1)S(1)} %copy-done.8), channel_id=1, source_target_pairs={{0,16},{8,24},{16,0},{24,8},{1,17},{9,25},{17,1},{25,9},{2,18},{10... | collective-permute-start | bytes 786440 | tf_op jit(solution)/shard_map/ppermute | solution.py:88
  113.3 19.6 %collective-permute-start.21 = (bf16[128,1024]{1,0:T(8,128)(2,1)S(1)}, bf16[128,1024]{1,0:T(8,128)(2,1)}, u32[]{:S(2)}, u32[]{:S(2)}) collective-permute-start(bf16[128,1024]{1,0:T(8,128)(2,1)S(1)} %copy-done.8), channel_id=1, source_target_pairs={{0,24},{8,16},{16,8},{24,0},{1,25},{9,17},{17,9},{25,1},{2,26},{10... | collective-permute-start | bytes 786440 | tf_op jit(solution)/shard_map/ppermute | solution.py:88
  115.8 29.3 %all-to-all-start.3 = ((bf16[8,88,640]{2,1,0:T(8,128)(2,1)}), bf16[8,88,640]{2,1,0:T(8,128)(2,1)}, u32[]{:S(2)}, u32[]{:S(2)}) async-start(bf16[8,88,640]{2,1,0:T(8,128)(2,1)} %get-tuple-element.156), calls=%async_computation.3 | async-start | bytes 1802240 | tf_op jit(solution)/shard_map/all_to_all | solution.py:92
  171.4 35.3 %all-to-all-start.4 = ((bf16[8,96,640]{2,1,0:T(8,128)(2,1)}), bf16[8,96,640]{2,1,0:T(8,128)(2,1)S(1)}, u32[]{:S(2)}, u32[]{:S(2)}) async-start(bf16[8,96,640]{2,1,0:T(8,128)(2,1)} %get-tuple-element.171), calls=%async_computation.4 | async-start | bytes 1966080 | tf_op jit(solution)/shard_map/all_to_all | solution.py:92
  183.1 30.8 %collective-permute-start.34 = (bf16[4,128,1024]{2,1,0:T(8,128)(2,1)}, bf16[4,128,1024]{2,1,0:T(8,128)(2,1)S(1)}, u32[]{:S(2)}, u32[]{:S(2)}) collective-permute-start(bf16[4,128,1024]{2,1,0:T(8,128)(2,1)} %down.2), channel_id=1, source_target_pairs={{0,1},{1,0},{2,3},{3,2},{4,5},{5,4},{6,7},{7,6},{8,9},{9,8},{10,11... | collective-permute-start | bytes 3145736 | tf_op jit(solution)/shard_map/ppermute | solution.py:88
  206.7 68.7 %all-to-all-start.5 = ((bf16[8,88,640]{2,1,0:T(8,128)(2,1)}), bf16[8,88,640]{2,1,0:T(8,128)(2,1)S(1)}, u32[]{:S(2)}, u32[]{:S(2)}) async-start(bf16[8,88,640]{2,1,0:T(8,128)(2,1)} %get-tuple-element.210), calls=%async_computation.5 | async-start | bytes 1802240 | tf_op jit(solution)/shard_map/all_to_all | solution.py:92
  222.2 38.3 %collective-permute-start.38 = (bf16[8,32,1024]{2,1,0:T(8,128)(2,1)}, bf16[8,32,1024]{2,1,0:T(8,128)(2,1)S(1)}, u32[]{:S(2)}, u32[]{:S(2)}) collective-permute-start(bf16[8,32,1024]{2,1,0:T(8,128)(2,1)} %get-tuple-element.202), channel_id=1, source_target_pairs={{0,8},{8,0},{16,24},{24,16},{1,9},{9,1},{17,25},{25,17},{2,10},{10... | collective-permute-start | bytes 1572872 | tf_op jit(solution)/shard_map/ppermute | solution.py:88
  222.7 38.3 %collective-permute-start.39 = (bf16[8,32,1024]{2,1,0:T(8,128)(2,1)}, bf16[8,32,1024]{2,1,0:T(8,128)(2,1)S(1)}, u32[]{:S(2)}, u32[]{:S(2)}) collective-permute-start(bf16[8,32,1024]{2,1,0:T(8,128)(2,1)} %get-tuple-element.203), channel_id=1, source_target_pairs={{0,16},{8,24},{16,0},{24,8},{1,17},{9,25},{17,1},{25,9},{2,18},{10... | collective-permute-start | bytes 1572872 | tf_op jit(solution)/shard_map/ppermute | solution.py:88
  223.2 35.7 %collective-permute-start.36 = (bf16[128,1024]{1,0:T(8,128)(2,1)}, bf16[128,1024]{1,0:T(8,128)(2,1)}, u32[]{:S(2)}, u32[]{:S(2)}) collective-permute-start(bf16[128,1024]{1,0:T(8,128)(2,1)} %get-tuple-element.198), channel_id=1, source_target_pairs={{0,16},{8,24},{16,0},{24,8},{1,17},{9,25},{17,1},{25,9},{2,18},{10... | collective-permute-start | bytes 786440 | tf_op jit(solution)/shard_map/ppermute | solution.py:88
  224.7 43.9 %collective-permute-start.40 = (bf16[8,32,1024]{2,1,0:T(8,128)(2,1)}, bf16[8,32,1024]{2,1,0:T(8,128)(2,1)S(1)}, u32[]{:S(2)}, u32[]{:S(2)}) collective-permute-start(bf16[8,32,1024]{2,1,0:T(8,128)(2,1)} %get-tuple-element.204), channel_id=1, source_target_pairs={{0,24},{8,16},{16,8},{24,0},{1,25},{9,17},{17,9},{25,1},{2,26},{10... | collective-permute-start | bytes 1572872 | tf_op jit(solution)/shard_map/ppermute | solution.py:88
  226.9 32.0 %collective-permute-start.37 = (bf16[128,1024]{1,0:T(8,128)(2,1)}, bf16[128,1024]{1,0:T(8,128)(2,1)}, u32[]{:S(2)}, u32[]{:S(2)}) collective-permute-start(bf16[128,1024]{1,0:T(8,128)(2,1)} %get-tuple-element.199), channel_id=1, source_target_pairs={{0,24},{8,16},{16,8},{24,0},{1,25},{9,17},{17,9},{25,1},{2,26},{10... | collective-permute-start | bytes 786440 | tf_op jit(solution)/shard_map/ppermute | solution.py:88
  258.9 33.4 %collective-permute-start.44 = (bf16[4,128,1024]{2,1,0:T(8,128)(2,1)}, bf16[4,128,1024]{2,1,0:T(8,128)(2,1)S(1)}, u32[]{:S(2)}, u32[]{:S(2)}) collective-permute-start(bf16[4,128,1024]{2,1,0:T(8,128)(2,1)} %first_grad.2), channel_id=1, source_target_pairs={{0,1},{1,0},{2,3},{3,2},{4,5},{5,4},{6,7},{7,6},{8,9},{9,8},{10,11... | collective-permute-start | bytes 3145736 | tf_op jit(solution)/shard_map/ppermute | solution.py:88
  287.3 45.0 %all-to-all-start.7 = ((bf16[8,32,1024]{2,1,0:T(8,128)(2,1)}), bf16[8,32,1024]{2,1,0:T(8,128)(2,1)S(1)}, u32[]{:S(2)}, u32[]{:S(2)}) async-start(bf16[8,32,1024]{2,1,0:T(8,128)(2,1)} %rep_sum.2), calls=%async_computation.7 | async-start | bytes 1048576 | tf_op jit(solution)/shard_map/all_to_all | solution.py:92
  296.1 25.1 %collective-permute-start.46 = (bf16[128,1024]{1,0:T(8,128)(2,1)}, bf16[128,1024]{1,0:T(8,128)(2,1)S(1)}, u32[]{:S(2)}, u32[]{:S(2)}) collective-permute-start(bf16[128,1024]{1,0:T(8,128)(2,1)} %get-tuple-element.214), channel_id=1, source_target_pairs={{0,4},{1,5},{2,6},{3,7},{4,0},{5,1},{6,2},{7,3},{8,12},{9,13},{10,... | collective-permute-start | bytes 786440 | tf_op jit(solution)/shard_map/ppermute | solution.py:88
  301.4 35.8 %collective-permute-start.51 = (bf16[2,184,640]{2,1,0:T(8,128)(2,1)}, bf16[2,184,640]{2,1,0:T(8,128)(2,1)S(1)}, u32[]{:S(2)}, u32[]{:S(2)}) collective-permute-start(bf16[2,184,640]{2,1,0:T(8,128)(2,1)} %core_sums.1.r_1_), channel_id=1, source_target_pairs={{0,8},{8,0},{16,24},{24,16},{1,9},{9,1},{17,25},{25,17},{2,10},{10... | collective-permute-start | bytes 1413128 | tf_op jit(solution)/shard_map/ppermute | solution.py:88
  302.8 34.9 %collective-permute-start.52 = (bf16[2,184,640]{2,1,0:T(8,128)(2,1)}, bf16[2,184,640]{2,1,0:T(8,128)(2,1)S(1)}, u32[]{:S(2)}, u32[]{:S(2)}) collective-permute-start(bf16[2,184,640]{2,1,0:T(8,128)(2,1)} %core_sums.1.r_1_), channel_id=1, source_target_pairs={{0,16},{8,24},{16,0},{24,8},{1,17},{9,25},{17,1},{25,9},{2,18},{10... | collective-permute-start | bytes 1413128 | tf_op jit(solution)/shard_map/ppermute | solution.py:88
  303.3 35.1 %collective-permute-start.53 = (bf16[2,184,640]{2,1,0:T(8,128)(2,1)}, bf16[2,184,640]{2,1,0:T(8,128)(2,1)S(1)}, u32[]{:S(2)}, u32[]{:S(2)}) collective-permute-start(bf16[2,184,640]{2,1,0:T(8,128)(2,1)} %core_sums.1.r_1_), channel_id=1, source_target_pairs={{0,24},{8,16},{16,8},{24,0},{1,25},{9,17},{17,9},{25,1},{2,26},{10... | collective-permute-start | bytes 1413128 | tf_op jit(solution)/shard_map/ppermute | solution.py:88
  311.3 17.5 %collective-permute-start.47 = (bf16[128,1024]{1,0:T(8,128)(2,1)S(1)}, bf16[128,1024]{1,0:T(8,128)(2,1)S(1)}, u32[]{:S(2)}, u32[]{:S(2)}) collective-permute-start(bf16[128,1024]{1,0:T(8,128)(2,1)S(1)} %copy-done.62), channel_id=1, source_target_pairs={{0,6},{1,7},{2,4},{3,5},{4,2},{5,3},{6,0},{7,1},{8,14},{9,15},{10,... | collective-permute-start | bytes 786440 | tf_op jit(solution)/shard_map/ppermute | solution.py:88
  328.8 19.7 %collective-permute-start.49 = (bf16[8,32,384]{2,1,0:T(8,128)(2,1)S(1)}, bf16[8,32,384]{2,1,0:T(8,128)(2,1)S(1)}, u32[]{:S(2)}, u32[]{:S(2)}) collective-permute-start(bf16[8,32,384]{2,1,0:T(8,128)(2,1)S(1)} %all_to_all.41.r_1_), channel_id=1, source_target_pairs={{0,16},{8,24},{16,0},{24,8},{1,17},{9,25},{17,1},{25,9},{2,18},{10... | collective-permute-start | bytes 589832 | tf_op jit(solution)/shard_map/ppermute | solution.py:88
  (109 other events, 1002.1 us)

commit v4 on v3

--- a/solution.py
+++ b/solution.py
@@ -309,7 +309,7 @@
 
 def attend_kernel(rows, n, me_ref, mine_ref, other_ref, *refs):
     w_ref, cos_ref, sin_ref, start_ref, first_ref, q_ref, k_ref, v_ref, gains_ref = refs[:9]
-    part_refs, mixed_ref = refs[9:-1], refs[-1]
+    mixed_ref = refs[9]
     core = me_ref[0] % 2
     length, head_cols = q_ref.shape
     heads = head_cols // HD
@@ -351,16 +351,11 @@
             mixed = head_of(dot(probs.astype(BF16), v_ref[past, :]), h, heads)
             total = mixed if total is None else total + mixed
         mixed_ref[span, :] = total.astype(BF16)
-    for i, ref in enumerate(part_refs):
-        ref[...] = mixed_ref[rows_at(me_ref[0] ^ i, rows), :]
-
-
-def attend_back_kernel(n, reps, rep_ref, me_ref, *refs):
-    parts, refs = refs[:n], refs[n:]
-    first_ref, q_ref, k_ref, v_ref, cos_ref, sin_ref, start_ref, dqkv_ref = refs[:8]
-    piece_refs, (g_ref, dk_ref, dv_ref, hold_ref) = refs[8 : 8 + reps], refs[8 + reps :]
-    for i, ref in enumerate(parts):
-        g_ref[rows_at(me_ref[0] ^ i, ref.shape[0]), :] = ref[...]
+
+
+def attend_back_kernel(reps, rep_ref, *refs):
+    g_ref, first_ref, q_ref, k_ref, v_ref, cos_ref, sin_ref, start_ref, dqkv_ref = refs[:9]
+    piece_refs, (dk_ref, dv_ref, hold_ref) = refs[9 : 9 + reps], refs[9 + reps :]
     length, head_cols = q_ref.shape
     heads = head_cols // HD
     block = min(256, length)
@@ -417,13 +412,9 @@
         ref[...] = (mine_ref[i].astype(F32) + other_ref[i].astype(F32)).astype(BF16)
 
 
-def middle_kernel(n, me_ref, tokens_ref, *refs):
-    parts, refs = refs[:n], refs[n:]
-    w_ref, gains_ref, middle_ref, second_ref, attended_ref, hold_ref = refs
+def middle_kernel(n, tokens_ref, mixed_ref, w_ref, gains_ref, middle_ref, second_ref, attended_ref):
     width = tokens_ref.shape[1]
-    for i, ref in enumerate(parts):
-        hold_ref[me_ref[0] ^ i] = ref[...]
-    attended = jnp.concatenate([hold_ref[s] for s in range(n)], axis=1)[:, :D]
+    attended = jnp.concatenate([mixed_ref[s] for s in range(n)], axis=1)[:, :D]
     attended = to_blocks(attended.astype(F32), n, width).astype(BF16)
     attended_ref[...] = attended
     middle = tokens_ref[...].astype(F32) + dot(attended, w_ref[...])
@@ -475,20 +466,21 @@
         sums = [
             sum(part[s].astype(F32) for s in range(core, part.shape[0], 2)) for part in refs[:-1]
         ]
-        out_ref[core] = jnp.concatenate(sums, axis=0).astype(BF16)
-
-
-def hidden_out_kernel(n, reps, each, rep_ref, *refs):
-    parts, refs = refs[:reps], refs[reps:]
-    gate_w_ref, up_w_ref, gain_ref, gate_ref, up_ref, down_ref, norm_ref, hold_ref = refs
+        total = jnp.concatenate(sums, axis=0).astype(BF16)
+        for r in range(out_ref.shape[0]):
+            out_ref[r, core] = total
+
+
+def hidden_out_kernel(
+    n, each, in_ref, gate_w_ref, up_w_ref, gain_ref, gate_ref, up_ref, down_ref, norm_ref
+):
+    reps = in_ref.shape[0]
     own = gate_ref.shape[0]
     units = 2 * reps * each
-    for i, part in enumerate(parts):
-        hold_ref[rep_ref[0] ^ i] = part[...]
-    cols = hold_ref.shape[3]
+    cols = in_ref.shape[3]
     boths = []
     for f in range(2 * reps):
-        both, down = unpack_message(hold_ref[f // 2, f % 2].astype(F32), own, each)
+        both, down = unpack_message(in_ref[f // 2, f % 2].astype(F32), own, each)
         boths.append(both)
         down_ref[f * each : (f + 1) * each, :] = down
     total = jnp.zeros((own, 1), F32)
@@ -517,10 +509,9 @@
     refs[-1][...] = from_blocks(total, n, own).T.astype(BF16)
 
 
-def middle_grad_kernel(n, own, reps, me_ref, *refs):
+def middle_grad_kernel(n, own, reps, *refs):
     parts, refs = refs[:reps], refs[reps:]
-    cot_ref, middle_ref, gains_ref, w_ref, grad_ref, branch_ref = refs[:6]
-    part_refs, hold_ref = refs[6:-1], refs[-1]
+    cot_ref, middle_ref, gains_ref, w_ref, grad_ref, branch_ref, heads_ref = refs
     rows = middle_ref.shape[0]
     middle = middle_ref[...]
     grad_second = sum(ref[...].astype(F32) for ref in parts)
@@ -531,17 +522,19 @@
     branch = grad.astype(BF16)
     branch_ref[...] = branch
     attended = from_blocks(contract_cols(branch, w_ref[...]), n, own)
-    head_cols = hold_ref.shape[2]
+    head_cols = heads_ref.shape[2]
     if n * head_cols > D:
         attended = jnp.concatenate([attended, jnp.zeros((rows, n * head_cols - D), F32)], axis=1)
     for s in range(n):
-        hold_ref[s] = attended[:, s * head_cols : (s + 1) * head_cols].astype(BF16)
-    for i, ref in enumerate(part_refs):
-        ref[...] = hold_ref[me_ref[0] ^ i]
-
-
-def out_weights_kernel(rep_ref, attended_ref, branch_ref, *refs):
-    store_pieces(rep_ref, refs[:-1], refs[-1], contract_rows(attended_ref[...], branch_ref[...]))
+        heads_ref[s] = attended[:, s * head_cols : (s + 1) * head_cols].astype(BF16)
+
+
+def out_weights_kernel(rep_ref, core_ref, attended_ref, branch_ref, mine_ref, other_ref, hold_ref):
+    store_pieces(rep_ref, (), hold_ref, contract_rows(attended_ref[...], branch_ref[...]))
+    for side, ref in enumerate((mine_ref, other_ref)):
+        for i in range(ref.shape[0]):
+            for z in range(ref.shape[1]):
+                ref[i, z] = hold_ref[2 * z + (core_ref[0] ^ side), rep_ref[0] ^ i]
 
 
 def rep_sum_kernel(reps, *refs):
@@ -665,7 +658,6 @@
     )
     w_qkv = w_qkv.reshape(width, qkv_cols)
     tokens_mine = exchange_z(after(tokens_tiled, arrived))
-    tokens_other = swap(tokens_mine, "shard", 1)
     (cot_in,) = call(
         lambda *r: blocks_kernel(n, *r), "cot_blocks", [(own_block, BF16)], after(cotangent.T, message)
     )
@@ -685,29 +677,30 @@
         w_down,
         scalars=(rep,),
     )
+    tokens_mine = after(tokens_mine, w_qkv, *messages)
+    tokens_other = swap(tokens_mine, "shard", 1)
     hidden_first = exchange(after(messages[0], tokens_mine))
 
     out_parts = spread(after(arrived, w_qkv)[:, :, qkv_cols:], "rep", 1)
 
     head_shape = (length, head_cols)
-    first_all, query, key, value, gains, *mixed = call(
+    first_all, query, key, value, gains, mixed = call(
         lambda *r: attend_kernel(rows, n, *r),
         "attend",
         [((length, width), BF16)]
         + [(head_shape, BF16)] * 3
         + [((2, width), F32)]
-        + [((rows, head_cols), BF16)] * n,
+        + [(head_shape, BF16)],
         tokens_mine,
         tokens_other,
         w_qkv,
         cosines,
         sines,
-        after(start, messages[0]),
+        start,
         scalars=(me,),
-        scratch=[(head_shape, BF16)],
-    )
-    mixed = deliver(later(mixed, hidden_first), "shard", 1)
-    hidden_rest = [exchange(after(message, *mixed)) for message in messages[1:]]
+    )
+    mixed = exchange(after(mixed, hidden_first).reshape(n, rows, head_cols))
+    hidden_rest = [exchange(after(message, mixed)) for message in messages[1:]]
     (out_full,) = call(
         lambda *r: join_out_kernel(reps, *r),
         "join_out",
@@ -722,11 +715,9 @@
         "middle",
         [(own_block, F32), (own_block, BF16), (own_block, BF16)],
         tokens_in,
-        *mixed,
+        mixed,
         out_full,
         gains,
-        scalars=(me,),
-        scratch=[((n, rows, head_cols), BF16)],
     )
     w_hidden, w_down_in = call(
         lambda *r: hidden_weights_in_kernel(n, own, each, *r),
@@ -756,7 +747,6 @@
     grad_mine, grads_mine, hidden_mine = hidden_side(
         after(second_mine, grad_other), cot_mine, "hidden_mine"
     )
-    sums, grad_second = plane_sums(grad_mine, grad_other)
     hidden_messages = call(
         lambda *r: hidden_weights_kernel(n, own, each, *r),
         "hidden_weights",
@@ -767,59 +757,66 @@
         cot_other,
         grads_mine,
         grads_other,
-        after(hidden_mine, sums[0]),
+        hidden_mine,
         hidden_other,
     )
     hidden_sums = [exchange(hidden_messages[0])]
+    sums, grad_second = plane_sums(after(grad_mine, hidden_messages[0]), grad_other)
     down_other, down_mine = [
         call(
             down_kernel,
             "down",
             [((reps, rows, width), BF16)],
-            after(hidden, hidden_messages[0]),
+            after(hidden, grad_second[1]),
             w_down_in,
         )[0]
         for hidden in (hidden_other, hidden_mine)
     ]
 
-    grad_middle, grad_branch, *grad_heads = call(
+    grad_middle, grad_branch, grad_heads = call(
         lambda *r: middle_grad_kernel(n, own, reps, *r),
         "middle_grad",
-        [(own_block, F32), (own_block, BF16)] + [((rows, head_cols), BF16)] * n,
+        [(own_block, F32), (own_block, BF16), ((n, rows, head_cols), BF16)],
         *grad_second,
         cot_in,
         after(middle, down_other, down_mine),
         gains,
         out_full,
-        scalars=(me,),
-        scratch=[((n, rows, head_cols), BF16)],
-    )
-    grad_heads = deliver(grad_heads, "shard", 1)
-    down_sums, down_parts = plane_sums(after(down_mine, grad_branch), down_other)
-    hidden_sums += [exchange(after(message, *grad_heads)) for message in hidden_messages[1:]]
+    )
+    grad_heads = exchange(after(grad_heads, *hidden_sums))
     out_pieces = call(
         out_weights_kernel,
         "out_weights",
-        [((n, piece, width), BF16)] * reps,
+        [((reps, nz, piece, width), BF16)] * 2,
         attended,
-        after(grad_branch, down_sums[0]),
-        scalars=(rep,),
+        grad_branch,
+        scalars=(rep, core),
         scratch=[((n, reps, piece, width), BF16)],
     )
+    down_sums, down_parts = plane_sums(after(down_mine, out_pieces[0]), down_other)
+    out_sums = call(
+        pair_sum_kernel,
+        "pair_sum",
+        [((nz, piece, width), BF16)] * reps,
+        after(out_pieces[0], down_sums[0]),
+        swap(out_pieces[1], "shard", 1),
+    )
+    hidden_sums += [exchange(after(message, grad_heads)) for message in hidden_messages[1:]]
+    grad_heads = grad_heads.reshape(head_shape)
     grad_qkv, *attention_pieces = call(
-        lambda *r: attend_back_kernel(n, reps, *r),
+        lambda *r: attend_back_kernel(reps, *r),
         "attend_back",
         [((length, qkv_cols), BF16)] + [((n, piece, qkv_cols), BF16)] * reps,
-        *grad_heads,
+        grad_heads,
         first_all,
         query,
         key,
         value,
         cosines,
         sines,
-        after(start, out_pieces[0], hidden_sums[0]),
-        scalars=(rep, me),
-        scratch=[(head_shape, BF16)] + [(head_shape, F32)] * 2 + [((n, reps, piece, qkv_cols), BF16)],
+        after(start, out_sums[0], down_sums[0]),
+        scalars=(rep,),
+        scratch=[(head_shape, F32)] * 2 + [((n, reps, piece, qkv_cols), BF16)],
     )
 
     def rep_sum(parts, *earlier):
@@ -850,7 +847,7 @@
         after(middle, first_mine),
         *down_parts,
     )
-    out_summed = rep_sum(deliver(out_pieces, "rep", 1), output)
+    out_summed = rep_sum(deliver(out_sums, "rep", 1), output)
     attention_summed = rep_sum(deliver(attention_pieces, "rep", 1), out_summed)
     first_sums = call(
         pair_sum_kernel,
@@ -864,11 +861,14 @@
     (core_sums,) = call(
         core_sums_kernel,
         "core_sums",
-        [((2, msg_rows, 2 * units), BF16)],
+        [((reps, 2, msg_rows, 2 * units), BF16)],
         after(hidden_sums[0], first_sums[0]),
         *hidden_sums[1:],
     )
-    out_moved = exchange(after(out_summed, attention_moved))
+    hidden_moved = lax.all_to_all(
+        after(core_sums, attention_moved), "rep", split_axis=0, concat_axis=0, tiled=True
+    )
+    out_moved = exchange_z(after(out_summed, hidden_moved))
 
     gain_rows = [gain.astype(F32)[None] for gain in (norm_one, norm_two)]
     (input_grad,) = call(
@@ -881,30 +881,28 @@
         grad_middle,
     )
 
-    grad_w_gate, grad_w_up, grad_w_down, grad_norm_two = call(
-        lambda *r: hidden_out_kernel(n, reps, each, *r),
-        "hidden_out",
-        [(w_gate.shape, F32), (w_up.shape, F32), (w_down.shape, F32), ((1, own), F32)],
-        *spread(core_sums, "rep", 1),
-        w_gate,
-        w_up,
-        after(gain_rows[1], input_grad),
-        scalars=(rep,),
-        scratch=[((reps, 2, msg_rows, 2 * units), BF16)],
-    )
-
     attention_parts = spread(attention_moved, "rep", 1)
     grad_w_query, grad_w_key, grad_w_value, grad_norm_one = call(
         lambda *r: attention_out_kernel(n, reps, *r),
         "attention_out",
         [(w_query.shape, F32), (w_key.shape[::-1], F32), (w_value.shape[::-1], F32), ((1, own), F32)],
         *attention_parts,
-        after(w_query, grad_norm_two),
+        after(w_query, input_grad),
         w_key.T,
         w_value.T,
         gain_rows[0],
         scalars=(rep,),
         scratch=[((reps, n, piece, qkv_cols), F32)],
+    )
+
+    grad_w_gate, grad_w_up, grad_w_down, grad_norm_two = call(
+        lambda *r: hidden_out_kernel(n, each, *r),
+        "hidden_out",
+        [(w_gate.shape, F32), (w_up.shape, F32), (w_down.shape, F32), ((1, own), F32)],
+        hidden_moved,
+        w_gate,
+        w_up,
+        after(gain_rows[1], grad_norm_one),
     )
 
     (out_piece,) = call(owner_sum_kernel, "owner_sum", [((piece, width), BF16)], after(out_moved, input_grad))

time: 361 us -> 380 us (1.053)
  blocking collectives: 29.1 us -> 45.6 us
    all_to_all x0 -> x1, blocking collectives: none -> 28.2 us  [shards(): lax.all_to_all(after(core_sums, attention_moved), 'rep', split_axis=0, co...]
    ppermute x57 -> x41, starting transfers between devices: 61.4 us -> 40.4 us  [swap(): return lax.ppermute(block, axis, [(i, i ^ k) for i in range(count)])]
    all_to_all x5 -> x7, starting transfers between devices: 30.7 us -> 49.8 us  [exchange(): lax.all_to_all(block, 'shard', split_axis=0, concat_axis=0, tiled=True)]
    all_to_all x1 -> x2, waiting for transfers between devices: 20.2 us -> 5.01 us  [exchange_z(): lax.all_to_all(blocks, 'shard', split_axis=0, concat_axis=0, axis_index_g...]
    all_to_all x5 -> x7, waiting for transfers between devices: 0.01 us -> 15 us  [exchange(): lax.all_to_all(block, 'shard', split_axis=0, concat_axis=0, tiled=True)]
    all_to_all x2 -> x1, blocking collectives: 29.1 us -> 17.4 us  [exchange(): lax.all_to_all(block, 'shard', split_axis=0, concat_axis=0, tiled=True)]
    all_to_all x1 -> x2, starting transfers between devices: 5.66 us -> 10.8 us  [exchange_z(): lax.all_to_all(blocks, 'shard', split_axis=0, concat_axis=0, axis_index_g...]
    unnamed x140 -> x114, local copies, waits for them, and re-layouts: 14.6 us -> 12.2 us
  transfers between devices with their start and end apart: 63 -> 50, of which waited for: 18 -> 18; matrix products, arithmetic and copies ran while one was open for 3% -> 2% of each run, Pallas kernels for 27% -> 25%
where the time goes in v4:
time: 380 us; the launch traced here: 372 us
  Pallas kernels  119 us (31%)
  starting transfers between devices  101 us (27%)
  waiting for transfers between devices  83.5 us (22%)
  blocking collectives  45.6 us (12%)
  local copies, waits for them, and re-layouts  14.3 us (4%)
  other arithmetic  7.21 us (2%)
    pallas_call x32, Pallas kernels, call(): pl.pallas_call(kernel, out_shape=[jax.ShapeDtypeStruct(shape, dtype) for...  119 us
    ppermute x41, waiting for transfers between devices, swap(): return lax.ppermute(block, axis, [(i, i ^ k) for i in range(count)])  63.5 us
    all_to_all x7, starting transfers between devices, exchange(): lax.all_to_all(block, 'shard', split_axis=0, concat_axis=0, tiled=True)  49.8 us
    ppermute x41, starting transfers between devices, swap(): return lax.ppermute(block, axis, [(i, i ^ k) for i in range(count)])  40.4 us
    all_to_all x1, blocking collectives, shards(): lax.all_to_all(after(core_sums, attention_moved), 'rep', split_axis=0, co...  28.2 us
    all_to_all x1, blocking collectives, exchange(): lax.all_to_all(block, 'shard', split_axis=0, concat_axis=0, tiled=True)  17.4 us
    all_to_all x7, waiting for transfers between devices, exchange(): lax.all_to_all(block, 'shard', split_axis=0, concat_axis=0, tiled=True)  15 us
    unnamed x114, local copies, waits for them, and re-layouts  12.2 us
  transfers between devices with their start and end apart: 50, of which 18 were waited for; matrix products, arithmetic and copies ran while one was open for 2% of the time, Pallas kernels for 25%

profile of v4, /device:TPU:10, one launch (start us, length us, event | category | flops | bytes accessed | tf_op | source)
XLA Modules:
  0.0 372.3 jit_solution(6884397058107013569)
XLA Ops:
  6.5 17.4 %all_to_all.55 = bf16[8,32,896]{2,1,0:T(8,128)(2,1)S(1)} all-to-all(bf16[8,32,896]{2,1,0:T(8,128)(2,1)} %attention_message.1), channel_id=1, replica_groups=mesh['rep'=4,'shard'=8] {'shard'}, dimensions={0} | all-to-all | bytes 917504 | tf_op jit(solution)/shard_map/all_to_all | solution.py:92
  23.9 5.5 %all-to-all-start.1 = ((bf16[4,128,1024]{2,1,0:T(8,128)(2,1)}), bf16[4,128,1024]{2,1,0:T(8,128)(2,1)S(1)}, u32[]{:S(2)}, u32[]{:S(2)}) async-start(bf16[4,128,1024]{2,1,0:T(8,128)(2,1)} %get-tuple-element.107), calls=%async_computation.1 | async-start | bytes 2097152 | tf_op jit(solution)/shard_map/all_to_all | solution.py:105
  51.9 6.7 %all-to-all-start.2 = ((bf16[8,96,640]{2,1,0:T(8,128)(2,1)}), bf16[8,96,640]{2,1,0:T(8,128)(2,1)S(1)}, u32[]{:S(2)}, u32[]{:S(2)}) async-start(bf16[8,96,640]{2,1,0:T(8,128)(2,1)} %get-tuple-element.115), calls=%async_computation.2 | async-start | bytes 1966080 | tf_op jit(solution)/shard_map/all_to_all | solution.py:92
  63.4 9.0 %attend.1 = (bf16[1024,1024]{1,0:T(8,128)(2,1)}, bf16[1024,128]{1,0:T(8,128)(2,1)}, bf16[1024,128]{1,0:T(8,128)(2,1)}, bf16[1024,128]{1,0:T(8,128)(2,1)}, f32[2,1024]{1,0:T(2,128)}, /*index=5*/bf16[1024,128]{1,0:T(8,128)(2,1)}) custom-call(s32[1]{0:T(128)} %bitcast.1.r_0_, bf16[4,128,1024]{2,1,0:T(8,128)(2,1)} %copy-done.2, ...), custom_call_target="tpu_custom_call" | custom-call | tf_op jit(solution)/shard_map/attend/pallas_call | solution.py:127
  74.3 6.1 %all-to-all-done.2.r_0_ = bf16[8,96,640]{2,1,0:T(8,128)(2,1)S(1)} async-done(((bf16[8,96,640]{2,1,0:T(8,128)(2,1)}), bf16[8,96,640]{2,1,0:T(8,128)(2,1)S(1)}, u32[]{:S(2)}, u32[]{:S(2)}) %all-to-all-start.2) | async-done | bytes 983072 | tf_op jit(solution)/shard_map/all_to_all | solution.py:92
  80.4 7.4 %all-to-all-start.3 = ((bf16[8,128,128]{2,1,0:T(8,128)(2,1)}), bf16[8,128,128]{2,1,0:T(8,128)(2,1)}, u32[]{:S(2)}, u32[]{:S(2)}) async-start(bf16[8,128,128]{2,1,0:T(8,128)(2,1)} %bitcast.53), calls=%async_computation.3 | async-start | bytes 524288 | tf_op jit(solution)/shard_map/all_to_all | solution.py:92
  95.8 6.3 %all-to-all-start.4 = ((bf16[8,88,640]{2,1,0:T(8,128)(2,1)}), bf16[8,88,640]{2,1,0:T(8,128)(2,1)}, u32[]{:S(2)}, u32[]{:S(2)}) async-start(bf16[8,88,640]{2,1,0:T(8,128)(2,1)} %get-tuple-element.125), calls=%async_computation.4 | async-start | bytes 1802240 | tf_op jit(solution)/shard_map/all_to_all | solution.py:92
  114.2 5.5 %collective-permute-done.10 = bf16[128,1024]{1,0:T(8,128)(2,1)S(1)} collective-permute-done((bf16[128,1024]{1,0:T(8,128)(2,1)}, bf16[128,1024]{1,0:T(8,128)(2,1)S(1)}, u32[]{:S(2)}, u32[]{:S(2)}) %collective-permute-start.10) | collective-permute-done | bytes 262176 | tf_op jit(solution)/shard_map/ppermute | solution.py:88
  129.2 5.8 %hidden_other.1 = (bf16[4,128,1024]{2,1,0:T(8,128)(2,1)}, bf16[512,640]{1,0:T(8,128)(2,1)}, bf16[512,320]{1,0:T(8,128)(2,1)}) custom-call(bf16[4,128,1024]{2,1,0:T(8,128)(2,1)} %collective-permute-done.11.second_ref.r_1_, bf16[4,128,1024]{2,1,0:T(8,128)(2,1)} %copy-done.4, bf16[1024,640]{1,0:T(8,128)(2,1)} %bitcast.43, ...), custom_call_target="tpu_custom_call" | custom-call | tf_op jit(solution)/shard_map/hidden_other/pallas_call | solution.py:127
  135.0 5.7 %hidden_mine.1 = (bf16[4,128,1024]{2,1,0:T(8,128)(2,1)}, bf16[512,640]{1,0:T(8,128)(2,1)}, bf16[512,320]{1,0:T(8,128)(2,1)}) custom-call(bf16[4,128,1024]{2,1,0:T(8,128)(2,1)} %copy-done.1, bf16[4,128,1024]{2,1,0:T(8,128)(2,1)} %copy-done, bf16[1024,640]{1,0:T(8,128)(2,1)} %bitcast.44, bf16[320,1024]{1,0:T(8,128)(2,1)} %get-tuple-element.127.down_ref.w_ref), custom_call_target="tpu_custom_call" | custom-call | tf_op jit(solution)/shard_map/hidden_mine/pallas_call | solution.py:127
  140.7 6.5 %hidden_weights.1 = (bf16[8,96,640]{2,1,0:T(8,128)(2,1)}, bf16[8,88,640]{2,1,0:T(8,128)(2,1)}) custom-call(bf16[4,128,1024]{2,1,0:T(8,128)(2,1)} %copy-done.1, bf16[4,128,1024]{2,1,0:T(8,128)(2,1)} %collective-permute-done.11.second_ref.r_1_, bf16[4,128,1024]{2,1,0:T(8,128)(2,1)} %copy-done, bf16[4,128,1024]{2,1,0:T(8,128)(2,1)} %copy-done.4, ...), custom_call_target="tpu_custom_call" | custom-call | tf_op jit(solution)/shard_map/hidden_weights/pallas_call | solution.py:127
  147.2 5.3 %all-to-all-start.5 = ((bf16[8,96,640]{2,1,0:T(8,128)(2,1)}), bf16[8,96,640]{2,1,0:T(8,128)(2,1)S(1)}, u32[]{:S(2)}, u32[]{:S(2)}) async-start(bf16[8,96,640]{2,1,0:T(8,128)(2,1)} %get-tuple-element.135), calls=%async_computation.5 | async-start | bytes 1966080 | tf_op jit(solution)/shard_map/all_to_all | solution.py:92
  162.1 5.9 %collective-permute-done.17.r_1_ = bf16[128,1024]{1,0:T(8,128)(2,1)S(1)} collective-permute-done((bf16[128,1024]{1,0:T(8,128)(2,1)}, bf16[128,1024]{1,0:T(8,128)(2,1)S(1)}, u32[]{:S(2)}, u32[]{:S(2)}) %collective-permute-start.17) | collective-permute-done | bytes 262176 | tf_op jit(solution)/shard_map/ppermute | solution.py:88
  191.7 13.8 %all-to-all-start.7 = ((bf16[8,88,640]{2,1,0:T(8,128)(2,1)}), bf16[8,88,640]{2,1,0:T(8,128)(2,1)S(1)}, u32[]{:S(2)}, u32[]{:S(2)}) async-start(bf16[8,88,640]{2,1,0:T(8,128)(2,1)} %get-tuple-element.175), calls=%async_computation.7 | async-start | bytes 1802240 | tf_op jit(solution)/shard_map/all_to_all | solution.py:92
  212.5 13.1 %attend_back.1 = (bf16[1024,384]{1,0:T(8,128)(2,1)}, bf16[8,32,384]{2,1,0:T(8,128)(2,1)}, bf16[8,32,384]{2,1,0:T(8,128)(2,1)}, bf16[8,32,384]{2,1,0:T(8,128)(2,1)}, bf16[8,32,384]{2,1,0:T(8,128)(2,1)}) custom-call(s32[1]{0:T(128)} %bitcast.2.r_0_.rep_ref, bf16[1024,128]{1,0:T(8,128)(2,1)} %bitcast.46, bf16[1024,1024]{1,0:T(8,128)(2,1)} %get-tuple-element.146.r_2_, ...), custom_call_target="tpu_custom_call" | custom-call | tf_op jit(solution)/shard_map/attend_back/pallas_call | solution.py:127
  234.1 9.9 %collective-permute-done.23.r_3_ = bf16[128,1024]{1,0:T(8,128)(2,1)S(1)} collective-permute-done((bf16[128,1024]{1,0:T(8,128)(2,1)S(1)}, bf16[128,1024]{1,0:T(8,128)(2,1)S(1)}, u32[]{:S(2)}, u32[]{:S(2)}) %collective-permute-start.23) | collective-permute-done | bytes 262176 | tf_op jit(solution)/shard_map/ppermute | solution.py:88
  247.7 7.6 %collective-permute-done.26.r_2_ = bf16[4,32,1024]{2,1,0:T(8,128)(2,1)S(1)} collective-permute-done((bf16[4,32,1024]{2,1,0:T(8,128)(2,1)S(1)}, bf16[4,32,1024]{2,1,0:T(8,128)(2,1)S(1)}, u32[]{:S(2)}, u32[]{:S(2)}) %collective-permute-start.26) | collective-permute-done | bytes 262176 | tf_op jit(solution)/shard_map/ppermute | solution.py:88
  268.9 5.1 %all-to-all-start.8 = ((bf16[8,32,384]{2,1,0:T(8,128)(2,1)}), bf16[8,32,384]{2,1,0:T(8,128)(2,1)S(1)}, u32[]{:S(2)}, u32[]{:S(2)}) async-start(bf16[8,32,384]{2,1,0:T(8,128)(2,1)} %rep_sum.3), calls=%async_computation.8 | async-start | bytes 393216 | tf_op jit(solution)/shard_map/all_to_all | solution.py:92
  280.8 28.2 %all_to_all.56.r_0_ = bf16[4,2,184,640]{3,2,1,0:T(8,128)(2,1)} all-to-all(bf16[4,2,184,640]{3,2,1,0:T(8,128)(2,1)} %core_sums.1), channel_id=1, replica_groups=mesh['rep'=4,'shard'=8] {'rep'}, dimensions={0} | all-to-all | bytes 3768320 | tf_op jit(solution)/shard_map/all_to_all | solution.py:868
  309.0 5.2 %all-to-all-start.10 = ((bf16[4,32,1024]{2,1,0:T(8,128)(2,1)}), bf16[4,32,1024]{2,1,0:T(8,128)(2,1)S(1)}, u32[]{:S(2)}, u32[]{:S(2)}) async-start(bf16[4,32,1024]{2,1,0:T(8,128)(2,1)} %rep_sum.2), calls=%async_computation.10 | async-start | bytes 524288 | tf_op jit(solution)/shard_map/all_to_all | solution.py:105
  319.5 8.3 %collective-permute-done.32.r_1_ = bf16[128,1024]{1,0:T(8,128)(2,1)S(1)} collective-permute-done((bf16[128,1024]{1,0:T(8,128)(2,1)S(1)}, bf16[128,1024]{1,0:T(8,128)(2,1)S(1)}, u32[]{:S(2)}, u32[]{:S(2)}) %collective-permute-start.32) | collective-permute-done | bytes 262176 | tf_op jit(solution)/shard_map/ppermute | solution.py:88
  327.8 8.8 %collective-permute-done.33.r_2_ = bf16[128,1024]{1,0:T(8,128)(2,1)S(1)} collective-permute-done((bf16[128,1024]{1,0:T(8,128)(2,1)S(1)}, bf16[128,1024]{1,0:T(8,128)(2,1)S(1)}, u32[]{:S(2)}, u32[]{:S(2)}) %collective-permute-start.33) | collective-permute-done | bytes 262176 | tf_op jit(solution)/shard_map/ppermute | solution.py:88
  336.6 6.7 %collective-permute-done.34.r_3_ = bf16[128,1024]{1,0:T(8,128)(2,1)S(1)} collective-permute-done((bf16[128,1024]{1,0:T(8,128)(2,1)S(1)}, bf16[128,1024]{1,0:T(8,128)(2,1)S(1)}, u32[]{:S(2)}, u32[]{:S(2)}) %collective-permute-start.34) | collective-permute-done | bytes 262176 | tf_op jit(solution)/shard_map/ppermute | solution.py:88
  361.8 7.0 %hidden_out.1 = (f32[120,2560]{1,0:T(8,128)}, f32[120,2560]{1,0:T(8,128)}, f32[320,960]{1,0:T(8,128)}, f32[1,120]{1,0:T(1,128)}) custom-call(bf16[4,2,184,640]{3,2,1,0:T(8,128)(2,1)} %all_to_all.56.r_0_, bf16[120,2560]{1,0:T(8,128)(2,1)} %r_1_.3, bf16[120,2560]{1,0:T(8,128)(2,1)} %r_2_.3, f32[1,120]{1,0:T(1,128)} %bitcast_convert_fusion.r_3_), custom_call_target="tpu_custom_call" | custom-call | tf_op jit(solution)/shard_map/hidden_out/pallas_call | solution.py:127
  (239 shorter events, 164.2 us)
Async XLA Ops:
  23.9 28.0 %all-to-all-start.1 = ((bf16[4,128,1024]{2,1,0:T(8,128)(2,1)}), bf16[4,128,1024]{2,1,0:T(8,128)(2,1)S(1)}, u32[]{:S(2)}, u32[]{:S(2)}) async-start(bf16[4,128,1024]{2,1,0:T(8,128)(2,1)} %get-tuple-element.107), calls=%async_computation.1 | async-start | bytes 2097152 | tf_op jit(solution)/shard_map/all_to_all | solution.py:105
  51.9 28.5 %all-to-all-start.2 = ((bf16[8,96,640]{2,1,0:T(8,128)(2,1)}), bf16[8,96,640]{2,1,0:T(8,128)(2,1)S(1)}, u32[]{:S(2)}, u32[]{:S(2)}) async-start(bf16[8,96,640]{2,1,0:T(8,128)(2,1)} %get-tuple-element.115), calls=%async_computation.2 | async-start | bytes 1966080 | tf_op jit(solution)/shard_map/all_to_all | solution.py:92
  74.2 27.9 %collective-permute-start.7 = (bf16[4,8,32,512]{3,2,1,0:T(8,128)(2,1)S(1)}, bf16[4,8,32,512]{3,2,1,0:T(8,128)(2,1)S(1)}, u32[]{:S(2)}, u32[]{:S(2)}) collective-permute-start(bf16[4,8,32,512]{3,2,1,0:T(8,128)(2,1)S(1)} %pad_maximum_fusion.r_2_), channel_id=1, source_target_pairs={{0,1},{1,0},{2,3},{3,2},{4,5},{5,4},{6,7},{7,6},{8,9},{9,8},{10,11... | collective-permute-start | bytes 3145736 | tf_op jit(solution)/shard_map/ppermute | solution.py:88
  80.4 15.4 %all-to-all-start.3 = ((bf16[8,128,128]{2,1,0:T(8,128)(2,1)}), bf16[8,128,128]{2,1,0:T(8,128)(2,1)}, u32[]{:S(2)}, u32[]{:S(2)}) async-start(bf16[8,128,128]{2,1,0:T(8,128)(2,1)} %bitcast.53), calls=%async_computation.3 | async-start | bytes 524288 | tf_op jit(solution)/shard_map/all_to_all | solution.py:92
  87.8 23.5 %collective-permute-start.14 = (bf16[128,1024]{1,0:T(8,128)(2,1)S(1)}, bf16[128,1024]{1,0:T(8,128)(2,1)}, u32[]{:S(2)}, u32[]{:S(2)}) collective-permute-start(bf16[128,1024]{1,0:T(8,128)(2,1)S(1)} %copy-done.8), channel_id=1, source_target_pairs={{0,24},{8,16},{16,8},{24,0},{1,25},{9,17},{17,9},{25,1},{2,26},{10... | collective-permute-start | bytes 786440 | tf_op jit(solution)/shard_map/ppermute | solution.py:88
  89.3 23.5 %collective-permute-start.13 = (bf16[128,1024]{1,0:T(8,128)(2,1)S(1)}, bf16[128,1024]{1,0:T(8,128)(2,1)}, u32[]{:S(2)}, u32[]{:S(2)}) collective-permute-start(bf16[128,1024]{1,0:T(8,128)(2,1)S(1)} %copy-done.8), channel_id=1, source_target_pairs={{0,16},{8,24},{16,0},{24,8},{1,17},{9,25},{17,1},{25,9},{2,18},{10... | collective-permute-start | bytes 786440 | tf_op jit(solution)/shard_map/ppermute | solution.py:88
  89.8 23.0 %collective-permute-start.12 = (bf16[128,1024]{1,0:T(8,128)(2,1)S(1)}, bf16[128,1024]{1,0:T(8,128)(2,1)}, u32[]{:S(2)}, u32[]{:S(2)}) collective-permute-start(bf16[128,1024]{1,0:T(8,128)(2,1)S(1)} %copy-done.8), channel_id=1, source_target_pairs={{0,8},{8,0},{16,24},{24,16},{1,9},{9,1},{17,25},{25,17},{2,10},{10... | collective-permute-start | bytes 786440 | tf_op jit(solution)/shard_map/ppermute | solution.py:88
  95.8 28.9 %all-to-all-start.4 = ((bf16[8,88,640]{2,1,0:T(8,128)(2,1)}), bf16[8,88,640]{2,1,0:T(8,128)(2,1)}, u32[]{:S(2)}, u32[]{:S(2)}) async-start(bf16[8,88,640]{2,1,0:T(8,128)(2,1)} %get-tuple-element.125), calls=%async_computation.4 | async-start | bytes 1802240 | tf_op jit(solution)/shard_map/all_to_all | solution.py:92
  147.2 31.5 %all-to-all-start.5 = ((bf16[8,96,640]{2,1,0:T(8,128)(2,1)}), bf16[8,96,640]{2,1,0:T(8,128)(2,1)S(1)}, u32[]{:S(2)}, u32[]{:S(2)}) async-start(bf16[8,96,640]{2,1,0:T(8,128)(2,1)} %get-tuple-element.135), calls=%async_computation.5 | async-start | bytes 1966080 | tf_op jit(solution)/shard_map/all_to_all | solution.py:92
  183.8 21.7 %collective-permute-start.20 = (bf16[4,128,1024]{2,1,0:T(8,128)(2,1)S(1)}, bf16[4,128,1024]{2,1,0:T(8,128)(2,1)}, u32[]{:S(2)}, u32[]{:S(2)}) collective-permute-start(bf16[4,128,1024]{2,1,0:T(8,128)(2,1)S(1)} %copy-done.13), channel_id=1, source_target_pairs={{0,1},{1,0},{2,3},{3,2},{4,5},{5,4},{6,7},{7,6},{8,9},{9,8},{10,11... | collective-permute-start | bytes 3145736 | tf_op jit(solution)/shard_map/ppermute | solution.py:88
  187.1 21.8 %collective-permute-start.21 = (bf16[4,4,32,1024]{3,2,1,0:T(8,128)(2,1)}, bf16[4,4,32,1024]{3,2,1,0:T(8,128)(2,1)}, u32[]{:S(2)}, u32[]{:S(2)}) collective-permute-start(bf16[4,4,32,1024]{3,2,1,0:T(8,128)(2,1)} %get-tuple-element.156), channel_id=1, source_target_pairs={{0,1},{1,0},{2,3},{3,2},{4,5},{5,4},{6,7},{7,6},{8,9},{9,8},{10,11... | collective-permute-start | bytes 3145736 | tf_op jit(solution)/shard_map/ppermute | solution.py:88
  191.7 77.2 %all-to-all-start.7 = ((bf16[8,88,640]{2,1,0:T(8,128)(2,1)}), bf16[8,88,640]{2,1,0:T(8,128)(2,1)S(1)}, u32[]{:S(2)}, u32[]{:S(2)}) async-start(bf16[8,88,640]{2,1,0:T(8,128)(2,1)} %get-tuple-element.175), calls=%async_computation.7 | async-start | bytes 1802240 | tf_op jit(solution)/shard_map/all_to_all | solution.py:92
  208.2 24.6 %collective-permute-start.22 = (bf16[128,1024]{1,0:T(8,128)(2,1)}, bf16[128,1024]{1,0:T(8,128)(2,1)S(1)}, u32[]{:S(2)}, u32[]{:S(2)}) collective-permute-start(bf16[128,1024]{1,0:T(8,128)(2,1)} %get-tuple-element.162), channel_id=1, source_target_pairs={{0,8},{8,0},{16,24},{24,16},{1,9},{9,1},{17,25},{25,17},{2,10},{10... | collective-permute-start | bytes 786440 | tf_op jit(solution)/shard_map/ppermute | solution.py:88
  229.3 44.7 %collective-permute-start.31 = (bf16[4,128,1024]{2,1,0:T(8,128)(2,1)}, bf16[4,128,1024]{2,1,0:T(8,128)(2,1)S(1)}, u32[]{:S(2)}, u32[]{:S(2)}) collective-permute-start(bf16[4,128,1024]{2,1,0:T(8,128)(2,1)} %first_grad.2), channel_id=1, source_target_pairs={{0,1},{1,0},{2,3},{3,2},{4,5},{5,4},{6,7},{7,6},{8,9},{9,8},{10,11... | collective-permute-start | bytes 3145736 | tf_op jit(solution)/shard_map/ppermute | solution.py:88
  232.8 22.5 %collective-permute-start.26 = (bf16[4,32,1024]{2,1,0:T(8,128)(2,1)S(1)}, bf16[4,32,1024]{2,1,0:T(8,128)(2,1)S(1)}, u32[]{:S(2)}, u32[]{:S(2)}) collective-permute-start(bf16[4,32,1024]{2,1,0:T(8,128)(2,1)S(1)} %copy-done.47), channel_id=1, source_target_pairs={{0,16},{8,24},{16,0},{24,8},{1,17},{9,25},{17,1},{25,9},{2,18},{10... | collective-permute-start | bytes 786440 | tf_op jit(solution)/shard_map/ppermute | solution.py:88
  244.0 18.7 %collective-permute-start.27 = (bf16[4,32,1024]{2,1,0:T(8,128)(2,1)S(1)}, bf16[4,32,1024]{2,1,0:T(8,128)(2,1)S(1)}, u32[]{:S(2)}, u32[]{:S(2)}) collective-permute-start(bf16[4,32,1024]{2,1,0:T(8,128)(2,1)S(1)} %copy-done.46), channel_id=1, source_target_pairs={{0,24},{8,16},{16,8},{24,0},{1,25},{9,17},{17,9},{25,1},{2,26},{10... | collective-permute-start | bytes 786440 | tf_op jit(solution)/shard_map/ppermute | solution.py:88
  245.5 20.0 %collective-permute-start.28 = (bf16[8,32,384]{2,1,0:T(8,128)(2,1)S(1)}, bf16[8,32,384]{2,1,0:T(8,128)(2,1)S(1)}, u32[]{:S(2)}, u32[]{:S(2)}) collective-permute-start(bf16[8,32,384]{2,1,0:T(8,128)(2,1)S(1)} %copy-done.56), channel_id=1, source_target_pairs={{0,8},{8,0},{16,24},{24,16},{1,9},{9,1},{17,25},{25,17},{2,10},{10... | collective-permute-start | bytes 589832 | tf_op jit(solution)/shard_map/ppermute | solution.py:88
  246.8 18.7 %collective-permute-start.29 = (bf16[8,32,384]{2,1,0:T(8,128)(2,1)S(1)}, bf16[8,32,384]{2,1,0:T(8,128)(2,1)S(1)}, u32[]{:S(2)}, u32[]{:S(2)}) collective-permute-start(bf16[8,32,384]{2,1,0:T(8,128)(2,1)S(1)} %copy-done.55), channel_id=1, source_target_pairs={{0,16},{8,24},{16,0},{24,8},{1,17},{9,25},{17,1},{25,9},{2,18},{10... | collective-permute-start | bytes 589832 | tf_op jit(solution)/shard_map/ppermute | solution.py:88
  309.0 40.9 %all-to-all-start.10 = ((bf16[4,32,1024]{2,1,0:T(8,128)(2,1)}), bf16[4,32,1024]{2,1,0:T(8,128)(2,1)S(1)}, u32[]{:S(2)}, u32[]{:S(2)}) async-start(bf16[4,32,1024]{2,1,0:T(8,128)(2,1)} %rep_sum.2), calls=%async_computation.10 | async-start | bytes 524288 | tf_op jit(solution)/shard_map/all_to_all | solution.py:105
  314.2 22.4 %collective-permute-start.33 = (bf16[128,1024]{1,0:T(8,128)(2,1)S(1)}, bf16[128,1024]{1,0:T(8,128)(2,1)S(1)}, u32[]{:S(2)}, u32[]{:S(2)}) collective-permute-start(bf16[128,1024]{1,0:T(8,128)(2,1)S(1)} %copy-done.52), channel_id=1, source_target_pairs={{0,4},{1,5},{2,6},{3,7},{4,0},{5,1},{6,2},{7,3},{8,12},{9,13},{10,... | collective-permute-start | bytes 786440 | tf_op jit(solution)/shard_map/ppermute | solution.py:88
  317.1 26.2 %collective-permute-start.34 = (bf16[128,1024]{1,0:T(8,128)(2,1)S(1)}, bf16[128,1024]{1,0:T(8,128)(2,1)S(1)}, u32[]{:S(2)}, u32[]{:S(2)}) collective-permute-start(bf16[128,1024]{1,0:T(8,128)(2,1)S(1)} %copy-done.51), channel_id=1, source_target_pairs={{0,6},{1,7},{2,4},{3,5},{4,2},{5,3},{6,0},{7,1},{8,14},{9,15},{10,... | collective-permute-start | bytes 786440 | tf_op jit(solution)/shard_map/ppermute | solution.py:88
  317.7 35.9 %collective-permute-start.35 = (bf16[8,32,384]{2,1,0:T(8,128)(2,1)S(1)}, bf16[8,32,384]{2,1,0:T(8,128)(2,1)S(1)}, u32[]{:S(2)}, u32[]{:S(2)}) collective-permute-start(bf16[8,32,384]{2,1,0:T(8,128)(2,1)S(1)} %all-to-all-done.8.r_1_), channel_id=1, source_target_pairs={{0,8},{8,0},{16,24},{24,16},{1,9},{9,1},{17,25},{25,17},{2,10},{10... | collective-permute-start | bytes 589832 | tf_op jit(solution)/shard_map/ppermute | solution.py:88
  352.1 16.7 %collective-permute-start.38 = (bf16[32,1024]{1,0:T(8,128)(2,1)}, bf16[32,1024]{1,0:T(8,128)(2,1)S(1)}, u32[]{:S(2)}, u32[]{:S(2)}) collective-permute-start(bf16[32,1024]{1,0:T(8,128)(2,1)} %owner_sum.1.r_1_), channel_id=1, source_target_pairs={{0,8},{8,0},{16,24},{24,16},{1,9},{9,1},{17,25},{25,17},{2,10},{10... | collective-permute-start | bytes 196616 | tf_op jit(solution)/shard_map/ppermute | solution.py:88
  352.7 16.1 %collective-permute-start.39 = (bf16[32,1024]{1,0:T(8,128)(2,1)}, bf16[32,1024]{1,0:T(8,128)(2,1)S(1)}, u32[]{:S(2)}, u32[]{:S(2)}) collective-permute-start(bf16[32,1024]{1,0:T(8,128)(2,1)} %owner_sum.1.r_1_), channel_id=1, source_target_pairs={{0,16},{8,24},{16,0},{24,8},{1,17},{9,25},{17,1},{25,9},{2,18},{10... | collective-permute-start | bytes 196616 | tf_op jit(solution)/shard_map/ppermute | solution.py:88
  (83 other events, 1023.1 us)
